TPU v7x, 32 devices: a whole 2x2x4 slice. The times are simulated.
32 devices in a mesh: shard: 4 (over z), ctx: 2 (over x), tp: 4 (over y, core).
Axes of the slice: x: 2, y: 2, z: 4, core: 2. Of those that a mesh axis runs over, the one named last changes fastest.
Arguments:
- tokens: bfloat16 [16, 1536, 960], P(('shard', 'tp'), 'ctx'), may hold values from -6 to 6
- span_ids: int32 [4], replicated, may hold values from 0 to 3, each once
- w_query: bfloat16 [2, 960, 960], P(None, ('shard', 'ctx')), may hold values from -0.1875 to 0.1875
- key_weight: bfloat16 [2, 960, 320], P(None, ('shard', 'ctx')), may hold values from -0.1875 to 0.1875
- value_weight: bfloat16 [2, 960, 320], P(None, ('shard', 'ctx')), may hold values from -0.1875 to 0.1875
- w_out: bfloat16 [2, 960, 960], P(None, None, ('shard', 'ctx')), may hold values from -2.5 to 2.5
- gain_attn: bfloat16 [2, 960], P(None, ('shard', 'ctx')), may hold values from 0.099609375 to 1.8984375
- gain_mlp: bfloat16 [2, 960], P(None, ('shard', 'ctx')), may hold values from 0.099609375 to 1.8984375
- w_gate: bfloat16 [2, 960, 2560], P(None, ('shard', 'ctx'), 'tp'), may hold values from -0.1875 to 0.1875
- w_up: bfloat16 [2, 960, 2560], P(None, ('shard', 'ctx'), 'tp'), may hold values from -0.1875 to 0.1875
- w_down: bfloat16 [2, 2560, 960], P(None, 'tp', ('shard', 'ctx')), may hold values from -0.125 to 0.125
- out_grad: bfloat16 [16, 1536, 960], P(('shard', 'tp'), 'ctx'), may hold values from -6 to 6
Outputs:
- block_out: bfloat16 [16, 1536, 960], P(('shard', 'tp'), 'ctx')
- tokens_grad: float32 [16, 1536, 960], P(('shard', 'tp'), 'ctx')
- grad_query: float32 [2, 960, 960], P(None, ('shard', 'ctx'))
- grad_key: float32 [2, 960, 320], P(None, ('shard', 'ctx'))
- grad_value: float32 [2, 960, 320], P(None, ('shard', 'ctx'))
- grad_out: float32 [2, 960, 960], P(None, None, ('shard', 'ctx'))
- grad_gain_attn: float32 [2, 960], P(None, ('shard', 'ctx'))
- grad_gain_mlp: float32 [2, 960], P(None, ('shard', 'ctx'))
- grad_gate: float32 [2, 960, 2560], P(None, ('shard', 'ctx'), 'tp')
- grad_up: float32 [2, 960, 2560], P(None, ('shard', 'ctx'), 'tp')
- grad_down: float32 [2, 2560, 960], P(None, 'tp', ('shard', 'ctx'))
Inputs may be any that keep to these rules, and one draw needn't show every extreme that they name: a permutation; stored row j of every sequence is its token at position span_ids[j // c] * c + j % c with c = 1536 // (2 * 2).
All inputs are finite; a program needn't handle non-finite values.
Results may differ from a plain program's by a relative error of at most 0.033.
Values may be sent and summed in bfloat16 or wider, within the bound.
No kernel may reach another device: no remote copies, remote signals or barrier semaphores. Data moves between devices by JAX's collectives and lax.ppermute only.
A program may use at most 512 MiB of HBM per device.

v0:
```python
import jax
import jax.numpy as jnp
from jax import lax
from jax.sharding import PartitionSpec as P

QUERY_HEADS = 15
KEY_VALUE_HEADS = 5
HEAD_DIM = 64
DECODER_LAYERS = 2


EPS = 1e-05
THETA = 10000.0
MASKED = -1e30


def rms_scale(hidden):
    return lax.rsqrt(jnp.mean(hidden * hidden, axis=-1, keepdims=True) + EPS)


def apply_rotation(values, cosine_table, sine_table):
    middle = values.shape[-1] // 2
    turned = jnp.concatenate([-values[..., middle:], values[..., :middle]], axis=-1)
    return values * cosine_table[:, None, :] + turned * sine_table[:, None, :]


def rotate_back(gradient, cosine_table, sine_table):
    middle = gradient.shape[-1] // 2
    moved = gradient * sine_table[:, None, :]
    turned = jnp.concatenate([moved[..., middle:], -moved[..., :middle]], axis=-1)
    return gradient * cosine_table[:, None, :] + turned


def norm_back(gradient, normed, scaling, gain_f):
    weighted = gradient * gain_f
    gain_grad = jnp.sum(gradient * normed, axis=0)
    return (
        scaling * (weighted - normed * jnp.mean(weighted * normed, axis=-1, keepdims=True)),
        gain_grad,
    )


def split_heads(query_rows, key_value_pair):
    row_total = query_rows.shape[0]
    key_value_width = key_value_pair.shape[-1] // 2
    key_matrix = key_value_pair[:, :key_value_width].reshape(-1, KEY_VALUE_HEADS, HEAD_DIM)
    value_matrix = key_value_pair[:, key_value_width:].reshape(-1, KEY_VALUE_HEADS, HEAD_DIM)
    grouped_keys = query_rows.reshape(
        row_total, KEY_VALUE_HEADS, QUERY_HEADS // KEY_VALUE_HEADS, HEAD_DIM
    )
    return (grouped_keys, key_matrix, value_matrix)


def seq_scores(grouped_keys, key_matrix, causal):
    scores = jnp.einsum(
        "qkgd,tkd->kgqt", grouped_keys, key_matrix, preferred_element_type=jnp.float32
    ) * HEAD_DIM ** (-0.5)
    return jnp.where(causal, scores, MASKED)


def attend(query_rows, key_value_pair, causal):
    grouped_keys, key_matrix, value_matrix = split_heads(query_rows, key_value_pair)
    scores = seq_scores(grouped_keys, key_matrix, causal)
    row_max = jnp.max(scores, axis=-1, keepdims=True)
    exp_scores = jnp.exp(scores - row_max)
    row_sum = jnp.sum(exp_scores, axis=-1, keepdims=True)
    attn_prob = (exp_scores / row_sum).astype(jnp.bfloat16)
    mixed = jnp.einsum(
        "kgqt,tkd->qkgd", attn_prob, value_matrix, preferred_element_type=jnp.float32
    )
    return (mixed.reshape(query_rows.shape[0], QUERY_HEADS * HEAD_DIM), row_max + jnp.log(row_sum))


def attend_back(query_rows, key_value_pair, mixture_gradient, log_total, causal):
    grouped_keys, key_matrix, value_matrix = split_heads(query_rows, key_value_pair)
    row_total = query_rows.shape[0]
    scores = seq_scores(grouped_keys, key_matrix, causal)
    attn_prob = jnp.exp(scores - log_total)
    grouped_gradient = mixture_gradient.reshape(
        row_total, KEY_VALUE_HEADS, QUERY_HEADS // KEY_VALUE_HEADS, HEAD_DIM
    )
    prob_grad = jnp.einsum(
        "qkgd,tkd->kgqt", grouped_gradient, value_matrix, preferred_element_type=jnp.float32
    )
    inner_sum = jnp.sum(attn_prob * prob_grad, axis=-1, keepdims=True)
    score_grad = (attn_prob * (prob_grad - inner_sum)).astype(jnp.bfloat16)
    query_grad = jnp.einsum(
        "kgqt,tkd->qkgd", score_grad, key_matrix, preferred_element_type=jnp.float32
    ) * HEAD_DIM ** (-0.5)
    key_gradient = jnp.einsum(
        "kgqt,qkgd->tkd", score_grad, grouped_keys, preferred_element_type=jnp.float32
    ) * HEAD_DIM ** (-0.5)
    value_gradient = jnp.einsum(
        "kgqt,qkgd->tkd",
        attn_prob.astype(jnp.bfloat16),
        grouped_gradient,
        preferred_element_type=jnp.float32,
    )
    key_total = key_matrix.shape[0]
    joined = jnp.concatenate(
        [
            key_gradient.reshape(key_total, KEY_VALUE_HEADS * HEAD_DIM),
            value_gradient.reshape(key_total, KEY_VALUE_HEADS * HEAD_DIM),
        ],
        axis=-1,
    )
    return (query_grad.reshape(row_total, QUERY_HEADS * HEAD_DIM), joined)


def forward_layer(hidden, gathered_w, cosine_table, sine_table, causal, group_count, local_length):
    wq_full, wk_full, wv_full, wo_full, gain_a, gain_m, wg_full, wu_full, wd_full = gathered_w
    row_total = hidden.shape[0]
    scale_a = rms_scale(hidden)
    normed_a = hidden * scale_a
    attention_input = (normed_a * gain_a.astype(jnp.float32)).astype(jnp.bfloat16)
    q_proj = jnp.dot(attention_input, wq_full, preferred_element_type=jnp.float32)
    key_projected = jnp.dot(attention_input, wk_full, preferred_element_type=jnp.float32)
    value_projected = jnp.dot(attention_input, wv_full, preferred_element_type=jnp.float32)
    query_rows = apply_rotation(
        q_proj.reshape(group_count, local_length, QUERY_HEADS, HEAD_DIM), cosine_table, sine_table
    ).astype(jnp.bfloat16)
    key_rotated = apply_rotation(
        key_projected.reshape(group_count, local_length, KEY_VALUE_HEADS, HEAD_DIM),
        cosine_table,
        sine_table,
    )
    key_value_pair = jnp.concatenate(
        [
            key_rotated.reshape(group_count, local_length, KEY_VALUE_HEADS * HEAD_DIM),
            value_projected.reshape(group_count, local_length, KEY_VALUE_HEADS * HEAD_DIM),
        ],
        axis=-1,
    ).astype(jnp.bfloat16)
    keyval_all = lax.all_gather(key_value_pair, "ctx", axis=1, tiled=True)

    def seq_forward(seq_pair):
        return attend(seq_pair[0], seq_pair[1], causal)

    mixed, log_total = lax.map(seq_forward, (query_rows, keyval_all))
    attn_mix = mixed.reshape(row_total, QUERY_HEADS * HEAD_DIM).astype(jnp.bfloat16)
    hidden_mid = hidden + jnp.dot(attn_mix, wo_full, preferred_element_type=jnp.float32)
    scale_m = rms_scale(hidden_mid)
    normed_m = hidden_mid * scale_m
    mlp_in = (normed_m * gain_m.astype(jnp.float32)).astype(jnp.bfloat16)
    mlp_rows = lax.all_gather(mlp_in, "tp", axis=0, tiled=True)
    gate_val = jnp.dot(mlp_rows, wg_full, preferred_element_type=jnp.float32)
    up_val = jnp.dot(mlp_rows, wu_full, preferred_element_type=jnp.float32)
    inner_act = (jax.nn.silu(gate_val) * up_val).astype(jnp.bfloat16)
    hidden_out = hidden_mid + lax.psum_scatter(
        jnp.dot(inner_act, wd_full, preferred_element_type=jnp.float32).astype(jnp.bfloat16),
        "tp",
        scatter_dimension=0,
        tiled=True,
    ).astype(jnp.float32)
    kept_acts = (
        normed_a,
        scale_a,
        attention_input,
        query_rows,
        keyval_all,
        attn_mix,
        log_total,
        normed_m,
        scale_m,
        mlp_rows,
        gate_val,
        up_val,
        inner_act,
    )
    return (hidden_out, kept_acts)


def backward_layer(
    grad_in, kept_acts, gathered_w, cosine_table, sine_table, causal, group_count, local_length
):
    wq_full, wk_full, wv_full, wo_full, gain_a, gain_m, wg_full, wu_full, wd_full = gathered_w
    (
        normed_a,
        scale_a,
        attention_input,
        query_rows,
        keyval_all,
        attn_mix,
        log_total,
        normed_m,
        scale_m,
        mlp_rows,
        gate_val,
        up_val,
        inner_act,
    ) = kept_acts
    row_total = grad_in.shape[0]
    down_in = grad_in.astype(jnp.bfloat16)
    wg_use, wu_use, wd_use = (wg_full, wu_full, wd_full)
    down_rows = lax.all_gather(down_in, "tp", axis=0, tiled=True)
    grad_wd = jnp.einsum("rf,rd->fd", inner_act, down_rows, preferred_element_type=jnp.float32)
    act_grad = jnp.einsum("rd,fd->rf", down_rows, wd_use, preferred_element_type=jnp.float32)
    sigm = jax.nn.sigmoid(gate_val)
    gate_grad = (act_grad * up_val * sigm * (1.0 + gate_val * (1.0 - sigm))).astype(jnp.bfloat16)
    up_grad = (act_grad * gate_val * sigm).astype(jnp.bfloat16)
    grad_wg = jnp.einsum("rd,rf->df", mlp_rows, gate_grad, preferred_element_type=jnp.float32)
    grad_wu = jnp.einsum("rd,rf->df", mlp_rows, up_grad, preferred_element_type=jnp.float32)
    mlp_in_grad = lax.psum_scatter(
        (
            jnp.einsum("rf,df->rd", gate_grad, wg_use, preferred_element_type=jnp.float32)
            + jnp.einsum("rf,df->rd", up_grad, wu_use, preferred_element_type=jnp.float32)
        ).astype(jnp.bfloat16),
        "tp",
        scatter_dimension=0,
        tiled=True,
    ).astype(jnp.float32)
    mid_part, grad_gm = norm_back(mlp_in_grad, normed_m, scale_m, gain_m.astype(jnp.float32))
    mid_grad = grad_in + mid_part
    proj_in = mid_grad.astype(jnp.bfloat16)
    grad_wo = jnp.einsum("rh,rd->hd", attn_mix, proj_in, preferred_element_type=jnp.float32)
    mixture_gradient = jnp.einsum(
        "rd,hd->rh", proj_in, wo_full, preferred_element_type=jnp.float32
    ).astype(jnp.bfloat16)

    def seq_backward(seq_items):
        return attend_back(seq_items[0], seq_items[1], seq_items[2], seq_items[3], causal)

    query_grad, keyval_grad = lax.map(
        seq_backward,
        (
            query_rows,
            keyval_all,
            mixture_gradient.reshape(group_count, local_length, QUERY_HEADS * HEAD_DIM),
            log_total,
        ),
    )
    key_value_local = lax.psum_scatter(
        keyval_grad.astype(jnp.bfloat16), "ctx", scatter_dimension=1, tiled=True
    ).astype(jnp.float32)
    key_value_width = KEY_VALUE_HEADS * HEAD_DIM
    key_gradient = rotate_back(
        key_value_local[..., :key_value_width].reshape(
            group_count, local_length, KEY_VALUE_HEADS, HEAD_DIM
        ),
        cosine_table,
        sine_table,
    )
    key_gradient = key_gradient.reshape(row_total, key_value_width).astype(jnp.bfloat16)
    value_gradient = (
        key_value_local[..., key_value_width:]
        .reshape(row_total, key_value_width)
        .astype(jnp.bfloat16)
    )
    query_back = rotate_back(
        query_grad.reshape(group_count, local_length, QUERY_HEADS, HEAD_DIM),
        cosine_table,
        sine_table,
    )
    query_back = query_back.reshape(row_total, QUERY_HEADS * HEAD_DIM).astype(jnp.bfloat16)
    grad_wq = jnp.einsum(
        "rd,rh->dh", attention_input, query_back, preferred_element_type=jnp.float32
    )
    grad_wk = jnp.einsum(
        "rd,rh->dh", attention_input, key_gradient, preferred_element_type=jnp.float32
    )
    grad_wv = jnp.einsum(
        "rd,rh->dh", attention_input, value_gradient, preferred_element_type=jnp.float32
    )
    in_grad = (
        jnp.einsum("rh,dh->rd", query_back, wq_full, preferred_element_type=jnp.float32)
        + jnp.einsum("rh,dh->rd", key_gradient, wk_full, preferred_element_type=jnp.float32)
        + jnp.einsum("rh,dh->rd", value_gradient, wv_full, preferred_element_type=jnp.float32)
    )
    low_part, grad_ga = norm_back(in_grad, normed_a, scale_a, gain_a.astype(jnp.float32))
    layer_grads = (grad_wq, grad_wk, grad_wv, grad_wo, grad_ga, grad_gm, grad_wg, grad_wu, grad_wd)
    return (mid_grad + low_part, layer_grads)


def local(
    tokens,
    span_ids,
    w_query,
    key_weight,
    value_weight,
    w_out,
    gain_attn,
    gain_mlp,
    w_gate,
    w_up,
    w_down,
    out_grad,
):
    group_count, local_length, model_width = tokens.shape
    n_ctx = lax.axis_size("ctx")
    sequence_length = local_length * n_ctx
    span_len = local_length // 2
    ctx_rank = lax.axis_index("ctx")
    slot_ids = jnp.arange(sequence_length, dtype=jnp.int32)
    picked = (slot_ids // span_len)[:, None] == jnp.arange(2 * n_ctx, dtype=jnp.int32)[None, :]
    key_place = (
        jnp.sum(jnp.where(picked, span_ids[None, :], 0), axis=1) * span_len + slot_ids % span_len
    )
    own_place = lax.dynamic_slice_in_dim(key_place, ctx_rank * local_length, local_length)
    causal = key_place[None, :] <= own_place[:, None]
    inverse_freq = THETA ** (-jnp.arange(HEAD_DIM // 2, dtype=jnp.float32) * 2.0 / HEAD_DIM)
    angles = own_place.astype(jnp.float32)[:, None] * inverse_freq[None, :]
    angles = jnp.concatenate([angles, angles], axis=-1)
    cosine_table = jnp.cos(angles)
    sine_table = jnp.sin(angles)
    row_total = group_count * local_length
    hidden = tokens.astype(jnp.float32).reshape(row_total, model_width)
    fetched = []
    fetched_full = []
    kept_list = []
    for layer_idx in range(DECODER_LAYERS):
        gathered_w = (
            lax.all_gather(w_query[layer_idx], ("shard", "ctx"), axis=0, tiled=True),
            lax.all_gather(key_weight[layer_idx], ("shard", "ctx"), axis=0, tiled=True),
            lax.all_gather(value_weight[layer_idx], ("shard", "ctx"), axis=0, tiled=True),
            lax.all_gather(w_out[layer_idx], ("shard", "ctx"), axis=1, tiled=True),
            lax.all_gather(gain_attn[layer_idx], ("shard", "ctx"), axis=0, tiled=True),
            lax.all_gather(gain_mlp[layer_idx], ("shard", "ctx"), axis=0, tiled=True),
            lax.all_gather(w_gate[layer_idx], ("shard", "ctx"), axis=0, tiled=True),
            lax.all_gather(w_up[layer_idx], ("shard", "ctx"), axis=0, tiled=True),
            lax.all_gather(w_down[layer_idx], ("shard", "ctx"), axis=1, tiled=True),
        )
        mlp_full = None
        hidden, kept_acts = forward_layer(
            hidden, gathered_w, cosine_table, sine_table, causal, group_count, local_length
        )
        fetched.append(gathered_w)
        fetched_full.append(mlp_full)
        kept_list.append(kept_acts)
    block_out = hidden.astype(jnp.bfloat16).reshape(group_count, local_length, model_width)
    grad_run = out_grad.astype(jnp.float32).reshape(row_total, model_width)
    collected = [None] * DECODER_LAYERS
    for layer_idx in reversed(range(DECODER_LAYERS)):
        gathered_w = (
            lax.all_gather(w_query[layer_idx], ("shard", "ctx"), axis=0, tiled=True),
            lax.all_gather(key_weight[layer_idx], ("shard", "ctx"), axis=0, tiled=True),
            lax.all_gather(value_weight[layer_idx], ("shard", "ctx"), axis=0, tiled=True),
            lax.all_gather(w_out[layer_idx], ("shard", "ctx"), axis=1, tiled=True),
            lax.all_gather(gain_attn[layer_idx], ("shard", "ctx"), axis=0, tiled=True),
            lax.all_gather(gain_mlp[layer_idx], ("shard", "ctx"), axis=0, tiled=True),
            lax.all_gather(w_gate[layer_idx], ("shard", "ctx"), axis=0, tiled=True),
            lax.all_gather(w_up[layer_idx], ("shard", "ctx"), axis=0, tiled=True),
            lax.all_gather(w_down[layer_idx], ("shard", "ctx"), axis=1, tiled=True),
        )
        mlp_full = None
        grad_run, layer_grads = backward_layer(
            grad_run,
            kept_list[layer_idx],
            gathered_w,
            cosine_table,
            sine_table,
            causal,
            group_count,
            local_length,
        )
        owned = (
            lax.psum_scatter(layer_grads[0], ("shard", "ctx"), scatter_dimension=0, tiled=True),
            lax.psum_scatter(layer_grads[1], ("shard", "ctx"), scatter_dimension=0, tiled=True),
            lax.psum_scatter(layer_grads[2], ("shard", "ctx"), scatter_dimension=0, tiled=True),
            lax.psum_scatter(layer_grads[3], ("shard", "ctx"), scatter_dimension=1, tiled=True),
            lax.psum_scatter(layer_grads[4], ("shard", "ctx"), scatter_dimension=0, tiled=True),
            lax.psum_scatter(layer_grads[5], ("shard", "ctx"), scatter_dimension=0, tiled=True),
            lax.psum_scatter(layer_grads[6], ("shard", "ctx"), scatter_dimension=0, tiled=True),
            lax.psum_scatter(layer_grads[7], ("shard", "ctx"), scatter_dimension=0, tiled=True),
            lax.psum_scatter(layer_grads[8], ("shard", "ctx"), scatter_dimension=1, tiled=True),
        )
        shared = (
            lax.psum(owned[0].astype(jnp.bfloat16), "tp").astype(jnp.float32),
            lax.psum(owned[1].astype(jnp.bfloat16), "tp").astype(jnp.float32),
            lax.psum(owned[2].astype(jnp.bfloat16), "tp").astype(jnp.float32),
            lax.psum(owned[3].astype(jnp.bfloat16), "tp").astype(jnp.float32),
            lax.psum(owned[4].astype(jnp.bfloat16), "tp").astype(jnp.float32),
            lax.psum(owned[5].astype(jnp.bfloat16), "tp").astype(jnp.float32),
        )
        mlp_owned = (owned[6], owned[7], owned[8])
        collected[layer_idx] = (
            shared[0],
            shared[1],
            shared[2],
            shared[3],
            shared[4],
            shared[5],
            mlp_owned[0],
            mlp_owned[1],
            mlp_owned[2],
        )
    tokens_grad = grad_run.reshape(group_count, local_length, model_width)
    stacked = [
        jnp.stack([collected[layer_idx][member] for layer_idx in range(DECODER_LAYERS)], axis=0)
        for member in range(9)
    ]
    return (
        block_out,
        tokens_grad,
        stacked[0],
        stacked[1],
        stacked[2],
        stacked[3],
        stacked[4],
        stacked[5],
        stacked[6],
        stacked[7],
        stacked[8],
    )


def solution(mesh):
    return jax.shard_map(
        local,
        mesh=mesh,
        in_specs=(
            P(("shard", "tp"), "ctx", None),
            P(),
            P(None, ("shard", "ctx"), None),
            P(None, ("shard", "ctx"), None),
            P(None, ("shard", "ctx"), None),
            P(None, None, ("shard", "ctx")),
            P(None, ("shard", "ctx")),
            P(None, ("shard", "ctx")),
            P(None, ("shard", "ctx"), "tp"),
            P(None, ("shard", "ctx"), "tp"),
            P(None, "tp", ("shard", "ctx")),
            P(("shard", "tp"), "ctx", None),
        ),
        out_specs=(
            P(("shard", "tp"), "ctx", None),
            P(("shard", "tp"), "ctx", None),
            P(None, ("shard", "ctx"), None),
            P(None, ("shard", "ctx"), None),
            P(None, ("shard", "ctx"), None),
            P(None, None, ("shard", "ctx")),
            P(None, ("shard", "ctx")),
            P(None, ("shard", "ctx")),
            P(None, ("shard", "ctx"), "tp"),
            P(None, ("shard", "ctx"), "tp"),
            P(None, "tp", ("shard", "ctx")),
        ),
        check_vma=False,
    )
```

profile of v0, /device:TPU:0, one launch (start us, length us, event | category | flops | bytes accessed | tf_op | source)
XLA Modules:
  0.0 2396.8 jit_solution(6120761117097378325)
XLA Ops:
  42.8 35.4 %all-gather.1 = bf16[1,960,320]{2,0,1:T(2,128)(2,1)S(1)} all-gather(bf16[1,120,320]{2,0,1:T(2,128)(2,1)} %copy.113), channel_id=3, replica_groups=mesh['shard'=4,'ctx'=2,'tp'=4] {'shard','ctx'}, dimensions={1}, use_global_device_ids=true | all-gather | bytes 691200 | tf_op jit(solution)/shard_map/all_gather | solution.py:313
  85.5 34.4 %all-gather.2 = bf16[1,960,320]{2,0,1:T(2,128)(2,1)S(1)} all-gather(bf16[1,120,320]{2,0,1:T(2,128)(2,1)S(1)} %copy.114), channel_id=4, replica_groups=mesh['shard'=4,'ctx'=2,'tp'=4] {'shard','ctx'}, dimensions={1}, use_global_device_ids=true | all-gather | bytes 691200 | tf_op jit(solution)/shard_map/all_gather | solution.py:314
  160.0 47.7 %all-gather.46.cloned.1.call-done = bf16[1,960,960]{2,1,0:T(8,128)(2,1)} async-done(((bf16[1,120,960]{2,1,0:T(8,128)(2,1)}), bf16[1,960,960]{2,1,0:T(8,128)(2,1)}) %all-gather.46.cloned.1.call-update) | async-done | bytes 1843216 | tf_op jit(solution)/shard_map/all_gather | solution.py:312
  212.1 27.6 %fusion.200 = (f32[5,3,768]{2,1,0:T(4,128)S(1)}, f32[5,3,768,1536]{2,3,1,0:T(8,128)}) fusion(bf16[1536,5,64,1]{0,2,3,1:T(8,128)(2,1)S(1)} %bitcast.471, bf16[768,5,3,64]{0,3,2,1:T(8,128)(2,1)S(1)} %fusion.56, pred[768,1536]{0,1:T(8,128)(4,1)} %broadcast_compare_fusion), kind=kOutput, calls=%fused_computation.307 | convolution fusion | flops 2317996800 | bytes 74462208 | tf_op jit(solution)/shard_map/while/body/eval_jaxpr/qkgd,tkd->kgqt/dot_general | solution.py:55
  322.2 45.0 %all-gather.38.cloned.1.call-done = bf16[3072,960]{0,1:T(8,128)(2,1)} async-done(((bf16[768,960]{0,1:T(8,128)(2,1)}), bf16[3072,960]{0,1:T(8,128)(2,1)}) %all-gather.38.cloned.1.call-update) | async-done | bytes 5898256 | tf_op jit(solution)/shard_map/all_gather | solution.py:145
  376.7 34.5 %all-gather.52.cloned.1.call-done = bf16[1,960,640]{2,1,0:T(8,128)(2,1)} async-done(((bf16[1,120,640]{2,1,0:T(8,128)(2,1)}), bf16[1,960,640]{2,1,0:T(8,128)(2,1)}) %all-gather.52.cloned.1.call-update) | async-done | bytes 1228816 | tf_op jit(solution)/shard_map/all_gather | solution.py:319
  422.9 31.4 %all-gather.54.cloned.1.call-done = bf16[1,640,960]{1,2,0:T(8,128)(2,1)} async-done(((bf16[1,640,120]{1,2,0:T(8,128)(2,1)}), bf16[1,640,960]{1,2,0:T(8,128)(2,1)}) %all-gather.54.cloned.1.call-update) | async-done | bytes 1228816 | tf_op jit(solution)/shard_map/all_gather | solution.py:320
  467.4 37.1 %all-gather.11 = bf16[1,960,320]{2,0,1:T(2,128)(2,1)} all-gather(bf16[1,120,320]{2,0,1:T(2,128)(2,1)S(1)} %copy.117), channel_id=13, replica_groups=mesh['shard'=4,'ctx'=2,'tp'=4] {'shard','ctx'}, dimensions={1}, use_global_device_ids=true | all-gather | bytes 691200 | tf_op jit(solution)/shard_map/all_gather | solution.py:314
  509.2 37.6 %all-gather.10 = bf16[1,960,320]{2,0,1:T(2,128)(2,1)} all-gather(bf16[1,120,320]{2,0,1:T(2,128)(2,1)S(1)} %copy.116), channel_id=12, replica_groups=mesh['shard'=4,'ctx'=2,'tp'=4] {'shard','ctx'}, dimensions={1}, use_global_device_ids=true | all-gather | bytes 691200 | tf_op jit(solution)/shard_map/all_gather | solution.py:313
  559.4 34.8 %all-gather.58.cloned.1.call-done = bf16[1,960,960]{1,0,2:T(2,128)(2,1)} async-done(((bf16[1,960,120]{1,0,2:T(2,128)(2,1)}), bf16[1,960,960]{1,0,2:T(2,128)(2,1)}) %all-gather.58.cloned.1.call-update) | async-done | bytes 1843216 | tf_op jit(solution)/shard_map/all_gather | solution.py:315
  605.1 37.6 %all-gather.56.cloned.1.call-done = bf16[1,960,960]{2,1,0:T(8,128)(2,1)} async-done(((bf16[1,120,960]{2,1,0:T(8,128)(2,1)}), bf16[1,960,960]{2,1,0:T(8,128)(2,1)}) %all-gather.56.cloned.1.call-update) | async-done | bytes 1843216 | tf_op jit(solution)/shard_map/all_gather | solution.py:312
  646.9 28.7 %all-gather.40.cloned.1.call-done = bf16[1,1536,640]{1,2,0:T(8,128)(2,1)} async-done(((bf16[1,768,640]{1,2,0:T(8,128)(2,1)}), bf16[1,1536,640]{1,2,0:T(8,128)(2,1)}) %all-gather.40.cloned.1.call-update) | async-done | bytes 1966096 | tf_op jit(solution)/shard_map/all_gather | solution.py:134
  678.2 27.4 %fusion.201 = (f32[5,3,768]{2,1,0:T(4,128)S(1)}, f32[5,3,768,1536]{2,3,1,0:T(8,128)}) fusion(bf16[1536,5,64,1]{0,2,3,1:T(8,128)(2,1)S(1)} %bitcast.473, bf16[768,5,3,64]{0,3,2,1:T(8,128)(2,1)S(1)} %fusion.58, pred[768,1536]{0,1:T(8,128)(4,1)} %broadcast_compare_fusion), kind=kOutput, calls=%fused_computation.308 | convolution fusion | flops 2317996800 | bytes 74462208 | tf_op jit(solution)/shard_map/while/body/eval_jaxpr/qkgd,tkd->kgqt/dot_general | solution.py:55
  761.6 42.5 %all-gather.42.cloned.1.call-done = bf16[3072,960]{0,1:T(8,128)(2,1)} async-done(((bf16[768,960]{0,1:T(8,128)(2,1)}), bf16[3072,960]{0,1:T(8,128)(2,1)}) %all-gather.42.cloned.1.call-update) | async-done | bytes 5898256 | tf_op jit(solution)/shard_map/all_gather | solution.py:145
  813.5 34.3 %all-gather.60.cloned.1.call-done = bf16[1,960,640]{2,1,0:T(8,128)(2,1)} async-done(((bf16[1,120,640]{2,1,0:T(8,128)(2,1)}), bf16[1,960,640]{2,1,0:T(8,128)(2,1)}) %all-gather.60.cloned.1.call-update) | async-done | bytes 1228816 | tf_op jit(solution)/shard_map/all_gather | solution.py:318
  857.2 33.1 %all-gather.64.cloned.1.call-done = bf16[1,640,960]{1,2,0:T(8,128)(2,1)} async-done(((bf16[1,640,120]{1,2,0:T(8,128)(2,1)}), bf16[1,640,960]{1,2,0:T(8,128)(2,1)}) %all-gather.64.cloned.1.call-update) | async-done | bytes 1228816 | tf_op jit(solution)/shard_map/all_gather | solution.py:320
  890.4 44.5 %all-gather.66.cloned.1.call-done = bf16[1,3072,960]{1,2,0:T(8,128)(2,1)} async-done(((bf16[1,768,960]{1,2,0:T(8,128)(2,1)}), bf16[1,3072,960]{1,2,0:T(8,128)(2,1)}) %all-gather.66.cloned.1.call-update) | async-done | bytes 5898256 | tf_op jit(solution)/shard_map/all_gather | solution.py:195
  978.3 45.0 %reduce-scatter.41.cloned.1.call-done = bf16[768,960]{0,1:T(8,128)(2,1)} async-done(((bf16[3072,960]{0,1:T(8,128)(2,1)}), bf16[768,960]{0,1:T(8,128)(2,1)}) %reduce-scatter.41.cloned.1.call-update) | async-done | bytes 1474576 | tf_op jit(solution)/shard_map/reduce_scatter | solution.py:203
  1026.3 55.2 %reduce-scatter.39.cloned.1.call-done = bf16[768,960]{0,1:T(8,128)(2,1)} async-done(((bf16[3072,960]{0,1:T(8,128)(2,1)}), bf16[768,960]{0,1:T(8,128)(2,1)}) %reduce-scatter.39.cloned.1.call-update) | async-done | bytes 1474576 | tf_op jit(solution)/shard_map/reduce_scatter | solution.py:149
  1112.5 45.1 %fusion.3 = (f32[5,3,768]{2,1,0:T(4,128)S(1)}, f32[5,1536,768,3]{2,1,3,0:T(8,128)}) fusion(f32[5,3,768,1536]{2,3,1,0:T(8,128)} %get-tuple-element.193, f32[5,3,768]{2,1,0:T(4,128)S(1)} %log_add_fusion.1, bf16[1536,5,64,1]{0,2,3,1:T(8,128)(2,1)} %bitcast.483, bf16[768,5,3,64]{0,3,2,1:T(8,128)(2,1)S(1)} %bitcast.465), kind=kOutput, calls=%fused_computation.7 | convolution fusion | flops 2317996800 | bytes 144107520 | tf_op jit(solution)/shard_map/while/body/eval_jaxpr/qkgd,tkd->kgqt/dot_general | solution.py:82
  1157.6 56.4 %fusion.5 = bf16[5,3,768,1536]{2,3,1,0:T(8,128)(2,1)} fusion(f32[5,1536,768,3]{2,1,3,0:T(8,128)} %get-tuple-element.197, f32[5,3,768,1536]{2,3,1,0:T(8,128)} %get-tuple-element.193, f32[5,3,768]{2,1,0:T(4,128)S(1)} %get-tuple-element.196, f32[5,3,768]{2,1,0:T(4,128)S(1)} %log_add_fusion.1), kind=kLoop, calls=%fused_computation.9 | loop fusion | flops 70778880 | bytes 177039360 | tf_op jit(solution)/shard_map/while/body/eval_jaxpr/convert_element_type | solution.py:86
  1273.2 44.3 %all-gather.44.cloned.1.call-done = bf16[3072,960]{0,1:T(8,128)(2,1)} async-done(((bf16[768,960]{0,1:T(8,128)(2,1)}), bf16[3072,960]{0,1:T(8,128)(2,1)}) %all-gather.44.cloned.1.call-update) | async-done | bytes 5898256 | tf_op jit(solution)/shard_map/all_gather | solution.py:195
  1428.5 49.7 %fusion = (f32[5,3,768]{2,1,0:T(4,128)S(1)}, f32[5,1536,768,3]{2,1,3,0:T(8,128)}) fusion(f32[5,3,768,1536]{2,3,1,0:T(8,128)} %get-tuple-element.187, f32[5,3,768]{2,1,0:T(4,128)S(1)} %log_add_fusion, bf16[1536,5,64,1]{0,2,3,1:T(8,128)(2,1)S(1)} %bitcast.482, bf16[768,5,3,64]{0,3,2,1:T(8,128)(2,1)S(1)} %bitcast.462), kind=kOutput, calls=%fused_computation.2 | convolution fusion | flops 2317996800 | bytes 144107520 | tf_op jit(solution)/shard_map/while/body/eval_jaxpr/qkgd,tkd->kgqt/dot_general | solution.py:82
  1478.2 57.7 %fusion.2 = bf16[5,3,768,1536]{2,3,1,0:T(8,128)(2,1)} fusion(f32[5,1536,768,3]{2,1,3,0:T(8,128)} %get-tuple-element.200, f32[5,3,768,1536]{2,3,1,0:T(8,128)} %get-tuple-element.187, f32[5,3,768]{2,1,0:T(4,128)S(1)} %get-tuple-element.199, f32[5,3,768]{2,1,0:T(4,128)S(1)} %log_add_fusion), kind=kLoop, calls=%fused_computation.4 | loop fusion | flops 70778880 | bytes 177039360 | tf_op jit(solution)/shard_map/while/body/eval_jaxpr/convert_element_type | solution.py:86
  1619.8 34.3 %reduce-scatter.67.cloned.1.call-done = f32[640,120]{0,1:T(8,128)} async-done(((f32[640,960]{0,1:T(8,128)}), f32[640,120]{0,1:T(8,128)}) %reduce-scatter.67.cloned.1.call-update) | async-done | bytes 307216
  1654.1 72.6 %reduce-scatter.65.cloned.1.call-done = f32[640,120]{0,1:T(8,128)} async-done(((f32[640,960]{0,1:T(8,128)}), f32[640,120]{0,1:T(8,128)}) %reduce-scatter.65.cloned.1.call-update) | async-done | bytes 307216
  1728.6 70.5 %reduce-scatter.59.cloned.1.call-done = f32[120,640]{1,0:T(8,128)} async-done(((f32[960,640]{1,0:T(8,128)}), f32[120,640]{1,0:T(8,128)}) %reduce-scatter.59.cloned.1.call-update) | async-done | bytes 307216
  1799.1 72.4 %reduce-scatter.57.cloned.1.call-done = f32[120,640]{1,0:T(8,128)} async-done(((f32[960,640]{1,0:T(8,128)}), f32[120,640]{1,0:T(8,128)}) %reduce-scatter.57.cloned.1.call-update) | async-done | bytes 307216
  1873.5 70.8 %reduce-scatter.63.cloned.1.call-done = f32[120,640]{1,0:T(8,128)} async-done(((f32[960,640]{1,0:T(8,128)}), f32[120,640]{1,0:T(8,128)}) %reduce-scatter.63.cloned.1.call-update) | async-done | bytes 307216
  1944.3 72.7 %reduce-scatter.61.cloned.1.call-done = f32[120,640]{1,0:T(8,128)} async-done(((f32[960,640]{1,0:T(8,128)}), f32[120,640]{1,0:T(8,128)}) %reduce-scatter.61.cloned.1.call-update) | async-done | bytes 307216
  2060.4 251.1 %all-reduce.26 = (bf16[960,320]{0,1:T(8,128)(2,1)}, bf16[960,320]{0,1:T(8,128)(2,1)}, bf16[960,320]{0,1:T(8,128)(2,1)}, bf16[960,320]{0,1:T(8,128)(2,1)}, bf16[9...) all-reduce(f32[960,320]{0,1:T(8,128)S(1)} %copy-done.24, ...), channel_id=30, replica_groups=mesh['shard'=4,'ctx'=2,'tp'=4] {'shard','ctx'}, use_global_device_ids=true, to_apply=%region_27.28.clone | all-reduce | flops 1232640 | bytes 7395840
  2346.8 35.3 %all-reduce.25.cloned.1.call-done = (bf16[1,120,960]{2,1,0:T(8,128)(2,1)}, bf16[1,120,960]{2,1,0:T(8,128)(2,1)}, bf16[1,120,320]{1,2,0:T(8,128)(2,1)}, bf16[1,12...) async-done(((bf16[1,120,960]{2,1,0:T(8,128)(2,1)}, ...) | async-done | bytes 1228816 | tf_op jit(solution)/shard_map/psum | solution.py:367
  (427 shorter events, 732.7 us)
Async XLA Ops:
  7.2 150.2 %all-gather.36.cloned.1.call-start = ((), (), s32[]{:S(2)}) async-start(), calls=%async_computation.16 | async-start | bytes 2949120 | tf_op jit(solution)/shard_map/all_gather | solution.py:134
  127.6 161.8 %all-gather.48.cloned.1.call-start = ((), (), s32[]{:S(2)}) async-start(), calls=%async_computation.30 | async-start | bytes 4423680 | tf_op jit(solution)/shard_map/all_gather | solution.py:315
  129.8 192.4 %all-gather.50.cloned.1.call-start = ((), (), s32[]{:S(2)}) async-start(), calls=%async_computation.31 | async-start | bytes 1382400 | tf_op jit(solution)/shard_map/all_gather | solution.py:318
  130.6 236.5 %all-gather.38.cloned.1.call-start = ((), (), s32[]{:S(2)}) async-start(), calls=%async_computation.17 | async-start | bytes 7372800 | tf_op jit(solution)/shard_map/all_gather | solution.py:145
  306.3 104.9 %all-gather.52.cloned.1.call-start = ((), (), s32[]{:S(2)}) async-start(), calls=%async_computation.32 | async-start | bytes 1382400 | tf_op jit(solution)/shard_map/all_gather | solution.py:319
  307.1 147.1 %all-gather.54.cloned.1.call-start = ((), (), s32[]{:S(2)}) async-start(), calls=%async_computation.33 | async-start | bytes 1382400 | tf_op jit(solution)/shard_map/all_gather | solution.py:320
  308.9 242.6 %reduce-scatter.37.cloned.1.call-start = ((), (), s32[]{:S(2)}) async-start(), calls=%async_computation.18 | async-start | bytes 7372800 | tf_op jit(solution)/shard_map/reduce_scatter | solution.py:149
  464.0 130.1 %all-gather.58.cloned.1.call-start = ((), (), s32[]{:S(2)}) async-start(), calls=%async_computation.35 | async-start | bytes 4423680 | tf_op jit(solution)/shard_map/all_gather | solution.py:315
  466.4 176.3 %all-gather.56.cloned.1.call-start = ((), (), s32[]{:S(2)}) async-start(), calls=%async_computation.34 | async-start | bytes 2211840 | tf_op jit(solution)/shard_map/all_gather | solution.py:312
  467.0 208.7 %all-gather.40.cloned.1.call-start = ((), (), s32[]{:S(2)}) async-start(), calls=%async_computation.19 | async-start | bytes 2949120 | tf_op jit(solution)/shard_map/all_gather | solution.py:134
  558.7 202.8 %all-gather.62.cloned.1.call-start = ((), (), s32[]{:S(2)}) async-start(), calls=%async_computation.37 | async-start | bytes 1382400 | tf_op jit(solution)/shard_map/all_gather | solution.py:319
  559.3 244.8 %all-gather.42.cloned.1.call-start = ((), (), s32[]{:S(2)}) async-start(), calls=%async_computation.20 | async-start | bytes 7372800 | tf_op jit(solution)/shard_map/all_gather | solution.py:145
  759.8 88.1 %all-gather.60.cloned.1.call-start = ((), (), s32[]{:S(2)}) async-start(), calls=%async_computation.36 | async-start | bytes 1382400 | tf_op jit(solution)/shard_map/all_gather | solution.py:318
  760.3 130.0 %all-gather.64.cloned.1.call-start = ((), (), s32[]{:S(2)}) async-start(), calls=%async_computation.38 | async-start | bytes 1382400 | tf_op jit(solution)/shard_map/all_gather | solution.py:320
  760.9 173.9 %all-gather.66.cloned.1.call-start = ((), (), s32[]{:S(2)}) async-start(), calls=%async_computation.39 | async-start | bytes 7372800 | tf_op jit(solution)/shard_map/all_gather | solution.py:195
  761.5 261.8 %reduce-scatter.41.cloned.1.call-start = ((), (), s32[]{:S(2)}) async-start(), calls=%async_computation.22 | async-start | bytes 7372800 | tf_op jit(solution)/shard_map/reduce_scatter | solution.py:203
  967.4 114.1 %reduce-scatter.39.cloned.1.call-start = ((), (), s32[]{:S(2)}) async-start(), calls=%async_computation.21 | async-start | bytes 7372800 | tf_op jit(solution)/shard_map/reduce_scatter | solution.py:149
  978.2 284.4 %reduce-scatter.43.cloned.1.call-start = ((), (), s32[]{:S(2)}) async-start(), calls=%async_computation.23 | async-start | bytes 2949120 | tf_op jit(solution)/shard_map/reduce_scatter | solution.py:232
  1232.0 85.4 %all-gather.44.cloned.1.call-start = ((), (), s32[]{:S(2)}) async-start(), calls=%async_computation.24 | async-start | bytes 7372800 | tf_op jit(solution)/shard_map/all_gather | solution.py:195
  1273.1 148.8 %reduce-scatter.45.cloned.1.call-start = ((), (), s32[]{:S(2)}) async-start(), calls=%async_computation.25 | async-start | bytes 7372800 | tf_op jit(solution)/shard_map/reduce_scatter | solution.py:203
  1348.6 267.5 %reduce-scatter.55.cloned.1.call-start = ((), (), s32[]{:S(2)}) async-start(), calls=%async_computation.41 | async-start | bytes 4423680
  1353.8 264.2 %reduce-scatter.51.cloned.1.call-start = ((), (), s32[]{:S(2)}) async-start(), calls=%async_computation.28 | async-start | bytes 4423680 | tf_op jit(solution)/shard_map/reduce_scatter | solution.py:356
  1359.7 294.3 %reduce-scatter.67.cloned.1.call-start = ((), (), s32[]{:S(2)}) async-start(), calls=%async_computation.47 | async-start | bytes 2764800
  1370.4 356.2 %reduce-scatter.65.cloned.1.call-start = ((), (), s32[]{:S(2)}) async-start(), calls=%async_computation.46 | async-start | bytes 2764800
  1380.5 418.6 %reduce-scatter.59.cloned.1.call-start = ((), (), s32[]{:S(2)}) async-start(), calls=%async_computation.43 | async-start | bytes 2764800
  1390.7 480.9 %reduce-scatter.57.cloned.1.call-start = ((), (), s32[]{:S(2)}) async-start(), calls=%async_computation.42 | async-start | bytes 2764800
  1400.9 543.4 %reduce-scatter.63.cloned.1.call-start = ((), (), s32[]{:S(2)}) async-start(), calls=%async_computation.45 | async-start | bytes 2764800
  1411.1 606.0 %reduce-scatter.61.cloned.1.call-start = ((), (), s32[]{:S(2)}) async-start(), calls=%async_computation.44 | async-start | bytes 2764800
  1421.4 627.2 %reduce-scatter.47.cloned.1.call-start = ((), (), s32[]{:S(2)}) async-start(), calls=%async_computation.26 | async-start | bytes 2949120 | tf_op jit(solution)/shard_map/reduce_scatter | solution.py:232
  1582.7 738.3 %reduce-scatter.53.cloned.1.call-start = ((), (), s32[]{:S(2)}) async-start(), calls=%async_computation.40 | async-start | bytes 4423680
  1588.0 750.8 %reduce-scatter.49.cloned.1.call-start = ((), (), s32[]{:S(2)}) async-start(), calls=%async_computation.27 | async-start | bytes 4423680 | tf_op jit(solution)/shard_map/reduce_scatter | solution.py:356
  1610.2 771.9 %all-reduce.25.cloned.1.call-start = ((), (), s32[]{:S(2)}) async-start(), calls=%async_computation.48 | async-start | bytes 2621440 | tf_op jit(solution)/shard_map/psum | solution.py:367
  (91 other events, 2035.2 us)
Sparse Core Ops, SparseCore 0:
  126.8 30.5 all-gather.35
  160.2 47.4 all-gather.45
  210.5 69.1 all-gather.47
  282.3 39.7 all-gather.49
  324.1 42.9 all-gather.37
  369.7 41.4 all-gather.51
  414.0 40.2 all-gather.53
  464.2 54.5 reduce-scatter.36
  521.8 72.3 all-gather.57
  597.0 45.6 all-gather.55
  644.9 30.7 all-gather.39
  678.5 41.4 all-gather.61
  759.9 44.1 all-gather.41
  806.4 41.4 all-gather.59
  850.1 40.2 all-gather.63
  891.9 42.9 all-gather.65
  967.5 55.7 reduce-scatter.40
  1025.7 55.7 reduce-scatter.38
  1232.1 30.3 reduce-scatter.42
  1273.2 44.1 all-gather.43
  1348.7 55.7 reduce-scatter.44
  1408.6 84.3 reduce-scatter.54
  1496.7 83.9 reduce-scatter.50
  1584.6 69.4 reduce-scatter.66
  1658.1 68.4 reduce-scatter.64
  1730.6 68.4 reduce-scatter.58
  1803.0 68.4 reduce-scatter.56
  1875.6 68.6 reduce-scatter.62
  1948.4 68.6 reduce-scatter.60
  2052.2 145.9 reduce-scatter.52
  2202.4 136.3 reduce-scatter.48
  2342.1 39.9 all-reduce.24
  (1 shorter events, 29.2 us)
where the time goes:
time: 2410 us; the launch traced here: 2400 us
  waiting for transfers between devices  1080 us (45%)
  matrix products  566 us (23%)
  blocking collectives  425 us (18%)
  other arithmetic  226 us (9%)
  local copies, waits for them, and re-layouts  83.3 us (3%)
    unnamed x41, waiting for transfers between devices  397 us
    unnamed x2, blocking collectives  275 us
    convert_element_type x2, other arithmetic, attend_back(): score_grad = (attn_prob * (prob_grad - inner_sum)).astype(jnp.bfloat16)  114 us
    dot_general x2, matrix products, attend_back(): jnp.einsum('qkgd,tkd->kgqt', grouped_gradient, value_matrix, preferred_el...  94.7 us
    all_gather x2, waiting for transfers between devices, backward_layer(): down_rows = lax.all_gather(down_in, 'tp', axis=0, tiled=True)  88.8 us
    all_gather x2, waiting for transfers between devices, forward_layer(): mlp_rows = lax.all_gather(mlp_in, 'tp', axis=0, tiled=True)  87.5 us
    all_gather x2, waiting for transfers between devices, local(): lax.all_gather(w_query[layer_idx], ('shard', 'ctx'), axis=0, tiled=True)  85.3 us
    all_gather x2, blocking collectives, local(): lax.all_gather(key_weight[layer_idx], ('shard', 'ctx'), axis=0, tiled=True)  73 us
  transfers between devices with their start and end apart: 33, of which 26 were waited for; matrix products, arithmetic and copies ran while one was open for 25% of the time, Pallas kernels for 0%

commit v1 on v0

v1 whole, which is shorter than its diff:
```python
import functools

import jax
import jax.numpy as jnp
from jax import lax
from jax.experimental import pallas as pl
from jax.experimental.pallas import tpu as pltpu
from jax.sharding import PartitionSpec as P

QUERY_HEADS = 15
KEY_VALUE_HEADS = 5
GROUP = QUERY_HEADS // KEY_VALUE_HEADS
HEAD_DIM = 64
DECODER_LAYERS = 2
WIDE = 1024

EPS = 1e-05
THETA = 10000.0
MASKED = -1e30
LOG2E = 1.4426950408889634
SCALE = HEAD_DIM**-0.5
BF = jnp.bfloat16
F32 = jnp.float32
VMEM_LIMIT = 60 * 1024 * 1024

NN = (((1,), (0,)), ((), ()))
NT = (((1,), (1,)), ((), ()))
TN = (((0,), (0,)), ((), ()))


def mm(left, right, dims=NN):
    return lax.dot_general(left, right, dims, preferred_element_type=F32)


CORE_SWAP = [(0, 1), (1, 0), (2, 3), (3, 2)]
PAIR_SWAP = [(0, 2), (2, 0), (1, 3), (3, 1)]


def pick(array, index, axis):
    return lax.dynamic_index_in_dim(array, index, axis, keepdims=False)


def line_reduce(array, axis, name):
    count = array.shape[axis]
    rank = lax.axis_index(name)
    total = pick(array, rank, axis).astype(F32)
    for shift in range(1, count):
        sent = pick(array, (rank + shift) % count, axis)
        total += lax.ppermute(
            sent, name, [(i, (i + shift) % count) for i in range(count)]
        ).astype(F32)
    return total.astype(BF)


def pair_reduce(array, axis):
    pair = lax.axis_index("tp") // 2
    return pick(array, pair, axis) + lax.ppermute(pick(array, 1 - pair, axis), "tp", PAIR_SWAP)


class Reduction:
    def __init__(self, there, here, n_shard, n_ctx, rows):
        self.shape = (2, n_shard, n_ctx, rows, there.shape[-1])
        self.stage = 0
        self.values = (there.reshape(self.shape), here.reshape(self.shape))

    def advance(self):
        self.stage += 1
        if self.stage == 1:
            there, here = self.values
            self.values = (here, lax.ppermute(there, "tp", CORE_SWAP))
        elif self.stage == 2:
            here, came = self.values
            half = self.shape[1] // 2
            first = here[:, :half] + came[:, :half]
            second = here[:, half:] + came[:, half:]
            self.values = (pair_reduce(first, 0), line_reduce(second, 2, "ctx"))
        elif self.stage == 3:
            first, second = self.values
            self.values = (line_reduce(first, 1, "ctx"), pair_reduce(second, 0))
        elif self.stage == 4:
            self.values = (line_reduce(jnp.concatenate(self.values, axis=0), 0, "shard"),)
        return self.values


def gather_pair(array):
    pair = lax.axis_index("tp") // 2
    far = lax.ppermute(array, "tp", PAIR_SWAP)
    return jnp.stack([jnp.where(pair == 0, array, far), jnp.where(pair == 0, far, array)])


def gather_core(array, axis):
    core = lax.axis_index("tp") % 2
    far = lax.ppermute(array, "tp", CORE_SWAP)
    return jnp.stack([jnp.where(core == 0, array, far), jnp.where(core == 0, far, array)], axis=axis)


def gather_line(array, name, axis):
    count = lax.axis_size(name)
    rank = lax.axis_index(name)
    pieces = jnp.stack(
        [array]
        + [
            lax.ppermute(array, name, [(i, (i + shift) % count) for i in range(count)])
            for shift in range(1, count)
        ]
    )
    return jnp.stack([pick(pieces, (rank - j) % count, 0) for j in range(count)], axis=axis)


class Gathering:
    def __init__(self, share):
        self.stage = 0
        self.values = (share,)

    def advance(self):
        self.stage += 1
        if self.stage == 1:
            pieces = gather_line(self.values[0], "shard", 0)
            half = pieces.shape[1] // 2
            self.values = (pieces[:, :half], pieces[:, half:])
        elif self.stage == 2:
            first, second = self.values
            self.values = (gather_line(first, "ctx", 1), gather_pair(second))
        elif self.stage == 3:
            first, second = self.values
            self.values = (gather_pair(first), gather_line(second, "ctx", 2))
        elif self.stage == 4:
            joined = gather_core(jnp.concatenate(self.values, axis=3), 1)
            self.values = (joined.reshape(4, WIDE, joined.shape[-1]),)
        return self.values


def call(kernel, grid, in_specs, out_specs, out_shape, scratch, flops, moved, operands, after=(), scalars=()):
    used = len(scalars) + len(operands)

    def body(*refs):
        kernel(*refs[:used], *refs[used + len(after) :])

    return pl.pallas_call(
        body,
        grid_spec=pltpu.PrefetchScalarGridSpec(
            num_scalar_prefetch=len(scalars),
            grid=grid,
            in_specs=list(in_specs) + [pl.BlockSpec(memory_space=pl.ANY)] * len(after),
            out_specs=out_specs,
            scratch_shapes=scratch,
        ),
        out_shape=out_shape,
        compiler_params=pltpu.CompilerParams(vmem_limit_bytes=VMEM_LIMIT),
        cost_estimate=pl.CostEstimate(flops=flops, bytes_accessed=moved, transcendentals=0),
    )(*scalars, *operands, *after)


def full(*shape):
    return pl.BlockSpec(shape, lambda *at: (0,) * len(shape))


def row_steps(rows):
    step = 256 if rows % 256 == 0 else rows
    return [pl.ds(at, step) for at in range(0, rows, step)]


def mlp_forward_kernel(normed_ref, mid_ref, gate_w, up_w, down_w, out_ref, gate_ref, up_ref):
    @pl.when(pl.program_id(0) == 0)
    def _():
        out_ref[...] = mid_ref[...]

    for part in row_steps(normed_ref.shape[0]):
        normed = normed_ref[part, :]
        gate = mm(normed, gate_w[0])
        up = mm(normed, up_w[0])
        gate_ref[0, part, :] = gate
        up_ref[0, part, :] = up
        inner = (gate * jax.nn.sigmoid(gate) * up).astype(BF)
        out_ref[part, :] += mm(inner, down_w[0], NT)


def weight_specs(columns):
    return [
        pl.BlockSpec((1, WIDE, columns), functools.partial(lambda c, t: (t, 0, c), c))
        for c in range(3)
    ]


def mlp_forward(normed, mid, weights, after=()):
    rows = normed.shape[0]
    columns = weights.shape[2] // 3
    parts = weights.shape[0]
    whole = pl.BlockSpec((rows, WIDE), lambda t: (0, 0))
    kept = pl.BlockSpec((1, rows, columns), lambda t: (t, 0, 0))
    return call(
        mlp_forward_kernel,
        (parts,),
        [whole, whole] + weight_specs(columns),
        [whole, kept, kept],
        [
            jax.ShapeDtypeStruct((rows, WIDE), F32),
            jax.ShapeDtypeStruct((parts, rows, columns), F32),
            jax.ShapeDtypeStruct((parts, rows, columns), F32),
        ],
        [],
        6 * rows * WIDE * columns * parts,
        weights.size * 2 + rows * (WIDE * 10 + columns * parts * 8),
        (normed, mid, weights, weights, weights),
        after,
    )


def mlp_backward_kernel(
    order_ref,
    grad_ref,
    normed_ref,
    base_ref,
    gate_ref,
    up_ref,
    gate_w,
    up_w,
    down_w,
    back_ref,
    out_w,
    inner,
    gate_g,
    up_g,
):
    @pl.when(pl.program_id(0) == 0)
    def _():
        back_ref[...] = base_ref[...]

    columns = gate_ref.shape[2]
    for part in row_steps(grad_ref.shape[0]):
        act_grad = mm(grad_ref[part, :], down_w[0])
        gate = gate_ref[0, part, :]
        up = up_ref[0, part, :]
        sig = jax.nn.sigmoid(gate)
        silu = gate * sig
        inner[part, :] = (silu * up).astype(BF)
        gate_part = (act_grad * up * sig * (1.0 + gate * (1.0 - sig))).astype(BF)
        up_part = (act_grad * silu).astype(BF)
        gate_g[part, :] = gate_part
        up_g[part, :] = up_part
        back_ref[part, :] += mm(gate_part, gate_w[0], NT) + mm(up_part, up_w[0], NT)
    for at in range(0, WIDE, 256):
        part = pl.ds(at, 256)
        normed = normed_ref[:, part]
        out_w[0, part, 0:columns] = mm(normed, gate_g[...], TN).astype(BF)
        out_w[0, part, columns : 2 * columns] = mm(normed, up_g[...], TN).astype(BF)
        out_w[0, part, 2 * columns : 3 * columns] = mm(grad_ref[:, part], inner[...], TN).astype(BF)


def mlp_backward(order, grad, normed, base, gate, up, weights, after=()):
    rows = normed.shape[0]
    columns = weights.shape[2] // 3
    parts = order.shape[0]
    whole = full(rows, WIDE)
    kept = pl.BlockSpec((1, rows, columns), lambda i, order: (order[i], 0, 0))
    weight_parts = [
        pl.BlockSpec((1, WIDE, columns), functools.partial(lambda c, i, order: (order[i], 0, c), c))
        for c in range(3)
    ]
    return call(
        mlp_backward_kernel,
        (parts,),
        [whole, whole, whole, kept, kept] + weight_parts,
        [whole, pl.BlockSpec((1, WIDE, 3 * columns), lambda i, order: (i, 0, 0))],
        [
            jax.ShapeDtypeStruct((rows, WIDE), F32),
            jax.ShapeDtypeStruct((parts, WIDE, 3 * columns), BF),
        ],
        [pltpu.VMEM((rows, columns), BF)] * 3,
        12 * rows * WIDE * columns * parts,
        parts * WIDE * columns * 12 + rows * (WIDE * 12 + columns * parts * 8),
        (grad, normed, base, gate, up, weights, weights, weights),
        after,
        (order,),
    )


def turn_pairs(values):
    lane = lax.broadcasted_iota(jnp.int32, values.shape, 1) % HEAD_DIM
    return jnp.where(
        lane < HEAD_DIM // 2, -pltpu.roll(values, 96, 1), pltpu.roll(values, 32, 1)
    )


def low_lanes(values):
    lane = lax.broadcasted_iota(jnp.int32, values.shape, 1)
    return jnp.where(lane < HEAD_DIM, values, jnp.zeros_like(values))


def high_lanes(values):
    lane = lax.broadcasted_iota(jnp.int32, values.shape, 1)
    return jnp.where(lane < HEAD_DIM, jnp.zeros_like(values), values)


def other_half(values):
    return jnp.concatenate([values[:, HEAD_DIM:], values[:, :HEAD_DIM]], axis=1)


def row_scale(hidden, width):
    return lax.rsqrt(jnp.sum(hidden * hidden, axis=-1, keepdims=True) / width + EPS)


def project_kernel(width, hidden_ref, gain_ref, weights_ref, cos_ref, sin_ref, normed_ref, query_ref, pair_ref):
    for rows in row_steps(hidden_ref.shape[0]):
        hidden = hidden_ref[rows, :]
        normed = (hidden * row_scale(hidden, width) * gain_ref[...]).astype(BF)
        normed_ref[rows, :] = normed
        cosine, sine = cos_ref[rows, :], sin_ref[rows, :]
        keys = []
        for part in range(3):
            block = mm(normed, weights_ref[part] if part < 2 else weights_ref[part, :, :384])
            for at in range(5 if part < 2 else 3):
                two = block[:, at * 128 : at * 128 + 128]
                if part < 2:
                    two = two * cosine + turn_pairs(two) * sine
                two = two.astype(BF)
                for side in range(2):
                    head = part * 10 + at * 2 + side
                    if head < QUERY_HEADS:
                        query_ref[head, rows, :] = low_lanes(other_half(two) if side else two)
                    elif head < QUERY_HEADS + KEY_VALUE_HEADS:
                        keys.append(low_lanes(other_half(two) if side else two))
                    elif head < QUERY_HEADS + 2 * KEY_VALUE_HEADS:
                        group = head - QUERY_HEADS - KEY_VALUE_HEADS
                        pair_ref[group, rows, :] = keys[group] + high_lanes(two if side else other_half(two))


def project(hidden, gain, weights, cosine, sine, width, after=()):
    rows = hidden.shape[0]
    return call(
        functools.partial(project_kernel, width),
        (1,),
        [full(rows, WIDE), full(1, WIDE), full(3, WIDE, 640), full(rows, 128), full(rows, 128)],
        [full(rows, WIDE), full(QUERY_HEADS, rows, 128), full(KEY_VALUE_HEADS, rows, 128)],
        [
            jax.ShapeDtypeStruct((rows, WIDE), BF),
            jax.ShapeDtypeStruct((QUERY_HEADS, rows, 128), BF),
            jax.ShapeDtypeStruct((KEY_VALUE_HEADS, rows, 128), BF),
        ],
        [],
        2 * rows * WIDE * 1600,
        WIDE * 1600 * 2 + rows * WIDE * 6 + rows * 128 * 48,
        (hidden, gain, weights, cosine, sine),
        after,
    )


def join_heads(heads):
    columns = [heads[0]]
    for at in range(1, len(heads), 2):
        columns.append(other_half(heads[at]) + heads[at + 1])
    return columns


def out_forward_kernel(width, mixed_ref, weights_ref, hidden_ref, gain_ref, first_ref, last_ref, mid_ref, normed_ref):
    for rows in row_steps(hidden_ref.shape[0]):
        heads = [mixed_ref[head, rows, :] for head in range(QUERY_HEADS)]
        blank = jnp.zeros_like(heads[0])
        first = jnp.concatenate([blank, blank] + join_heads(heads[:5]), axis=1)
        pairs = [other_half(heads[at]) + heads[at + 1] for at in range(5, QUERY_HEADS, 2)]
        last = jnp.concatenate(pairs, axis=1)
        first_ref[rows, :] = first
        last_ref[rows, :] = last
        mid = hidden_ref[rows, :] + mm(first, weights_ref[0], NT) + mm(last, weights_ref[1], NT)
        mid_ref[rows, :] = mid
        normed_ref[rows, :] = (mid * row_scale(mid, width) * gain_ref[...]).astype(BF)


def out_forward(mixed, weights, hidden, gain, width, after=()):
    rows = hidden.shape[0]
    return call(
        functools.partial(out_forward_kernel, width),
        (1,),
        [
            full(QUERY_HEADS, rows, 128),
            pl.BlockSpec((2, WIDE, 640), lambda i: (1, 0, 0)),
            full(rows, WIDE),
            full(1, WIDE),
        ],
        [full(rows, 640), full(rows, 640), full(rows, WIDE), full(rows, WIDE)],
        [
            jax.ShapeDtypeStruct((rows, 640), BF),
            jax.ShapeDtypeStruct((rows, 640), BF),
            jax.ShapeDtypeStruct((rows, WIDE), F32),
            jax.ShapeDtypeStruct((rows, WIDE), BF),
        ],
        [],
        4 * rows * WIDE * 640,
        WIDE * 640 * 4 + rows * WIDE * 10 + rows * 6400,
        (mixed, weights, hidden, gain),
        after,
    )


def norm_back(gradient, hidden, gain, width):
    scaling = row_scale(hidden, width)
    normed = hidden * scaling
    weighted = gradient * gain
    inner = jnp.sum(weighted * normed, axis=-1, keepdims=True) / width
    gain_grad = jnp.sum(gradient * normed, axis=0, keepdims=True)
    return scaling * (weighted - normed * inner), gain_grad


def out_backward_kernel(
    width, back_ref, mid_ref, grad_ref, gain_ref, weights_ref, mid_g, rounded_ref, mixed_g, gain_g
):
    gain_g[...] = jnp.zeros_like(gain_g)
    for rows in row_steps(mid_ref.shape[0]):
        change, gain_part = norm_back(back_ref[rows, :], mid_ref[rows, :], gain_ref[...], width)
        gain_g[...] += gain_part
        change += grad_ref[rows, :]
        mid_g[rows, :] = change
        rounded = change.astype(BF)
        rounded_ref[rows, :] = rounded
        for part in range(2):
            block = mm(rounded, weights_ref[part]).astype(BF)
            for at in range(5):
                for side in range(2):
                    head = part * 10 + at * 2 + side - 5
                    if head >= 0:
                        two = block[:, at * 128 : at * 128 + 128]
                        mixed_g[head, rows, :] = high_lanes(two if side else other_half(two))


def out_backward(back, mid, grad, gain, weights, width, after=()):
    rows = mid.shape[0]
    return call(
        functools.partial(out_backward_kernel, width),
        (1,),
        [
            full(rows, WIDE),
            full(rows, WIDE),
            full(rows, WIDE),
            full(1, WIDE),
            pl.BlockSpec((2, WIDE, 640), lambda i: (1, 0, 0)),
        ],
        [full(rows, WIDE), full(rows, WIDE), full(QUERY_HEADS, rows, 128), full(1, WIDE)],
        [
            jax.ShapeDtypeStruct((rows, WIDE), F32),
            jax.ShapeDtypeStruct((rows, WIDE), BF),
            jax.ShapeDtypeStruct((QUERY_HEADS, rows, 128), BF),
            jax.ShapeDtypeStruct((1, WIDE), F32),
        ],
        [],
        4 * rows * WIDE * 640,
        WIDE * 640 * 4 + rows * WIDE * 18 + rows * 3840,
        (back, mid, grad, gain, weights),
        after,
    )


def outer_products(left, right):
    return [mm(left[:, at : at + 256], right, TN).astype(BF) for at in range(0, WIDE, 256)]


def query_backward_kernel(query_g, normed_ref, rounded_ref, last_ref, first_ref, out_w):
    for rows in row_steps(normed_ref.shape[0]):
        first_ref[rows, :] = jnp.concatenate(
            [query_g[at, rows, :] + other_half(query_g[at + 1, rows, :]) for at in range(0, 10, 2)], axis=1
        )
    for slot, left, right in ((0, normed_ref, first_ref), (1, rounded_ref, last_ref)):
        for at in range(0, WIDE, 256):
            out_w[slot, pl.ds(at, 256), :] = mm(left[:, pl.ds(at, 256)], right[...], TN).astype(BF)


def query_backward(query_g, normed, rounded, last, after=()):
    rows = normed.shape[0]
    return call(
        query_backward_kernel,
        (1,),
        [full(10, rows, 128), full(rows, WIDE), full(rows, WIDE), full(rows, 640)],
        [full(rows, 640), full(2, WIDE, 640)],
        [jax.ShapeDtypeStruct((rows, 640), BF), jax.ShapeDtypeStruct((2, WIDE, 640), BF)],
        [],
        4 * rows * WIDE * 640,
        WIDE * 640 * 4 + rows * WIDE * 4 + rows * 5120,
        (query_g, normed, rounded, last),
        after,
    )


def key_backward_kernel(
    width,
    shares,
    *refs,
):
    pairs = refs[:shares]
    query_g, first_ref, mixed_ref, normed_ref, rounded_ref, weights_ref, hidden_ref, mid_g, gain_ref = refs[shares : shares + 9]
    cos_ref, sin_ref, grad_ref, out_w, gain_g, second, third = refs[shares + 9 :]
    gain_g[...] = jnp.zeros_like(gain_g)
    for rows in row_steps(hidden_ref.shape[0]):
        keys, values = [], []
        for group in range(KEY_VALUE_HEADS):
            pair = pairs[0][group, rows, :]
            for other in pairs[1:]:
                pair = pair + other[group, rows, :].astype(F32)
            moved = pair * sin_ref[rows, :]
            lane = lax.broadcasted_iota(jnp.int32, pair.shape, 1)
            turned = jnp.where(lane < HEAD_DIM // 2, pltpu.roll(moved, 96, 1), -pltpu.roll(moved, 32, 1))
            key = pair * cos_ref[rows, :] + turned
            keys.append(low_lanes(key).astype(BF))
            values.append(high_lanes(pair).astype(BF))
        heads = [query_g[at, rows, :] for at in range(5)] + keys
        second_part = jnp.concatenate(
            [heads[at] + other_half(heads[at + 1]) for at in range(0, 10, 2)], axis=1
        )
        blank = jnp.zeros_like(values[0])
        third_part = jnp.concatenate(
            [
                other_half(values[0]) + values[1],
                other_half(values[2]) + values[3],
                other_half(values[4]),
                blank,
                blank,
            ],
            axis=1,
        )
        second[rows, :] = second_part
        third[rows, :] = third_part
        back = (
            mm(first_ref[rows, :], weights_ref[0], NT)
            + mm(second_part, weights_ref[1], NT)
            + mm(third_part, weights_ref[2], NT)
        )
        change, gain_part = norm_back(back, hidden_ref[rows, :], gain_ref[...], width)
        gain_g[...] += gain_part
        grad_ref[rows, :] = mid_g[rows, :] + change
    for at in range(0, WIDE, 256):
        part = pl.ds(at, 256)
        out_w[0, part, :] = mm(normed_ref[:, part], second[...], TN).astype(BF)
        out_w[1, part, :] = (
            mm(normed_ref[:, part], third[...], TN) + mm(rounded_ref[:, part], mixed_ref[...], TN)
        ).astype(BF)


def key_backward(
    pair_g, arrived, query_g, first, mixed, normed, rounded, weights, hidden, mid_g, gain, cosine, sine, width, after=()
):
    rows = hidden.shape[0]
    own = pl.BlockSpec((KEY_VALUE_HEADS, rows, 128), lambda i: (0, 0, 0))
    return call(
        functools.partial(key_backward_kernel, width, 1 + len(arrived)),
        (1,),
        [own] * (1 + len(arrived))
        + [
            pl.BlockSpec((5, rows, 128), lambda i: (2, 0, 0)),
            full(rows, 640),
            full(rows, 640),
            full(rows, WIDE),
            full(rows, WIDE),
            full(3, WIDE, 640),
            full(rows, WIDE),
            full(rows, WIDE),
            full(1, WIDE),
            full(rows, 128),
            full(rows, 128),
        ],
        [full(rows, WIDE), full(2, WIDE, 640), full(1, WIDE)],
        [
            jax.ShapeDtypeStruct((rows, WIDE), F32),
            jax.ShapeDtypeStruct((2, WIDE, 640), BF),
            jax.ShapeDtypeStruct((1, WIDE), F32),
        ],
        [pltpu.VMEM((rows, 640), BF)] * 2,
        12 * rows * WIDE * 640,
        WIDE * 640 * 10 + rows * WIDE * 16 + rows * 12800,
        (pair_g, *arrived, query_g, first, mixed, normed, rounded, weights, hidden, mid_g, gain, cosine, sine),
        after,
    )


def attend_kernel(ids_ref, query_ref, pair_ref, out_ref, total_ref, turned, top, norm, mixed):
    span = query_ref.shape[1] // 2
    spans = pair_ref.shape[1] // span
    width = GROUP * span
    for j in range(spans):
        values = pair_ref[0, j * span : (j + 1) * span, :].astype(F32)
        turned[:, j * span : (j + 1) * span] = values.T[HEAD_DIM:, :].astype(BF)
    key_at = lax.broadcasted_iota(jnp.int32, (span, span), 0)
    query_at = lax.broadcasted_iota(jnp.int32, (span, span), 1)
    bias = jnp.where(key_at <= query_at, 0.0, MASKED)
    bias = jnp.concatenate([bias] * GROUP, axis=1)
    for s in range(2):
        query = query_ref[:, s * span : (s + 1) * span, :].reshape(width, 128)

        def scores(j):
            return mm(pair_ref[0, j * span : (j + 1) * span, :], query, NT) * (SCALE * LOG2E)

        first = scores(s) + bias
        peak = jnp.max(first, axis=0, keepdims=True)
        weight = jnp.exp2(first - peak)
        top[...] = peak
        norm[...] = jnp.sum(weight, axis=0, keepdims=True)
        mixed[...] = mm(turned[:, s * span : (s + 1) * span], weight.astype(BF))
        for j in range(spans):
            if j == s:
                continue

            @pl.when(ids_ref[j] < ids_ref[s])
            def _():
                more = scores(j)
                old = top[...]
                peak = jnp.maximum(old, jnp.max(more, axis=0, keepdims=True))
                keep = jnp.exp2(old - peak)
                weight = jnp.exp2(more - peak)
                top[...] = peak
                norm[...] = norm[...] * keep + jnp.sum(weight, axis=0, keepdims=True)
                mixed[...] = mixed[...] * keep + mm(
                    turned[:, j * span : (j + 1) * span], weight.astype(BF)
                )

        total_ref[0, s] = top[...] + jnp.log2(norm[...])
        result = mixed[...] / norm[...]
        result = jnp.concatenate([jnp.zeros_like(result), result], axis=0).T.astype(BF)
        out_ref[:, s * span : (s + 1) * span, :] = result.reshape(GROUP, span, 128)


def attend(ids, query, pairs, after=()):
    rows = query.shape[1]
    keys = pairs.shape[1]
    width = GROUP * rows // 2
    heads = pl.BlockSpec((GROUP, rows, 128), lambda g, ids: (g, 0, 0))
    return call(
        attend_kernel,
        (KEY_VALUE_HEADS,),
        [heads, pl.BlockSpec((1, keys, 128), lambda g, ids: (g, 0, 0))],
        [heads, pl.BlockSpec((1, 2, 1, width), lambda g, ids: (g, 0, 0, 0))],
        [
            jax.ShapeDtypeStruct((QUERY_HEADS, rows, 128), BF),
            jax.ShapeDtypeStruct((KEY_VALUE_HEADS, 2, 1, width), F32),
        ],
        [
            pltpu.VMEM((HEAD_DIM, keys), BF),
            pltpu.VMEM((1, width), F32),
            pltpu.VMEM((1, width), F32),
            pltpu.VMEM((HEAD_DIM, width), F32),
        ],
        8 * QUERY_HEADS * rows * keys * 128,
        QUERY_HEADS * rows * 1024,
        (query, pairs),
        after,
        (ids,),
    )


def attend_back_kernel(
    ids_ref, query_ref, pair_ref, grad_ref, out_ref, total_ref, cos_ref, sin_ref, query_g, pair_g, turned, deltas, mixed
):
    span = query_ref.shape[1] // 2
    spans = pair_ref.shape[1] // span
    width = GROUP * span
    half = HEAD_DIM // 2
    for j in range(spans):
        values = pair_ref[0, j * span : (j + 1) * span, :].astype(F32)
        turned[:, j * span : (j + 1) * span] = values.T[:HEAD_DIM, :].astype(BF)
    pair_g[...] = jnp.zeros_like(pair_g)
    key_at = lax.broadcasted_iota(jnp.int32, (span, span), 0)
    query_at = lax.broadcasted_iota(jnp.int32, (span, span), 1)
    bias = jnp.where(key_at <= query_at, 0.0, MASKED)
    bias = jnp.concatenate([bias] * GROUP, axis=1)
    for s in range(2):
        own = slice(s * span, (s + 1) * span)
        query = query_ref[:, own, :].reshape(width, 128)
        grad = grad_ref[:, own, :].reshape(width, 128)
        product = grad.astype(F32) * out_ref[:, own, :].reshape(width, 128).astype(F32)
        deltas[...] = jnp.sum(product.T, axis=0, keepdims=True)

        def block(j, diagonal):
            at = slice(j * span, (j + 1) * span)
            pair = pair_ref[0, at, :]
            scores = mm(pair, query, NT) * (SCALE * LOG2E) - total_ref[0, s]
            if diagonal:
                scores = scores + bias
            weight = jnp.exp2(scores)
            change = (weight * (mm(pair, grad, NT) - deltas[...])).astype(BF)
            pair_g[0, at, :] += mm(change, query) * SCALE + mm(weight.astype(BF), grad)
            return mm(turned[:, at], change)

        mixed[...] = block(s, True)
        for j in range(spans):
            if j == s:
                continue

            @pl.when(ids_ref[j] < ids_ref[s])
            def _():
                mixed[...] += block(j, False)

        cosine = jnp.concatenate([cos_ref[:, own]] * GROUP, axis=1)
        sine = jnp.concatenate([sin_ref[:, own]] * GROUP, axis=1)
        change = mixed[...] * SCALE
        moved = change * sine
        change = change * cosine + jnp.concatenate([moved[half:], -moved[:half]], axis=0)
        change = jnp.concatenate([change, jnp.zeros_like(change)], axis=0).T.astype(BF)
        query_g[:, own, :] = change.reshape(GROUP, span, 128)


def attend_back(ids, query, pairs, grad, out, total, cosine_t, sine_t, after=()):
    rows = query.shape[1]
    keys = pairs.shape[1]
    width = GROUP * rows // 2
    heads = pl.BlockSpec((GROUP, rows, 128), lambda g, ids: (g, 0, 0))
    both = pl.BlockSpec((1, keys, 128), lambda g, ids: (g, 0, 0))
    return call(
        attend_back_kernel,
        (KEY_VALUE_HEADS,),
        [
            heads,
            both,
            heads,
            heads,
            pl.BlockSpec((1, 2, 1, width), lambda g, ids: (g, 0, 0, 0)),
            full(HEAD_DIM, rows),
            full(HEAD_DIM, rows),
        ],
        [heads, both],
        [
            jax.ShapeDtypeStruct((QUERY_HEADS, rows, 128), BF),
            jax.ShapeDtypeStruct((KEY_VALUE_HEADS, keys, 128), F32),
        ],
        [
            pltpu.VMEM((HEAD_DIM, keys), BF),
            pltpu.VMEM((1, width), F32),
            pltpu.VMEM((HEAD_DIM, width), F32),
        ],
        20 * QUERY_HEADS * rows * keys * 128,
        QUERY_HEADS * rows * 2048,
        (query, pairs, grad, out, total, cosine_t, sine_t),
        after,
        (ids,),
    )


def plain_scores(query, pairs, places, own):
    grouped = query[..., :HEAD_DIM].reshape(KEY_VALUE_HEADS, GROUP, -1, HEAD_DIM)
    scores = jnp.einsum("kgqd,ktd->kgqt", grouped, pairs[..., :HEAD_DIM], preferred_element_type=F32)
    return grouped, jnp.where(places[None, :] <= own[:, None], scores * SCALE, MASKED)


def plain_attend(places, query, pairs, after=()):
    rows = query.shape[1]
    _, scores = plain_scores(query, pairs, places, places[:rows])
    top = jnp.max(scores, axis=-1, keepdims=True)
    weight = jnp.exp(scores - top)
    norm = jnp.sum(weight, axis=-1, keepdims=True)
    mixed = jnp.einsum(
        "kgqt,ktd->kgqd", (weight / norm).astype(BF), pairs[..., HEAD_DIM:], preferred_element_type=F32
    )
    mixed = jnp.pad(mixed.reshape(QUERY_HEADS, rows, HEAD_DIM), ((0, 0), (0, 0), (HEAD_DIM, 0)))
    return mixed.astype(BF), top + jnp.log(norm)


def plain_attend_back(places, query, pairs, grad, out, total, cosine_t, sine_t, after=()):
    rows = query.shape[1]
    half = HEAD_DIM // 2
    grouped, scores = plain_scores(query, pairs, places, places[:rows])
    weight = jnp.exp(scores - total)
    grad = grad[..., HEAD_DIM:].reshape(grouped.shape)
    reach = jnp.einsum("kgqd,ktd->kgqt", grad, pairs[..., HEAD_DIM:], preferred_element_type=F32)
    change = (weight * (reach - jnp.sum(weight * reach, axis=-1, keepdims=True))).astype(BF)
    query_g = SCALE * jnp.einsum("kgqt,ktd->kgqd", change, pairs[..., :HEAD_DIM], preferred_element_type=F32)
    key_g = SCALE * jnp.einsum("kgqt,kgqd->ktd", change, grouped, preferred_element_type=F32)
    value_g = jnp.einsum("kgqt,kgqd->ktd", weight.astype(BF), grad, preferred_element_type=F32)
    moved = query_g * sine_t.T
    query_g = query_g * cosine_t.T + jnp.concatenate([moved[..., half:], -moved[..., :half]], axis=-1)
    query_g = jnp.pad(query_g.reshape(QUERY_HEADS, rows, HEAD_DIM), ((0, 0), (0, 0), (0, HEAD_DIM)))
    return query_g.astype(BF), jnp.concatenate([key_g, value_g], axis=-1)


def local(
    tokens,
    span_ids,
    w_query,
    key_weight,
    value_weight,
    w_out,
    gain_attn,
    gain_mlp,
    w_gate,
    w_up,
    w_down,
    out_grad,
):
    group_count, local_length, model_width = tokens.shape
    assert group_count == 1
    n_ctx = lax.axis_size("ctx")
    n_shard = lax.axis_size("shard")
    blocks = n_ctx * n_shard
    own_rows = model_width // blocks
    rows = WIDE // blocks
    extra = rows - own_rows
    tp_rank = lax.axis_index("tp")
    ctx_rank = lax.axis_index("ctx")
    span = local_length // 2

    ids = jnp.concatenate(
        [lax.dynamic_slice_in_dim(span_ids, 2 * ((ctx_rank - i) % n_ctx), 2) for i in range(n_ctx)]
    )
    places = (ids[:, None] * span + jnp.arange(span, dtype=jnp.int32)[None, :]).reshape(-1)
    own_place = places[:local_length].astype(F32)
    inverse_freq = THETA ** (-jnp.arange(HEAD_DIM // 2, dtype=F32) * 2.0 / HEAD_DIM)
    angles = own_place[:, None] * jnp.tile(inverse_freq, 4)[None, :]
    cosine, sine = jnp.cos(angles), jnp.sin(angles)
    angles_t = jnp.tile(inverse_freq, 2)[:, None] * own_place[None, :]
    cosine_t, sine_t = jnp.cos(angles_t), jnp.sin(angles_t)

    source = jnp.arange(model_width, dtype=jnp.int32)
    target = source // own_rows * rows + source % own_rows
    spread = (target[:, None] == jnp.arange(WIDE, dtype=jnp.int32)[None, :]).astype(BF)

    def attn_share(layer):
        joined = jnp.concatenate(
            [w_query[layer], key_weight[layer], value_weight[layer], w_out[layer].T], axis=1
        )
        share = lax.dynamic_slice_in_dim(joined, tp_rank * 640, 640, 1)
        gains = jnp.concatenate(
            [
                jnp.pad(gain_attn[layer], (0, 128 - own_rows)),
                jnp.pad(gain_mlp[layer], (0, 640 - 128 - own_rows)),
            ]
        )
        gains = jnp.where(tp_rank == 0, gains, jnp.zeros_like(gains))
        return jnp.concatenate([share, gains[None, :], jnp.zeros((extra - 1, 640), BF)], axis=0)

    def mlp_share(layer):
        joined = jnp.concatenate([w_gate[layer], w_up[layer], w_down[layer].T], axis=1)
        return jnp.pad(joined, ((0, extra), (0, 0)))

    def gather(share):
        return lax.all_gather(share, ("tp", "shard", "ctx"), axis=0, tiled=True).reshape(
            4, WIDE, share.shape[1]
        )

    def gains_of(weights):
        lines = weights[0].reshape(blocks, rows, 640)[:, own_rows, :]
        return tuple(
            lines[:, at : at + rows].reshape(WIDE).astype(F32)[None, :] for at in (0, 128)
        )

    use_kernels = span % 128 == 0
    if use_kernels:
        attend_call = functools.partial(attend, ids)
        attend_back_call = functools.partial(attend_back, ids)
    else:
        attend_call = functools.partial(plain_attend, places)
        attend_back_call = functools.partial(plain_attend_back, places)

    mlp_w = [gather(mlp_share(layer)) for layer in range(DECODER_LAYERS)]
    attn_now = Gathering(attn_share(0))
    for _ in range(4):
        attn_now.advance()

    hidden = mm(tokens[0], spread)
    kept = []
    for layer in range(DECODER_LAYERS):
        weights = attn_now.values[0]
        gain_a, gain_m = gains_of(weights)
        if layer + 1 < DECODER_LAYERS:
            attn_now = Gathering(attn_share(layer + 1))
            following = attn_now.advance
        else:
            following = tuple
        attn_in, query, pair = project(hidden, gain_a, weights, cosine, sine, model_width)
        ready = following()
        around = [pair]
        for shift in range(1, n_ctx):
            around.append(
                lax.ppermute(pair, "ctx", [(i, (i + shift) % n_ctx) for i in range(n_ctx)])
            )
        pairs = jnp.concatenate(around, axis=1)
        mixed, total = attend_call(query, pairs, after=ready)
        ready = following()
        first, last, mid, mlp_in = out_forward(mixed, weights, hidden, gain_m, model_width, after=ready)
        ready = following()
        result, gate, up = mlp_forward(mlp_in, mid, mlp_w[layer], after=ready)
        following()
        kept.append(
            (hidden, weights, gain_a, gain_m, attn_in, query, pairs, mixed, total, first, last, mid, mlp_in, gate, up)
        )
        hidden = result
    block_out = mm(hidden.astype(BF), spread, NT).astype(BF)[None]

    core = tp_rank % 2
    grad_run = mm(out_grad[0], spread)
    blank = jnp.zeros_like(grad_run)
    mlp_done, attn_done = [None] * DECODER_LAYERS, [None] * DECODER_LAYERS
    attn_sum = None
    for layer in reversed(range(DECODER_LAYERS)):
        (hidden, weights, gain_a, gain_m, attn_in, query, pairs, mixed, total, first, last, mid, mlp_in, gate, up) = kept[layer]
        attn_step = attn_sum.advance if attn_sum is not None else tuple
        grad_in = grad_run.astype(BF)
        sources = (gate, up, mlp_w[layer])
        mlp_step = tuple
        if layer > 0:
            back, parts = mlp_backward(jnp.arange(4, dtype=jnp.int32), grad_in, mlp_in, blank, *sources)
            summed = lax.psum_scatter(
                parts.reshape(4 * WIDE, -1), ("tp", "shard", "ctx"), scatter_dimension=0, tiled=True
            )
            mlp_done[layer] = summed
            ready = ()
        else:
            pair_at = jnp.array([0, 2], jnp.int32)
            ready = attn_step()
            back, there = mlp_backward(pair_at + 1 - core, grad_in, mlp_in, blank, *sources)
            ready = attn_step()
            back, here = mlp_backward(pair_at + core, grad_in, mlp_in, back, *sources, after=ready[:0])
            mlp_sum = Reduction(there, here, n_shard, n_ctx, rows)
            mlp_step = mlp_sum.advance
            mlp_step()
            ready = ready + mlp_sum.values[1:]
        mid_g, rounded, mixed_g, gain_m_grad = out_backward(
            back, mid, grad_run, gain_m, weights, model_width, after=ready
        )
        ready = attn_step()
        mlp_step()
        query_g, pair_g = attend_back_call(query, pairs, mixed_g, mixed, total, cosine_t, sine_t, after=ready)
        ready = attn_step() + (mlp_sum.values if layer == 0 else ())
        arrived = [
            lax.ppermute(
                pair_g[:, shift * local_length : (shift + 1) * local_length].astype(BF),
                "ctx",
                [(i, (i - shift) % n_ctx) for i in range(n_ctx)],
            )
            for shift in range(1, n_ctx)
        ]
        first_g, early = query_backward(query_g, attn_in, rounded, last, after=ready)
        mlp_step()
        if attn_sum is not None:
            attn_done[layer + 1] = gather_core(gather_pair(attn_sum.values[0]), 1)
        ready = mlp_sum.values if layer == 0 else ()
        grad_run, late, gain_a_grad = key_backward(
            pair_g,
            arrived,
            query_g,
            first_g,
            first,
            attn_in,
            rounded,
            weights,
            hidden,
            mid_g,
            gain_a,
            cosine,
            sine,
            model_width,
            after=ready,
        )
        mlp_step()
        lines = jnp.concatenate(
            [
                jnp.pad(gain_a_grad.reshape(blocks, rows), ((0, 0), (0, 128 - rows))),
                jnp.pad(gain_m_grad.reshape(blocks, rows), ((0, 0), (0, 640 - 128 - rows))),
            ],
            axis=1,
        ).astype(BF)
        at = lax.broadcasted_iota(jnp.int32, (1, rows, 1), 1)
        second_w = jnp.where(at == own_rows, lines[:, None, :], late[0].reshape(blocks, rows, 640))
        second_w = second_w.reshape(WIDE, 640)
        there = jnp.stack([jnp.where(core == 0, second_w, early[0]), jnp.where(core == 0, early[1], late[1])])
        here = jnp.stack([jnp.where(core == 0, early[0], second_w), jnp.where(core == 0, late[1], early[1])])
        attn_sum = Reduction(there, here, n_shard, n_ctx, rows)
    for _ in range(4):
        attn_sum.advance()
    attn_done[0] = gather_core(gather_pair(attn_sum.values[0]), 1)
    mlp_done[0] = mlp_sum.values[0]

    grad_high = grad_run.astype(BF)
    grad_low = (grad_run - grad_high.astype(F32)).astype(BF)
    tokens_grad = (mm(grad_high, spread, NT) + mm(grad_low, spread, NT))[None]

    outs = [[] for _ in range(9)]
    for mlp, attn in zip(mlp_done, attn_done):
        attn = attn.reshape(4, rows, 640)
        line = attn[1, own_rows].astype(F32)
        attn = attn[:, :own_rows].transpose(1, 0, 2).reshape(own_rows, 2560).astype(F32)
        mlp = mlp[:own_rows].astype(F32)
        columns = mlp.shape[1] // 3
        for slot, value in enumerate(
            (
                attn[:, :960],
                attn[:, 960:1280],
                attn[:, 1280:1600],
                attn[:, 1600:].T,
                line[:own_rows],
                line[128 : 128 + own_rows],
                mlp[:, :columns],
                mlp[:, columns : 2 * columns],
                mlp[:, 2 * columns :].T,
            )
        ):
            outs[slot].append(value)
    return (block_out, tokens_grad, *[jnp.stack(parts) for parts in outs])


def solution(mesh):
    return jax.shard_map(
        local,
        mesh=mesh,
        in_specs=(
            P(("shard", "tp"), "ctx", None),
            P(),
            P(None, ("shard", "ctx"), None),
            P(None, ("shard", "ctx"), None),
            P(None, ("shard", "ctx"), None),
            P(None, None, ("shard", "ctx")),
            P(None, ("shard", "ctx")),
            P(None, ("shard", "ctx")),
            P(None, ("shard", "ctx"), "tp"),
            P(None, ("shard", "ctx"), "tp"),
            P(None, "tp", ("shard", "ctx")),
            P(("shard", "tp"), "ctx", None),
        ),
        out_specs=(
            P(("shard", "tp"), "ctx", None),
            P(("shard", "tp"), "ctx", None),
            P(None, ("shard", "ctx"), None),
            P(None, ("shard", "ctx"), None),
            P(None, ("shard", "ctx"), None),
            P(None, None, ("shard", "ctx")),
            P(None, ("shard", "ctx")),
            P(None, ("shard", "ctx")),
            P(None, ("shard", "ctx"), "tp"),
            P(None, ("shard", "ctx"), "tp"),
            P(None, "tp", ("shard", "ctx")),
        ),
        check_vma=False,
    )
```

time: 2410 us -> 945 us (0.39)
  waiting for transfers between devices: 1080 us -> 331 us
  matrix products: 566 us -> 17.7 us
  blocking collectives: 425 us -> 0 us
  Pallas kernels: 0 us -> 344 us
  other arithmetic: 226 us -> 66.8 us
  starting transfers between devices: 2.52 us -> 95.4 us
    dot_general x52 -> x5, matrix products: 556 us -> 17.7 us  [mm(): return lax.dot_general(left, right, dims, preferred_element_type=F32)]
    all_gather x16 -> x2, waiting for transfers between devices: 496 us -> 0.01 us  [gather(): lax.all_gather(share, ('tp', 'shard', 'ctx'), axis=0, tiled=True)]
    unnamed x41 -> x3, waiting for transfers between devices: 397 us -> 0.05 us
    pallas_call x0 -> x19, Pallas kernels: none -> 344 us  [call(): pl.pallas_call(body, grid_spec=pltpu.PrefetchScalarGridSpec(num_scalar_pr...]
    ppermute x0 -> x48, waiting for transfers between devices: none -> 331 us  [the longest x10 103 us: gather_line(): lax.ppermute(array, name, [(i, (i + shift) % count) for i in range(count)])]
    unnamed x2 -> x0, blocking collectives: 275 us -> none
    reduce_scatter x8 -> x1, waiting for transfers between devices: 149 us -> 0.01 us  [local(): lax.psum_scatter(parts.reshape(4 * WIDE, -1), ('tp', 'shard', 'ctx'), sca...]
    all_gather x4 -> x0, blocking collectives: 145 us -> none  [the longest x2 73 us: local(): lax.all_gather(key_weight[layer_idx], ('shard', 'ctx'), axis=0, tiled=True)]
  transfers between devices with their start and end apart: 33 -> 51, of which waited for: 26 -> 26; matrix products, arithmetic and copies ran while one was open for 25% -> 12% of each run, Pallas kernels for 0% -> 21%
where the time goes in v1:
time: 945 us; the launch traced here: 938 us
  Pallas kernels  344 us (36%)
  waiting for transfers between devices  331 us (35%)
  starting transfers between devices  95.4 us (10%)
  local copies, waits for them, and re-layouts  68.3 us (7%)
  other arithmetic  66.8 us (7%)
  matrix products  17.7 us (2%)
  between operations  15.5 us (2%)
    pallas_call x19, Pallas kernels, call(): pl.pallas_call(body, grid_spec=pltpu.PrefetchScalarGridSpec(num_scalar_pr...  344 us
    ppermute x10, waiting for transfers between devices, gather_line(): lax.ppermute(array, name, [(i, (i + shift) % count) for i in range(count)])  103 us
    ppermute x6, waiting for transfers between devices, pair_reduce(): lax.ppermute(pick(array, 1 - pair, axis), 'tp', PAIR_SWAP)  93.5 us
    ppermute x15, waiting for transfers between devices, line_reduce(): lax.ppermute(sent, name, [(i, (i + shift) % count) for i in range(count)])  75.4 us
    ppermute x2, waiting for transfers between devices, local(): lax.ppermute(pair, 'ctx', [(i, (i + shift) % n_ctx) for i in range(n_ctx)])  37.2 us
    ppermute x2, starting transfers between devices, local(): lax.ppermute(pair_g[:, shift * local_length:(shift + 1) * local_length].a...  37.1 us
    ppermute x15, starting transfers between devices, line_reduce(): lax.ppermute(sent, name, [(i, (i + shift) % count) for i in range(count)])  22.1 us
    unnamed x137, local copies, waits for them, and re-layouts  20.1 us
  transfers between devices with their start and end apart: 51, of which 26 were waited for; matrix products, arithmetic and copies ran while one was open for 12% of the time, Pallas kernels for 21%

profile of v1, /device:TPU:0, one launch (start us, length us, event | category | flops | bytes accessed | tf_op | source)
XLA Modules:
  0.0 938.2 jit_solution(8405406909613528484)
XLA Ops:
  33.9 16.4 %collective-permute-done.1 = bf16[128,640]{1,0:T(8,128)(2,1)S(1)} collective-permute-done((bf16[128,640]{1,0:T(8,128)(2,1)S(1)}, bf16[128,640]{1,0:T(8,128)(2,1)S(1)}, u32[]{:S(2)}, u32[]{:S(2)}) %collective-permute-start.1) | collective-permute-done | bytes 163872 | tf_op jit(solution)/shard_map/ppermute | solution.py:103
  62.6 19.1 %collective-permute-done.10 = bf16[128,640]{1,0:T(8,128)(2,1)S(1)} collective-permute-done((bf16[128,640]{1,0:T(8,128)(2,1)}, bf16[128,640]{1,0:T(8,128)(2,1)S(1)}, u32[]{:S(2)}, u32[]{:S(2)}) %collective-permute-start.10) | collective-permute-done | bytes 163872 | tf_op jit(solution)/shard_map/ppermute | solution.py:103
  97.6 32.8 %collective-permute-done.12 = bf16[4,64,640]{2,1,0:T(8,128)(2,1)S(1)} collective-permute-done((bf16[4,64,640]{2,1,0:T(8,128)(2,1)S(1)}, bf16[4,64,640]{2,1,0:T(8,128)(2,1)S(1)}, u32[]{:S(2)}, u32[]{:S(2)}) %collective-permute-start.12) | collective-permute-done | bytes 327712 | tf_op jit(solution)/shard_map/ppermute | solution.py:103
  134.6 12.8 %collective-permute-done.15 = bf16[2,4,64,640]{3,2,1,0:T(8,128)(2,1)S(1)} collective-permute-done((bf16[2,4,64,640]{3,2,1,0:T(8,128)(2,1)S(1)}, bf16[2,4,64,640]{3,2,1,0:T(8,128)(2,1)S(1)}, u32[]{:S(2)}, u32[]{:S(2)}) %collective-permute-start.15) | collective-permute-done | bytes 655392 | tf_op jit(solution)/shard_map/ppermute | solution.py:103
  172.6 8.9 shard_map.212
  190.5 21.0 %collective-permute-done.8 = bf16[5,768,128]{2,1,0:T(8,128)(2,1)S(1)} collective-permute-done((bf16[5,768,128]{2,1,0:T(8,128)(2,1)}, bf16[5,768,128]{2,1,0:T(8,128)(2,1)S(1)}, u32[]{:S(2)}, u32[]{:S(2)}) %collective-permute-start.8) | collective-permute-done | bytes 983072 | tf_op jit(solution)/shard_map/ppermute | solution.py:867
  212.9 21.6 %shard_map.213 = (bf16[15,768,128]{2,1,0:T(8,128)(2,1)}, f32[5,2,1,1152]{3,2,1,0:T(1,128)}) custom-call(s32[4]{0:T(128)} %get-tuple-element.149.refs_0_, bf16[15,768,128]{2,1,0:T(8,128)(2,1)} %get-tuple-element.63.refs_1_, bf16[5,1536,128]{2,1,0:T(8,128)(2,1)} %copy-done.44, bf16[4,64,640]{2,1,0:T(8,128)(2,1)} %copy-done.48, bf16[4,64,640]{2,1,0:T(8,128)(2,1)} %copy-done.49), custom_call_target="tpu_custom_call" | custom-call | flops 18119393280 | bytes 11796480 | tf_op jit(solution)/shard_map/pallas_call | solution.py:139
  234.5 9.2 shard_map.214
  243.6 22.0 %shard_map.215 = (f32[768,1024]{1,0:T(8,128)}, f32[4,768,640]{2,1,0:T(8,128)}, f32[4,768,640]{2,1,0:T(8,128)}) custom-call(bf16[768,1024]{1,0:T(8,128)(2,1)} %get-tuple-element.66.refs_0_.refs_2_, f32[768,1024]{1,0:T(8,128)} %get-tuple-element.67.refs_1_, bf16[4,1024,1920]{2,1,0:T(8,128)(2,1)} %bitcast.323, bf16[4,1024,1920]{2,1,0:T(8,128)(2,1)} %bitcast.324, ...), custom_call_target="tpu_custom_call" | custom-call | flops 12079595520 | bytes 39321600 | tf_op jit(solution)/shard_map/pallas_call | solution.py:139
  265.6 8.9 shard_map.216
  274.5 10.1 %collective-permute-start.17 = (bf16[5,768,128]{2,1,0:T(8,128)(2,1)}, bf16[5,768,128]{2,1,0:T(8,128)(2,1)S(1)}, u32[]{:S(2)}, u32[]{:S(2)}) collective-permute-start(bf16[5,768,128]{2,1,0:T(8,128)(2,1)} %get-tuple-element.70), channel_id=1, source_target_pairs={{0,4},{4,0},{1,5},{5,1},{2,6},{6,2},{3,7},{7,3},{8,12},{12,8},{9,1... | collective-permute-start | bytes 2949128 | tf_op jit(solution)/shard_map/ppermute | solution.py:867
  290.5 16.2 %collective-permute-done.17 = bf16[5,768,128]{2,1,0:T(8,128)(2,1)S(1)} collective-permute-done((bf16[5,768,128]{2,1,0:T(8,128)(2,1)}, bf16[5,768,128]{2,1,0:T(8,128)(2,1)S(1)}, u32[]{:S(2)}, u32[]{:S(2)}) %collective-permute-start.17) | collective-permute-done | bytes 983072 | tf_op jit(solution)/shard_map/ppermute | solution.py:867
  308.1 21.7 %shard_map.217 = (bf16[15,768,128]{2,1,0:T(8,128)(2,1)}, f32[5,2,1,1152]{3,2,1,0:T(1,128)}) custom-call(s32[4]{0:T(128)} %get-tuple-element.149.refs_0_, bf16[15,768,128]{2,1,0:T(8,128)(2,1)} %get-tuple-element.69.refs_1_, bf16[5,1536,128]{2,1,0:T(8,128)(2,1)} %copy-done.45), custom_call_target="tpu_custom_call" | custom-call | flops 18119393280 | bytes 11796480 | tf_op jit(solution)/shard_map/pallas_call | solution.py:139
  329.8 8.8 shard_map.218
  338.6 22.5 %shard_map.219 = (f32[768,1024]{1,0:T(8,128)}, f32[4,768,640]{2,1,0:T(8,128)}, f32[4,768,640]{2,1,0:T(8,128)}) custom-call(bf16[768,1024]{1,0:T(8,128)(2,1)} %get-tuple-element.72.refs_0_.refs_2_, f32[768,1024]{1,0:T(8,128)} %get-tuple-element.73.refs_1_, bf16[4,1024,1920]{2,1,0:T(8,128)(2,1)} %bitcast.332, bf16[4,1024,1920]{2,1,0:T(8,128)(2,1)} %bitcast.333, ...), custom_call_target="tpu_custom_call" | custom-call | flops 12079595520 | bytes 39321600 | tf_op jit(solution)/shard_map/pallas_call | solution.py:139
  363.7 40.5 %shard_map.220 = (f32[768,1024]{1,0:T(8,128)}, bf16[4,1024,1920]{2,1,0:T(8,128)(2,1)}) custom-call(s32[4]{0:T(128)} %iota.44.refs_0_, bf16[768,1024]{1,0:T(8,128)(2,1)} %get-tuple-element.278.refs_1_, bf16[768,1024]{1,0:T(8,128)(2,1)} %get-tuple-element.72.refs_0_.refs_2_, f32[768,1024]{1,0:T(8,128)} %broadcast_in_dim.62.refs_3_, ...), custom_call_target="tpu_custom_call" | custom-call | flops 24159191040 | bytes 56623104 | tf_op jit(solution)/shard_map/pallas_call | solution.py:139
  404.1 10.2 %shard_map.221 = (f32[768,1024]{1,0:T(8,128)}, bf16[768,1024]{1,0:T(8,128)(2,1)}, bf16[15,768,128]{2,1,0:T(8,128)(2,1)}, f32[1,1024]{1,0:T(1,128)}) custom-call(f32[768,1024]{1,0:T(8,128)} %get-tuple-element.77.refs_0_, f32[768,1024]{1,0:T(8,128)} %get-tuple-element.73.refs_1_, f32[768,1024]{1,0:T(8,128)} %get-tuple-element.279.refs_2_, ...), custom_call_target="tpu_custom_call" | custom-call | flops 2013265920 | bytes 19726336 | tf_op jit(solution)/shard_map/pallas_call | solution.py:139
  414.3 30.8 %shard_map.222 = (bf16[15,768,128]{2,1,0:T(8,128)(2,1)}, f32[5,1536,128]{2,1,0:T(8,128)}) custom-call(s32[4]{0:T(128)} %get-tuple-element.149.refs_0_, bf16[15,768,128]{2,1,0:T(8,128)(2,1)} %get-tuple-element.69.refs_1_, bf16[5,1536,128]{2,1,0:T(8,128)(2,1)} %copy-done.45, bf16[15,768,128]{2,1,0:T(8,128)(2,1)} %get-tuple-element.78.refs_3_, ...), custom_call_target="tpu_custom_call" | custom-call | flops 45298483200 | bytes 23592960 | tf_op jit(solution)/shard_map/pallas_call | solution.py:139
  446.7 24.0 %collective-permute-start.18 = (bf16[5,768,128]{2,1,0:T(8,128)(2,1)S(1)}, bf16[5,768,128]{2,1,0:T(8,128)(2,1)S(1)}, u32[]{:S(2)}, u32[]{:S(2)}) collective-permute-start(bf16[5,768,128]{2,1,0:T(8,128)(2,1)S(1)} %slice.469), channel_id=1, source_target_pairs={{0,4},{4,0},{1,5},{5,1},{2,6},{6,2},{3,7},{7,3},{8,12},{12,8},{9,1... | collective-permute-start | bytes 2949128 | tf_op jit(solution)/shard_map/ppermute | solution.py:918
  478.4 13.4 %collective-permute-done.18.refs_1_ = bf16[5,768,128]{2,1,0:T(8,128)(2,1)S(1)} collective-permute-done((bf16[5,768,128]{2,1,0:T(8,128)(2,1)S(1)}, bf16[5,768,128]{2,1,0:T(8,128)(2,1)S(1)}, u32[]{:S(2)}, u32[]{:S(2)}) %collective-permute-start.18) | collective-permute-done | bytes 983072 | tf_op jit(solution)/shard_map/ppermute | solution.py:918
  492.8 16.9 %shard_map.224 = (f32[768,1024]{1,0:T(8,128)}, bf16[2,1024,640]{2,1,0:T(8,128)(2,1)}, f32[1,1024]{1,0:T(1,128)}) custom-call(f32[5,1536,128]{2,1,0:T(8,128)} %get-tuple-element.80.refs_0_, bf16[5,768,128]{2,1,0:T(8,128)(2,1)} %copy-done.42, bf16[15,768,128]{2,1,0:T(8,128)(2,1)} %get-tuple-element.81.refs_0_.refs_2_, ...), custom_call_target="tpu_custom_call" | custom-call | flops 6039797760 | bytes 28966912 | tf_op jit(solution)/shard_map/pallas_call | solution.py:139
  512.9 24.8 %shard_map.225 = (f32[768,1024]{1,0:T(8,128)}, bf16[2,1024,1920]{2,1,0:T(8,128)(2,1)}) custom-call(s32[2]{0:T(128)} %get-tuple-element.284.refs_0_, bf16[768,1024]{1,0:T(8,128)(2,1)} %convert_element_type.283.refs_1_, bf16[768,1024]{1,0:T(8,128)(2,1)} %get-tuple-element.66.refs_0_.refs_2_, f32[768,1024]{1,0:T(8,128)} %broadcast_in_dim.62.refs_3_, ...), custom_call_target="tpu_custom_call" | custom-call | flops 12079595520 | bytes 33030144 | tf_op jit(solution)/shard_map/pallas_call | solution.py:139
  550.8 24.7 %shard_map.226 = (f32[768,1024]{1,0:T(8,128)}, bf16[2,1024,1920]{2,1,0:T(8,128)(2,1)}) custom-call(s32[2]{0:T(128)} %get-tuple-element.285.refs_0_, bf16[768,1024]{1,0:T(8,128)(2,1)} %convert_element_type.283.refs_1_, bf16[768,1024]{1,0:T(8,128)(2,1)} %get-tuple-element.66.refs_0_.refs_2_, f32[768,1024]{1,0:T(8,128)} %get-tuple-element.91.refs_3_, ...), custom_call_target="tpu_custom_call" | custom-call | flops 12079595520 | bytes 33030144 | tf_op jit(solution)/shard_map/pallas_call | solution.py:139
  583.0 11.8 %collective-permute-done.20 = bf16[2,2,128,640]{3,2,0,1:T(8,128)(2,1)S(1)} collective-permute-done((bf16[2,2,128,640]{3,2,0,1:T(8,128)(2,1)S(1)}, bf16[2,2,128,640]{3,2,0,1:T(8,128)(2,1)S(1)}, u32[]{:S(2)}, u32[]{:S(2)}) %collective-permute-start.20) | collective-permute-done | bytes 655392 | tf_op jit(solution)/shard_map/ppermute | solution.py:57
  617.8 66.2 %collective-permute-done.24 = bf16[2,128,640]{2,1,0:T(8,128)(2,1)S(1)} collective-permute-done((bf16[2,128,640]{2,1,0:T(8,128)(2,1)S(1)}, bf16[2,128,640]{2,1,0:T(8,128)(2,1)S(1)}, u32[]{:S(2)}, u32[]{:S(2)}) %collective-permute-start.24) | collective-permute-done | bytes 327712 | tf_op jit(solution)/shard_map/ppermute | solution.py:57
  694.6 19.5 %collective-permute-done.27 = bf16[128,640]{1,0:T(8,128)(2,1)S(1)} collective-permute-done((bf16[128,640]{1,0:T(8,128)(2,1)S(1)}, bf16[128,640]{1,0:T(8,128)(2,1)S(1)}, u32[]{:S(2)}, u32[]{:S(2)}) %collective-permute-start.27) | collective-permute-done | bytes 163872 | tf_op jit(solution)/shard_map/ppermute | solution.py:49
  722.4 10.3 %shard_map.227 = (f32[768,1024]{1,0:T(8,128)}, bf16[768,1024]{1,0:T(8,128)(2,1)}, bf16[15,768,128]{2,1,0:T(8,128)(2,1)}, f32[1,1024]{1,0:T(1,128)}) custom-call(f32[768,1024]{1,0:T(8,128)} %get-tuple-element.92.refs_0_, f32[768,1024]{1,0:T(8,128)} %get-tuple-element.67.refs_1_, f32[768,1024]{1,0:T(8,128)} %get-tuple-element.88.refs_2_, f32[1,1024]{1,0:T(1,128)} %bitcast.389, ...), custom_call_target="tpu_custom_call" | custom-call | flops 2013265920 | bytes 19726336 | tf_op jit(solution)/shard_map/pallas_call | solution.py:139
  742.3 30.9 %shard_map.228 = (bf16[15,768,128]{2,1,0:T(8,128)(2,1)}, f32[5,1536,128]{2,1,0:T(8,128)}) custom-call(s32[4]{0:T(128)} %get-tuple-element.149.refs_0_, bf16[15,768,128]{2,1,0:T(8,128)(2,1)} %get-tuple-element.63.refs_1_, bf16[5,1536,128]{2,1,0:T(8,128)(2,1)} %copy-done.44, bf16[15,768,128]{2,1,0:T(8,128)(2,1)} %get-tuple-element.98.refs_3_, ...), custom_call_target="tpu_custom_call" | custom-call | flops 45298483200 | bytes 23592960 | tf_op jit(solution)/shard_map/pallas_call | solution.py:139
  775.8 13.1 %collective-permute-start.25 = (bf16[5,768,128]{2,1,0:T(8,128)(2,1)}, bf16[5,768,128]{2,1,0:T(8,128)(2,1)S(1)}, u32[]{:S(2)}, u32[]{:S(2)}) collective-permute-start(bf16[5,768,128]{2,1,0:T(8,128)(2,1)} %slice.468), channel_id=1, source_target_pairs={{0,4},{4,0},{1,5},{5,1},{2,6},{6,2},{3,7},{7,3},{8,12},{12,8},{9,1... | collective-permute-start | bytes 2949128 | tf_op jit(solution)/shard_map/ppermute | solution.py:918
  803.4 17.0 %shard_map.230 = (f32[768,1024]{1,0:T(8,128)}, bf16[2,1024,640]{2,1,0:T(8,128)(2,1)}, f32[1,1024]{1,0:T(1,128)}) custom-call(f32[5,1536,128]{2,1,0:T(8,128)} %get-tuple-element.100.refs_0_, bf16[5,768,128]{2,1,0:T(8,128)(2,1)} %copy-done.39, bf16[15,768,128]{2,1,0:T(8,128)(2,1)} %get-tuple-element.101.refs_0_.refs_2_, ...), custom_call_target="tpu_custom_call" | custom-call | flops 6039797760 | bytes 28966912 | tf_op jit(solution)/shard_map/pallas_call | solution.py:139
  837.4 14.7 %collective-permute-done.34 = bf16[2,2,128,640]{3,2,0,1:T(8,128)(2,1)S(1)} collective-permute-done((bf16[2,2,128,640]{3,2,0,1:T(8,128)(2,1)S(1)}, bf16[2,2,128,640]{3,2,0,1:T(8,128)(2,1)S(1)}, u32[]{:S(2)}, u32[]{:S(2)}) %collective-permute-start.34) | collective-permute-done | bytes 655392 | tf_op jit(solution)/shard_map/ppermute | solution.py:57
  885.1 33.5 %collective-permute-done.46 = bf16[128,1920]{1,0:T(8,128)(2,1)S(1)} collective-permute-done((bf16[128,1920]{1,0:T(8,128)(2,1)S(1)}, bf16[128,1920]{1,0:T(8,128)(2,1)S(1)}, u32[]{:S(2)}, u32[]{:S(2)}) %collective-permute-start.46) | collective-permute-done | bytes 491552 | tf_op jit(solution)/shard_map/ppermute | solution.py:49
  (402 shorter events, 268.7 us)
Async XLA Ops:
  7.2 236.4 %all-gather.3.cloned.1.call-start = ((), (), s32[]{:S(2)}) async-start(), calls=%async_computation.1 | async-start | bytes 16220160 | tf_op jit(solution)/shard_map/all_gather | solution.py:829
  10.5 328.1 %all-gather.5.cloned.1.call-start = ((), (), s32[]{:S(2)}) async-start(), calls=%async_computation.2 | async-start | bytes 16220160 | tf_op jit(solution)/shard_map/all_gather | solution.py:829
  11.4 916.0 %reduce-scatter.2.cloned.1.call-start = ((), (), s32[]{:S(2)}) async-start(), calls=%async_computation.3 | async-start | bytes 16220160 | tf_op jit(solution)/shard_map/reduce_scatter | solution.py:895
  25.8 24.4 %collective-permute-start.1 = (bf16[128,640]{1,0:T(8,128)(2,1)S(1)}, bf16[128,640]{1,0:T(8,128)(2,1)S(1)}, u32[]{:S(2)}, u32[]{:S(2)}) collective-permute-start(bf16[128,640]{1,0:T(8,128)(2,1)S(1)} %get-tuple-element.270), channel_id=1, source_target_pairs={{0,16},{8,24},{16,0},{24,8},{1,17},{9,25},{17,1},{25,9},{2,18},{10... | collective-permute-start | bytes 491528 | tf_op jit(solution)/shard_map/ppermute | solution.py:103
  25.8 24.4 %collective-permute-start = (bf16[128,640]{1,0:T(8,128)(2,1)S(1)}, bf16[128,640]{1,0:T(8,128)(2,1)S(1)}, u32[]{:S(2)}, u32[]{:S(2)}) collective-permute-start(bf16[128,640]{1,0:T(8,128)(2,1)S(1)} %get-tuple-element.270), channel_id=1, source_target_pairs={{0,8},{8,16},{16,24},{24,0},{1,9},{9,17},{17,25},{25,1},{2,10},{10... | collective-permute-start | bytes 491528 | tf_op jit(solution)/shard_map/ppermute | solution.py:103
  50.6 31.3 %collective-permute-start.5 = (bf16[4,64,640]{2,1,0:T(8,128)(2,1)S(1)}, bf16[4,64,640]{2,1,0:T(8,128)(2,1)S(1)}, u32[]{:S(2)}, u32[]{:S(2)}) collective-permute-start(bf16[4,64,640]{2,1,0:T(8,128)(2,1)S(1)} %slice.322), channel_id=1, source_target_pairs={{0,2},{2,0},{1,3},{3,1},{4,6},{6,4},{5,7},{7,5},{8,10},{10,8},{9,1... | collective-permute-start | bytes 983048 | tf_op jit(solution)/shard_map/ppermute | solution.py:87
  52.2 29.6 %collective-permute-start.10 = (bf16[128,640]{1,0:T(8,128)(2,1)}, bf16[128,640]{1,0:T(8,128)(2,1)S(1)}, u32[]{:S(2)}, u32[]{:S(2)}) collective-permute-start(bf16[128,640]{1,0:T(8,128)(2,1)} %get-tuple-element.255), channel_id=1, source_target_pairs={{0,16},{8,24},{16,0},{24,8},{1,17},{9,25},{17,1},{25,9},{2,18},{10... | collective-permute-start | bytes 491528 | tf_op jit(solution)/shard_map/ppermute | solution.py:103
  53.9 27.8 %collective-permute-start.9 = (bf16[128,640]{1,0:T(8,128)(2,1)}, bf16[128,640]{1,0:T(8,128)(2,1)S(1)}, u32[]{:S(2)}, u32[]{:S(2)}) collective-permute-start(bf16[128,640]{1,0:T(8,128)(2,1)} %get-tuple-element.255), channel_id=1, source_target_pairs={{0,8},{8,16},{16,24},{24,0},{1,9},{9,17},{17,25},{25,1},{2,10},{10... | collective-permute-start | bytes 491528 | tf_op jit(solution)/shard_map/ppermute | solution.py:103
  83.9 46.8 %collective-permute-start.6 = (bf16[2,4,64,640]{3,2,1,0:T(8,128)(2,1)S(1)}, bf16[2,4,64,640]{3,2,1,0:T(8,128)(2,1)S(1)}, u32[]{:S(2)}, u32[]{:S(2)}) collective-permute-start(bf16[2,4,64,640]{3,2,1,0:T(8,128)(2,1)S(1)} %get-tuple-element.230), channel_id=1, source_target_pairs={{0,4},{4,0},{1,5},{5,1},{2,6},{6,2},{3,7},{7,3},{8,12},{12,8},{9,1... | collective-permute-start | bytes 1966088 | tf_op jit(solution)/shard_map/ppermute | solution.py:103
  93.0 38.3 %collective-permute-start.4 = (bf16[4,2,64,640]{3,2,1,0:T(8,128)(2,1)S(1)}, bf16[4,2,64,640]{3,2,1,0:T(8,128)(2,1)S(1)}, u32[]{:S(2)}, u32[]{:S(2)}) collective-permute-start(bf16[4,2,64,640]{3,2,1,0:T(8,128)(2,1)S(1)} %pad_maximum_fusion.12), channel_id=1, source_target_pairs={{0,2},{2,0},{1,3},{3,1},{4,6},{6,4},{5,7},{7,5},{8,10},{10,8},{9,1... | collective-permute-start | bytes 1966088 | tf_op jit(solution)/shard_map/ppermute | solution.py:87
  94.6 35.8 %collective-permute-start.12 = (bf16[4,64,640]{2,1,0:T(8,128)(2,1)S(1)}, bf16[4,64,640]{2,1,0:T(8,128)(2,1)S(1)}, u32[]{:S(2)}, u32[]{:S(2)}) collective-permute-start(bf16[4,64,640]{2,1,0:T(8,128)(2,1)S(1)} %get-tuple-element.219.refs_3_), channel_id=1, source_target_pairs={{0,4},{4,0},{1,5},{5,1},{2,6},{6,2},{3,7},{7,3},{8,12},{12,8},{9,1... | collective-permute-start | bytes 983048 | tf_op jit(solution)/shard_map/ppermute | solution.py:103
  96.1 51.3 %collective-permute-start.15 = (bf16[2,4,64,640]{3,2,1,0:T(8,128)(2,1)S(1)}, bf16[2,4,64,640]{3,2,1,0:T(8,128)(2,1)S(1)}, u32[]{:S(2)}, u32[]{:S(2)}) collective-permute-start(bf16[2,4,64,640]{3,2,1,0:T(8,128)(2,1)S(1)} %get-tuple-element.217.refs_5_), channel_id=1, source_target_pairs={{0,4},{4,0},{1,5},{5,1},{2,6},{6,2},{3,7},{7,3},{8,12},{12,8},{9,1... | collective-permute-start | bytes 1966088 | tf_op jit(solution)/shard_map/ppermute | solution.py:103
  133.7 31.4 %collective-permute-start.7 = (bf16[2,4,2,128,640]{4,3,2,1,0:T(8,128)(2,1)}, bf16[2,4,2,128,640]{4,3,2,1,0:T(8,128)(2,1)}, u32[]{:S(2)}, u32[]{:S(2)}) collective-permute-start(bf16[2,4,2,128,640]{4,3,2,1,0:T(8,128)(2,1)} %maximum_maximum_fusion), channel_id=1, source_target_pairs={{0,1},{1,0},{2,3},{3,2},{4,5},{5,4},{6,7},{7,6},{8,9},{9,8},{10,11... | collective-permute-start | bytes 7864328 | tf_op jit(solution)/shard_map/ppermute | solution.py:93
  154.8 28.6 %collective-permute-start.16 = (bf16[2,4,2,128,640]{4,3,2,1,0:T(8,128)(2,1)}, bf16[2,4,2,128,640]{4,3,2,1,0:T(8,128)(2,1)}, u32[]{:S(2)}, u32[]{:S(2)}) collective-permute-start(bf16[2,4,2,128,640]{4,3,2,1,0:T(8,128)(2,1)} %maximum_maximum_fusion.1), channel_id=1, source_target_pairs={{0,1},{1,0},{2,3},{3,2},{4,5},{5,4},{6,7},{7,6},{8,9},{9,8},{10,11... | collective-permute-start | bytes 7864328 | tf_op jit(solution)/shard_map/ppermute | solution.py:93
  181.5 30.0 %collective-permute-start.8 = (bf16[5,768,128]{2,1,0:T(8,128)(2,1)}, bf16[5,768,128]{2,1,0:T(8,128)(2,1)S(1)}, u32[]{:S(2)}, u32[]{:S(2)}) collective-permute-start(bf16[5,768,128]{2,1,0:T(8,128)(2,1)} %get-tuple-element.64), channel_id=1, source_target_pairs={{0,4},{4,0},{1,5},{5,1},{2,6},{6,2},{3,7},{7,3},{8,12},{12,8},{9,1... | collective-permute-start | bytes 2949128 | tf_op jit(solution)/shard_map/ppermute | solution.py:867
  274.5 32.2 %collective-permute-start.17 = (bf16[5,768,128]{2,1,0:T(8,128)(2,1)}, bf16[5,768,128]{2,1,0:T(8,128)(2,1)S(1)}, u32[]{:S(2)}, u32[]{:S(2)}) collective-permute-start(bf16[5,768,128]{2,1,0:T(8,128)(2,1)} %get-tuple-element.70), channel_id=1, source_target_pairs={{0,4},{4,0},{1,5},{5,1},{2,6},{6,2},{3,7},{7,3},{8,12},{12,8},{9,1... | collective-permute-start | bytes 2949128 | tf_op jit(solution)/shard_map/ppermute | solution.py:867
  446.7 45.1 %collective-permute-start.18 = (bf16[5,768,128]{2,1,0:T(8,128)(2,1)S(1)}, bf16[5,768,128]{2,1,0:T(8,128)(2,1)S(1)}, u32[]{:S(2)}, u32[]{:S(2)}) collective-permute-start(bf16[5,768,128]{2,1,0:T(8,128)(2,1)S(1)} %slice.469), channel_id=1, source_target_pairs={{0,4},{4,0},{1,5},{5,1},{2,6},{6,2},{3,7},{7,3},{8,12},{12,8},{9,1... | collective-permute-start | bytes 2949128 | tf_op jit(solution)/shard_map/ppermute | solution.py:918
  545.1 49.7 %collective-permute-start.22 = (bf16[2,4,2,128,1920]{4,3,1,0,2:T(8,128)(2,1)}, bf16[2,4,2,128,1920]{4,3,1,0,2:T(8,128)(2,1)}, u32[]{:S(2)}, u32[]{:S(2)}) collective-permute-start(bf16[2,4,2,128,1920]{4,3,1,0,2:T(8,128)(2,1)} %copy.91), channel_id=1, source_target_pairs={{0,1},{1,0},{2,3},{3,2},{4,5},{5,4},{6,7},{7,6},{8,9},{9,8},{10,11... | collective-permute-start | bytes 23592968 | tf_op jit(solution)/shard_map/ppermute | solution.py:70
  548.4 27.2 %collective-permute-start.19 = (bf16[2,4,2,128,640]{4,3,1,0,2:T(8,128)(2,1)}, bf16[2,4,2,128,640]{4,3,1,0,2:T(8,128)(2,1)}, u32[]{:S(2)}, u32[]{:S(2)}) collective-permute-start(bf16[2,4,2,128,640]{4,3,1,0,2:T(8,128)(2,1)} %copy.109), channel_id=1, source_target_pairs={{0,1},{1,0},{2,3},{3,2},{4,5},{5,4},{6,7},{7,6},{8,9},{9,8},{10,11... | collective-permute-start | bytes 7864328 | tf_op jit(solution)/shard_map/ppermute | solution.py:70
  581.2 25.9 %collective-permute-start.21 = (bf16[2,2,128,640]{3,2,1,0:T(8,128)(2,1)S(1)}, bf16[2,2,128,640]{3,2,1,0:T(8,128)(2,1)S(1)}, u32[]{:S(2)}, u32[]{:S(2)}) collective-permute-start(bf16[2,2,128,640]{3,2,1,0:T(8,128)(2,1)S(1)} %dynamic-slice_bitcast_fusion.5), channel_id=1, source_target_pairs={{0,4},{4,0},{1,5},{5,1},{2,6},{6,2},{3,7},{7,3},{8,12},{12,8},{9,1... | collective-permute-start | bytes 1966088 | tf_op jit(solution)/shard_map/ppermute | solution.py:49
  605.0 127.7 %collective-permute-start.29 = (bf16[2,2,128,1920]{3,2,0,1:T(8,128)(2,1)}, bf16[2,2,128,1920]{3,2,0,1:T(8,128)(2,1)}, u32[]{:S(2)}, u32[]{:S(2)}) collective-permute-start(bf16[2,2,128,1920]{3,2,0,1:T(8,128)(2,1)} %dynamic-slice_bitcast_fusion.1), channel_id=1, source_target_pairs={{0,2},{2,0},{1,3},{3,1},{4,6},{6,4},{5,7},{7,5},{8,10},{10,8},{9,1... | collective-permute-start | bytes 5898248 | tf_op jit(solution)/shard_map/ppermute | solution.py:57
  607.3 76.6 %collective-permute-start.24 = (bf16[2,128,640]{2,1,0:T(8,128)(2,1)S(1)}, bf16[2,128,640]{2,1,0:T(8,128)(2,1)S(1)}, u32[]{:S(2)}, u32[]{:S(2)}) collective-permute-start(bf16[2,128,640]{2,1,0:T(8,128)(2,1)S(1)} %dynamic-slice_bitcast_fusion.9), channel_id=1, source_target_pairs={{0,2},{2,0},{1,3},{3,1},{4,6},{6,4},{5,7},{7,5},{8,10},{10,8},{9,1... | collective-permute-start | bytes 983048 | tf_op jit(solution)/shard_map/ppermute | solution.py:57
  610.6 127.5 %collective-permute-start.30 = (bf16[2,2,128,1920]{3,2,1,0:T(8,128)(2,1)}, bf16[2,2,128,1920]{3,2,1,0:T(8,128)(2,1)}, u32[]{:S(2)}, u32[]{:S(2)}) collective-permute-start(bf16[2,2,128,1920]{3,2,1,0:T(8,128)(2,1)} %dynamic-slice_bitcast_fusion), channel_id=1, source_target_pairs={{0,4},{4,0},{1,5},{5,1},{2,6},{6,2},{3,7},{7,3},{8,12},{12,8},{9,1... | collective-permute-start | bytes 5898248 | tf_op jit(solution)/shard_map/ppermute | solution.py:49
  684.3 29.7 %collective-permute-start.27 = (bf16[128,640]{1,0:T(8,128)(2,1)S(1)}, bf16[128,640]{1,0:T(8,128)(2,1)S(1)}, u32[]{:S(2)}, u32[]{:S(2)}) collective-permute-start(bf16[128,640]{1,0:T(8,128)(2,1)S(1)} %get-tuple-element.214), channel_id=1, source_target_pairs={{0,16},{8,24},{16,0},{24,8},{1,17},{9,25},{17,1},{25,9},{2,18},{10... | collective-permute-start | bytes 491528 | tf_op jit(solution)/shard_map/ppermute | solution.py:49
  691.3 22.7 %collective-permute-start.26 = (bf16[128,640]{1,0:T(8,128)(2,1)S(1)}, bf16[128,640]{1,0:T(8,128)(2,1)S(1)}, u32[]{:S(2)}, u32[]{:S(2)}) collective-permute-start(bf16[128,640]{1,0:T(8,128)(2,1)S(1)} %get-tuple-element.213), channel_id=1, source_target_pairs={{0,8},{8,16},{16,24},{24,0},{1,9},{9,17},{17,25},{25,1},{2,10},{10... | collective-permute-start | bytes 491528 | tf_op jit(solution)/shard_map/ppermute | solution.py:49
  736.3 61.2 %collective-permute-start.31 = (bf16[2,128,1920]{2,1,0:T(8,128)(2,1)}, bf16[2,128,1920]{2,1,0:T(8,128)(2,1)}, u32[]{:S(2)}, u32[]{:S(2)}) collective-permute-start(bf16[2,128,1920]{2,1,0:T(8,128)(2,1)} %dynamic-slice_bitcast_fusion.3), channel_id=1, source_target_pairs={{0,4},{4,0},{1,5},{5,1},{2,6},{6,2},{3,7},{7,3},{8,12},{12,8},{9,1... | collective-permute-start | bytes 2949128 | tf_op jit(solution)/shard_map/ppermute | solution.py:49
  741.3 58.8 %collective-permute-start.32 = (bf16[2,128,1920]{2,1,0:T(8,128)(2,1)}, bf16[2,128,1920]{2,1,0:T(8,128)(2,1)}, u32[]{:S(2)}, u32[]{:S(2)}) collective-permute-start(bf16[2,128,1920]{2,1,0:T(8,128)(2,1)} %dynamic-slice_bitcast_fusion.2), channel_id=1, source_target_pairs={{0,2},{2,0},{1,3},{3,1},{4,6},{6,4},{5,7},{7,5},{8,10},{10,8},{9,1... | collective-permute-start | bytes 2949128 | tf_op jit(solution)/shard_map/ppermute | solution.py:57
  775.8 26.6 %collective-permute-start.25 = (bf16[5,768,128]{2,1,0:T(8,128)(2,1)}, bf16[5,768,128]{2,1,0:T(8,128)(2,1)S(1)}, u32[]{:S(2)}, u32[]{:S(2)}) collective-permute-start(bf16[5,768,128]{2,1,0:T(8,128)(2,1)} %slice.468), channel_id=1, source_target_pairs={{0,4},{4,0},{1,5},{5,1},{2,6},{6,2},{3,7},{7,3},{8,12},{12,8},{9,1... | collective-permute-start | bytes 2949128 | tf_op jit(solution)/shard_map/ppermute | solution.py:918
  865.7 19.4 %collective-permute-start.47 = (bf16[128,1920]{1,0:T(8,128)(2,1)S(1)}, bf16[128,1920]{1,0:T(8,128)(2,1)S(1)}, u32[]{:S(2)}, u32[]{:S(2)}) collective-permute-start(bf16[128,1920]{1,0:T(8,128)(2,1)S(1)} %get-tuple-element.177), channel_id=1, source_target_pairs={{0,24},{8,0},{16,8},{24,16},{1,25},{9,1},{17,9},{25,17},{2,26},{10... | collective-permute-start | bytes 1474568 | tf_op jit(solution)/shard_map/ppermute | solution.py:49
  868.1 50.4 %collective-permute-start.46 = (bf16[128,1920]{1,0:T(8,128)(2,1)S(1)}, bf16[128,1920]{1,0:T(8,128)(2,1)S(1)}, u32[]{:S(2)}, u32[]{:S(2)}) collective-permute-start(bf16[128,1920]{1,0:T(8,128)(2,1)S(1)} %get-tuple-element.176), channel_id=1, source_target_pairs={{0,16},{8,24},{16,0},{24,8},{1,17},{9,25},{17,1},{25,9},{2,18},{10... | collective-permute-start | bytes 1474568 | tf_op jit(solution)/shard_map/ppermute | solution.py:49
  872.3 46.2 %collective-permute-start.45 = (bf16[128,1920]{1,0:T(8,128)(2,1)S(1)}, bf16[128,1920]{1,0:T(8,128)(2,1)S(1)}, u32[]{:S(2)}, u32[]{:S(2)}) collective-permute-start(bf16[128,1920]{1,0:T(8,128)(2,1)S(1)} %get-tuple-element.174), channel_id=1, source_target_pairs={{0,8},{8,16},{16,24},{24,0},{1,9},{9,17},{17,25},{25,1},{2,10},{10... | collective-permute-start | bytes 1474568 | tf_op jit(solution)/shard_map/ppermute | solution.py:49
  883.0 36.7 %collective-permute-start.42 = (bf16[2,128,640]{2,1,0:T(8,128)(2,1)S(1)}, bf16[2,128,640]{2,1,0:T(8,128)(2,1)S(1)}, u32[]{:S(2)}, u32[]{:S(2)}) collective-permute-start(bf16[2,128,640]{2,1,0:T(8,128)(2,1)S(1)} %pad_maximum_fusion.25), channel_id=1, source_target_pairs={{0,1},{1,0},{2,3},{3,2},{4,5},{5,4},{6,7},{7,6},{8,9},{9,8},{10,11... | collective-permute-start | bytes 983048 | tf_op jit(solution)/shard_map/ppermute | solution.py:93
  (81 other events, 1322.1 us)
Sparse Core Ops, SparseCore 0:
  11.6 160.1 all-gather.2
  175.3 115.4 all-gather.4
  549.1 202.1 reduce-scatter.1

commit v2 on v1

--- a/solution.py
+++ b/solution.py
@@ -40,45 +40,62 @@
     return lax.dynamic_index_in_dim(array, index, axis, keepdims=False)
 
 
-def line_reduce(array, axis, name):
-    count = array.shape[axis]
+def pick_sum(arrays, index, axis):
+    total = pick(arrays[0], index, axis)
+    for array in arrays[1:]:
+        total = total + pick(array, index, axis)
+    return total
+
+
+def tips(arrays):
+    return tuple(array[(0,) * (array.ndim - 2)][:8, :128] for array in arrays)
+
+
+def line_reduce(arrays, axis, name, start=0):
+    count = arrays[0].shape[axis]
     rank = lax.axis_index(name)
-    total = pick(array, rank, axis).astype(F32)
+    total = pick_sum(arrays, rank, axis).astype(F32)
     for shift in range(1, count):
-        sent = pick(array, (rank + shift) % count, axis)
+        sent = pick_sum(arrays, (rank + shift) % count + start, axis)
         total += lax.ppermute(
             sent, name, [(i, (i + shift) % count) for i in range(count)]
         ).astype(F32)
     return total.astype(BF)
 
 
-def pair_reduce(array, axis):
+def pair_reduce(arrays, axis, start=0):
     pair = lax.axis_index("tp") // 2
-    return pick(array, pair, axis) + lax.ppermute(pick(array, 1 - pair, axis), "tp", PAIR_SWAP)
+    sent = lax.ppermute(pick_sum(arrays, 1 - pair + start, axis), "tp", PAIR_SWAP)
+    return pick_sum(arrays, pair, axis) + sent
 
 
 class Reduction:
     def __init__(self, there, here, n_shard, n_ctx, rows):
-        self.shape = (2, n_shard, n_ctx, rows, there.shape[-1])
+        self.shape = (2, n_shard // 2, n_ctx, rows, there[0].shape[-1])
         self.stage = 0
-        self.values = (there.reshape(self.shape), here.reshape(self.shape))
-
-    def advance(self):
+        self.values = (there, here)
+
+    def advance(self, start=0):
         self.stage += 1
         if self.stage == 1:
             there, here = self.values
-            self.values = (here, lax.ppermute(there, "tp", CORE_SWAP))
+            came = tuple(lax.ppermute(part, "tp", CORE_SWAP) for part in there)
+            self.values = came + tuple(here)
         elif self.stage == 2:
-            here, came = self.values
-            half = self.shape[1] // 2
-            first = here[:, :half] + came[:, :half]
-            second = here[:, half:] + came[:, half:]
-            self.values = (pair_reduce(first, 0), line_reduce(second, 2, "ctx"))
+            parts = [part.reshape(self.shape) for part in self.values]
+            self.values = (
+                pair_reduce(parts[0::2], 0, start),
+                line_reduce(parts[1::2], 2, "ctx", start),
+            )
         elif self.stage == 3:
             first, second = self.values
-            self.values = (line_reduce(first, 1, "ctx"), pair_reduce(second, 0))
+            self.values = (
+                line_reduce([first], 1, "ctx", start),
+                pair_reduce([second], 0, start),
+            )
         elif self.stage == 4:
-            self.values = (line_reduce(jnp.concatenate(self.values, axis=0), 0, "shard"),)
+            joined = jnp.concatenate(self.values, axis=0)
+            self.values = (line_reduce([joined], 0, "shard", start),)
         return self.values
 
 
@@ -94,47 +111,14 @@
     return jnp.stack([jnp.where(core == 0, array, far), jnp.where(core == 0, far, array)], axis=axis)
 
 
-def gather_line(array, name, axis):
-    count = lax.axis_size(name)
-    rank = lax.axis_index(name)
-    pieces = jnp.stack(
-        [array]
-        + [
-            lax.ppermute(array, name, [(i, (i + shift) % count) for i in range(count)])
-            for shift in range(1, count)
-        ]
-    )
-    return jnp.stack([pick(pieces, (rank - j) % count, 0) for j in range(count)], axis=axis)
-
-
-class Gathering:
-    def __init__(self, share):
-        self.stage = 0
-        self.values = (share,)
-
-    def advance(self):
-        self.stage += 1
-        if self.stage == 1:
-            pieces = gather_line(self.values[0], "shard", 0)
-            half = pieces.shape[1] // 2
-            self.values = (pieces[:, :half], pieces[:, half:])
-        elif self.stage == 2:
-            first, second = self.values
-            self.values = (gather_line(first, "ctx", 1), gather_pair(second))
-        elif self.stage == 3:
-            first, second = self.values
-            self.values = (gather_pair(first), gather_line(second, "ctx", 2))
-        elif self.stage == 4:
-            joined = gather_core(jnp.concatenate(self.values, axis=3), 1)
-            self.values = (joined.reshape(4, WIDE, joined.shape[-1]),)
-        return self.values
-
-
 def call(kernel, grid, in_specs, out_specs, out_shape, scratch, flops, moved, operands, after=(), scalars=()):
     used = len(scalars) + len(operands)
+    outs = len(out_shape)
 
     def body(*refs):
-        kernel(*refs[:used], *refs[used + len(after) :])
+        kept = refs[used + len(after) :]
+        kept[outs][0] = 0
+        kernel(*refs[:used], *kept[:outs], *kept[outs + 1 :])
 
     return pl.pallas_call(
         body,
@@ -142,10 +126,10 @@
             num_scalar_prefetch=len(scalars),
             grid=grid,
             in_specs=list(in_specs) + [pl.BlockSpec(memory_space=pl.ANY)] * len(after),
-            out_specs=out_specs,
+            out_specs=list(out_specs) + [pl.BlockSpec(memory_space=pltpu.SMEM)],
             scratch_shapes=scratch,
         ),
-        out_shape=out_shape,
+        out_shape=list(out_shape) + [jax.ShapeDtypeStruct((1,), jnp.int32)],
         compiler_params=pltpu.CompilerParams(vmem_limit_bytes=VMEM_LIMIT),
         cost_estimate=pl.CostEstimate(flops=flops, bytes_accessed=moved, transcendentals=0),
     )(*scalars, *operands, *after)
@@ -175,23 +159,19 @@
         out_ref[part, :] += mm(inner, down_w[0], NT)
 
 
-def weight_specs(columns):
-    return [
-        pl.BlockSpec((1, WIDE, columns), functools.partial(lambda c, t: (t, 0, c), c))
-        for c in range(3)
-    ]
-
-
-def mlp_forward(normed, mid, weights, after=()):
+def mlp_forward(normed, mid, weights, start, columns, after=()):
     rows = normed.shape[0]
-    columns = weights.shape[2] // 3
     parts = weights.shape[0]
-    whole = pl.BlockSpec((rows, WIDE), lambda t: (0, 0))
+    whole = full(rows, WIDE)
     kept = pl.BlockSpec((1, rows, columns), lambda t: (t, 0, 0))
     return call(
         mlp_forward_kernel,
         (parts,),
-        [whole, whole] + weight_specs(columns),
+        [whole, whole]
+        + [
+            pl.BlockSpec((1, WIDE, columns), functools.partial(lambda c, t: (t, 0, c), start + c))
+            for c in range(3)
+        ],
         [whole, kept, kept],
         [
             jax.ShapeDtypeStruct((rows, WIDE), F32),
@@ -200,7 +180,7 @@
         ],
         [],
         6 * rows * WIDE * columns * parts,
-        weights.size * 2 + rows * (WIDE * 10 + columns * parts * 8),
+        WIDE * columns * parts * 6 + rows * (WIDE * 10 + columns * parts * 8),
         (normed, mid, weights, weights, weights),
         after,
     )
@@ -217,11 +197,9 @@
     up_w,
     down_w,
     back_ref,
-    out_w,
-    inner,
-    gate_g,
-    up_g,
+    *rest,
 ):
+    *outs, inner, gate_g, up_g = rest
     @pl.when(pl.program_id(0) == 0)
     def _():
         back_ref[...] = base_ref[...]
@@ -242,30 +220,29 @@
     for at in range(0, WIDE, 256):
         part = pl.ds(at, 256)
         normed = normed_ref[:, part]
+        out_w = outs[at * len(outs) // WIDE]
+        part = pl.ds(at % (WIDE // len(outs)), 256)
         out_w[0, part, 0:columns] = mm(normed, gate_g[...], TN).astype(BF)
         out_w[0, part, columns : 2 * columns] = mm(normed, up_g[...], TN).astype(BF)
-        out_w[0, part, 2 * columns : 3 * columns] = mm(grad_ref[:, part], inner[...], TN).astype(BF)
-
-
-def mlp_backward(order, grad, normed, base, gate, up, weights, after=()):
-    rows = normed.shape[0]
-    columns = weights.shape[2] // 3
+        out_w[0, part, 2 * columns : 3 * columns] = mm(grad_ref[:, pl.ds(at, 256)], inner[...], TN).astype(BF)
+
+
+def mlp_backward(order, pieces, grad, normed, base, gate, up, weights, start, after=()):
+    rows, columns = gate.shape[1:]
     parts = order.shape[0]
     whole = full(rows, WIDE)
     kept = pl.BlockSpec((1, rows, columns), lambda i, order: (order[i], 0, 0))
     weight_parts = [
-        pl.BlockSpec((1, WIDE, columns), functools.partial(lambda c, i, order: (order[i], 0, c), c))
+        pl.BlockSpec((1, WIDE, columns), functools.partial(lambda c, i, order: (order[i], 0, c), start + c))
         for c in range(3)
     ]
     return call(
         mlp_backward_kernel,
         (parts,),
         [whole, whole, whole, kept, kept] + weight_parts,
-        [whole, pl.BlockSpec((1, WIDE, 3 * columns), lambda i, order: (i, 0, 0))],
-        [
-            jax.ShapeDtypeStruct((rows, WIDE), F32),
-            jax.ShapeDtypeStruct((parts, WIDE, 3 * columns), BF),
-        ],
+        [whole] + [pl.BlockSpec((1, WIDE // pieces, 3 * columns), lambda i, order: (i, 0, 0))] * pieces,
+        [jax.ShapeDtypeStruct((rows, WIDE), F32)]
+        + [jax.ShapeDtypeStruct((parts, WIDE // pieces, 3 * columns), BF)] * pieces,
         [pltpu.VMEM((rows, columns), BF)] * 3,
         12 * rows * WIDE * columns * parts,
         parts * WIDE * columns * 12 + rows * (WIDE * 12 + columns * parts * 8),
@@ -325,12 +302,18 @@
                         pair_ref[group, rows, :] = keys[group] + high_lanes(two if side else other_half(two))
 
 
-def project(hidden, gain, weights, cosine, sine, width, after=()):
+def project(hidden, gain, weights, layer, cosine, sine, width, after=()):
     rows = hidden.shape[0]
     return call(
         functools.partial(project_kernel, width),
         (1,),
-        [full(rows, WIDE), full(1, WIDE), full(3, WIDE, 640), full(rows, 128), full(rows, 128)],
+        [
+            full(rows, WIDE),
+            full(1, WIDE),
+            pl.BlockSpec((3, WIDE, 640), lambda i: (0, 0, layer)),
+            full(rows, 128),
+            full(rows, 128),
+        ],
         [full(rows, WIDE), full(QUERY_HEADS, rows, 128), full(KEY_VALUE_HEADS, rows, 128)],
         [
             jax.ShapeDtypeStruct((rows, WIDE), BF),
@@ -366,14 +349,14 @@
         normed_ref[rows, :] = (mid * row_scale(mid, width) * gain_ref[...]).astype(BF)
 
 
-def out_forward(mixed, weights, hidden, gain, width, after=()):
+def out_forward(mixed, weights, layer, hidden, gain, width, after=()):
     rows = hidden.shape[0]
     return call(
         functools.partial(out_forward_kernel, width),
         (1,),
         [
             full(QUERY_HEADS, rows, 128),
-            pl.BlockSpec((2, WIDE, 640), lambda i: (1, 0, 0)),
+            pl.BlockSpec((2, WIDE, 640), lambda i: (1, 0, layer)),
             full(rows, WIDE),
             full(1, WIDE),
         ],
@@ -422,7 +405,7 @@
                         mixed_g[head, rows, :] = high_lanes(two if side else other_half(two))
 
 
-def out_backward(back, mid, grad, gain, weights, width, after=()):
+def out_backward(back, mid, grad, gain, weights, layer, width, after=()):
     rows = mid.shape[0]
     return call(
         functools.partial(out_backward_kernel, width),
@@ -432,7 +415,7 @@
             full(rows, WIDE),
             full(rows, WIDE),
             full(1, WIDE),
-            pl.BlockSpec((2, WIDE, 640), lambda i: (1, 0, 0)),
+            pl.BlockSpec((2, WIDE, 640), lambda i: (1, 0, layer)),
         ],
         [full(rows, WIDE), full(rows, WIDE), full(QUERY_HEADS, rows, 128), full(1, WIDE)],
         [
@@ -449,44 +432,54 @@
     )
 
 
-def outer_products(left, right):
-    return [mm(left[:, at : at + 256], right, TN).astype(BF) for at in range(0, WIDE, 256)]
-
-
-def query_backward_kernel(query_g, normed_ref, rounded_ref, last_ref, first_ref, out_w):
+def query_backward_kernel(
+    query_g, normed_ref, rounded_ref, mixed_ref, last_ref, weights_ref, back_ref, out_w, mixed_w, first
+):
     for rows in row_steps(normed_ref.shape[0]):
-        first_ref[rows, :] = jnp.concatenate(
+        part = jnp.concatenate(
             [query_g[at, rows, :] + other_half(query_g[at + 1, rows, :]) for at in range(0, 10, 2)], axis=1
         )
-    for slot, left, right in ((0, normed_ref, first_ref), (1, rounded_ref, last_ref)):
-        for at in range(0, WIDE, 256):
-            out_w[slot, pl.ds(at, 256), :] = mm(left[:, pl.ds(at, 256)], right[...], TN).astype(BF)
-
-
-def query_backward(query_g, normed, rounded, last, after=()):
+        first[rows, :] = part
+        back_ref[rows, :] = mm(part, weights_ref[0], NT)
+    for at in range(0, WIDE, 256):
+        part = pl.ds(at, 256)
+        out_w[0, part, :] = mm(normed_ref[:, part], first[...], TN).astype(BF)
+        rounded = rounded_ref[:, part]
+        out_w[1, part, :] = mm(rounded, last_ref[...], TN).astype(BF)
+        mixed_w[part, :] = mm(rounded, mixed_ref[...], TN)
+
+
+def query_backward(query_g, normed, rounded, mixed, last, weights, layer, after=()):
     rows = normed.shape[0]
     return call(
         query_backward_kernel,
         (1,),
-        [full(10, rows, 128), full(rows, WIDE), full(rows, WIDE), full(rows, 640)],
-        [full(rows, 640), full(2, WIDE, 640)],
-        [jax.ShapeDtypeStruct((rows, 640), BF), jax.ShapeDtypeStruct((2, WIDE, 640), BF)],
-        [],
-        4 * rows * WIDE * 640,
-        WIDE * 640 * 4 + rows * WIDE * 4 + rows * 5120,
-        (query_g, normed, rounded, last),
+        [
+            full(10, rows, 128),
+            full(rows, WIDE),
+            full(rows, WIDE),
+            full(rows, 640),
+            full(rows, 640),
+            pl.BlockSpec((1, WIDE, 640), lambda i: (0, 0, layer)),
+        ],
+        [full(rows, WIDE), full(2, WIDE, 640), full(WIDE, 640)],
+        [
+            jax.ShapeDtypeStruct((rows, WIDE), F32),
+            jax.ShapeDtypeStruct((2, WIDE, 640), BF),
+            jax.ShapeDtypeStruct((WIDE, 640), F32),
+        ],
+        [pltpu.VMEM((rows, 640), BF)],
+        8 * rows * WIDE * 640,
+        WIDE * 640 * 10 + rows * WIDE * 8 + rows * 5120,
+        (query_g, normed, rounded, mixed, last, weights),
         after,
     )
 
 
-def key_backward_kernel(
-    width,
-    shares,
-    *refs,
-):
+def key_backward_kernel(width, shares, *refs):
     pairs = refs[:shares]
-    query_g, first_ref, mixed_ref, normed_ref, rounded_ref, weights_ref, hidden_ref, mid_g, gain_ref = refs[shares : shares + 9]
-    cos_ref, sin_ref, grad_ref, out_w, gain_g, second, third = refs[shares + 9 :]
+    query_g, back_ref, mixed_w, normed_ref, weights_ref, hidden_ref, mid_g, gain_ref = refs[shares : shares + 8]
+    cos_ref, sin_ref, grad_ref, rounded_ref, out_w, gain_g, second, third = refs[shares + 8 :]
     gain_g[...] = jnp.zeros_like(gain_g)
     for rows in row_steps(hidden_ref.shape[0]):
         keys, values = [], []
@@ -504,37 +497,32 @@
         second_part = jnp.concatenate(
             [heads[at] + other_half(heads[at + 1]) for at in range(0, 10, 2)], axis=1
         )
-        blank = jnp.zeros_like(values[0])
         third_part = jnp.concatenate(
-            [
-                other_half(values[0]) + values[1],
-                other_half(values[2]) + values[3],
-                other_half(values[4]),
-                blank,
-                blank,
-            ],
+            [other_half(values[0]) + values[1], other_half(values[2]) + values[3], other_half(values[4])],
             axis=1,
         )
         second[rows, :] = second_part
         third[rows, :] = third_part
         back = (
-            mm(first_ref[rows, :], weights_ref[0], NT)
+            back_ref[rows, :]
             + mm(second_part, weights_ref[1], NT)
-            + mm(third_part, weights_ref[2], NT)
+            + mm(third_part, weights_ref[2, :, :384], NT)
         )
         change, gain_part = norm_back(back, hidden_ref[rows, :], gain_ref[...], width)
         gain_g[...] += gain_part
-        grad_ref[rows, :] = mid_g[rows, :] + change
+        grad = mid_g[rows, :] + change
+        grad_ref[rows, :] = grad
+        rounded_ref[rows, :] = grad.astype(BF)
     for at in range(0, WIDE, 256):
         part = pl.ds(at, 256)
-        out_w[0, part, :] = mm(normed_ref[:, part], second[...], TN).astype(BF)
-        out_w[1, part, :] = (
-            mm(normed_ref[:, part], third[...], TN) + mm(rounded_ref[:, part], mixed_ref[...], TN)
-        ).astype(BF)
+        normed = normed_ref[:, part]
+        out_w[0, part, :] = mm(normed, second[...], TN).astype(BF)
+        out_w[1, part, :384] = (mm(normed, third[...], TN) + mixed_w[part, :384]).astype(BF)
+        out_w[1, part, 384:] = mixed_w[part, 384:].astype(BF)
 
 
 def key_backward(
-    pair_g, arrived, query_g, first, mixed, normed, rounded, weights, hidden, mid_g, gain, cosine, sine, width, after=()
+    pair_g, arrived, query_g, back, mixed_w, normed, weights, layer, hidden, mid_g, gain, cosine, sine, width, after=()
 ):
     rows = hidden.shape[0]
     own = pl.BlockSpec((KEY_VALUE_HEADS, rows, 128), lambda i: (0, 0, 0))
@@ -544,27 +532,27 @@
         [own] * (1 + len(arrived))
         + [
             pl.BlockSpec((5, rows, 128), lambda i: (2, 0, 0)),
-            full(rows, 640),
-            full(rows, 640),
             full(rows, WIDE),
+            full(WIDE, 640),
             full(rows, WIDE),
-            full(3, WIDE, 640),
+            pl.BlockSpec((3, WIDE, 640), lambda i: (0, 0, layer)),
             full(rows, WIDE),
             full(rows, WIDE),
             full(1, WIDE),
             full(rows, 128),
             full(rows, 128),
         ],
-        [full(rows, WIDE), full(2, WIDE, 640), full(1, WIDE)],
+        [full(rows, WIDE), full(rows, WIDE), full(2, WIDE, 640), full(1, WIDE)],
         [
             jax.ShapeDtypeStruct((rows, WIDE), F32),
+            jax.ShapeDtypeStruct((rows, WIDE), BF),
             jax.ShapeDtypeStruct((2, WIDE, 640), BF),
             jax.ShapeDtypeStruct((1, WIDE), F32),
         ],
-        [pltpu.VMEM((rows, 640), BF)] * 2,
-        12 * rows * WIDE * 640,
-        WIDE * 640 * 10 + rows * WIDE * 16 + rows * 12800,
-        (pair_g, *arrived, query_g, first, mixed, normed, rounded, weights, hidden, mid_g, gain, cosine, sine),
+        [pltpu.VMEM((rows, 640), BF), pltpu.VMEM((rows, 384), BF)],
+        7 * rows * WIDE * 640,
+        WIDE * 640 * 12 + rows * WIDE * 20 + rows * 12800,
+        (pair_g, *arrived, query_g, back, mixed_w, normed, weights, hidden, mid_g, gain, cosine, sine),
         after,
     )
 
@@ -746,7 +734,7 @@
         "kgqt,ktd->kgqd", (weight / norm).astype(BF), pairs[..., HEAD_DIM:], preferred_element_type=F32
     )
     mixed = jnp.pad(mixed.reshape(QUERY_HEADS, rows, HEAD_DIM), ((0, 0), (0, 0), (HEAD_DIM, 0)))
-    return mixed.astype(BF), top + jnp.log(norm)
+    return mixed.astype(BF), top + jnp.log(norm), jnp.zeros((1,), jnp.int32)
 
 
 def plain_attend_back(places, query, pairs, grad, out, total, cosine_t, sine_t, after=()):
@@ -763,7 +751,7 @@
     moved = query_g * sine_t.T
     query_g = query_g * cosine_t.T + jnp.concatenate([moved[..., half:], -moved[..., :half]], axis=-1)
     query_g = jnp.pad(query_g.reshape(QUERY_HEADS, rows, HEAD_DIM), ((0, 0), (0, 0), (0, HEAD_DIM)))
-    return query_g.astype(BF), jnp.concatenate([key_g, value_g], axis=-1)
+    return query_g.astype(BF), jnp.concatenate([key_g, value_g], axis=-1), jnp.zeros((1,), jnp.int32)
 
 
 def local(
@@ -811,15 +799,14 @@
         joined = jnp.concatenate(
             [w_query[layer], key_weight[layer], value_weight[layer], w_out[layer].T], axis=1
         )
-        share = lax.dynamic_slice_in_dim(joined, tp_rank * 640, 640, 1)
         gains = jnp.concatenate(
             [
                 jnp.pad(gain_attn[layer], (0, 128 - own_rows)),
-                jnp.pad(gain_mlp[layer], (0, 640 - 128 - own_rows)),
+                jnp.pad(gain_mlp[layer], (0, 2560 - 128 - own_rows)),
             ]
         )
-        gains = jnp.where(tp_rank == 0, gains, jnp.zeros_like(gains))
-        return jnp.concatenate([share, gains[None, :], jnp.zeros((extra - 1, 640), BF)], axis=0)
+        joined = jnp.concatenate([joined, gains[None, :], jnp.zeros((extra - 1, 2560), BF)], axis=0)
+        return lax.dynamic_slice_in_dim(joined, tp_rank * 640, 640, 1)
 
     def mlp_share(layer):
         joined = jnp.concatenate([w_gate[layer], w_up[layer], w_down[layer].T], axis=1)
@@ -830,8 +817,9 @@
             4, WIDE, share.shape[1]
         )
 
-    def gains_of(weights):
-        lines = weights[0].reshape(blocks, rows, 640)[:, own_rows, :]
+
+    def gains_of(weights, layer):
+        lines = weights[0, :, layer * 640 : layer * 640 + 640].reshape(blocks, rows, 640)[:, own_rows, :]
         return tuple(
             lines[:, at : at + rows].reshape(WIDE).astype(F32)[None, :] for at in (0, 128)
         )
@@ -844,35 +832,28 @@
         attend_call = functools.partial(plain_attend, places)
         attend_back_call = functools.partial(plain_attend_back, places)
 
-    mlp_w = [gather(mlp_share(layer)) for layer in range(DECODER_LAYERS)]
-    attn_now = Gathering(attn_share(0))
-    for _ in range(4):
-        attn_now.advance()
+    columns = w_gate.shape[2]
+    shares = [attn_share(layer) for layer in range(DECODER_LAYERS)]
+    front_w = gather(jnp.concatenate([*shares, mlp_share(0)], axis=1))
+    mlp_w = [(front_w, DECODER_LAYERS)]
+    for layer in range(1, DECODER_LAYERS):
+        mlp_w.append((gather(mlp_share(layer)), 0))
 
     hidden = mm(tokens[0], spread)
     kept = []
     for layer in range(DECODER_LAYERS):
-        weights = attn_now.values[0]
-        gain_a, gain_m = gains_of(weights)
-        if layer + 1 < DECODER_LAYERS:
-            attn_now = Gathering(attn_share(layer + 1))
-            following = attn_now.advance
-        else:
-            following = tuple
-        attn_in, query, pair = project(hidden, gain_a, weights, cosine, sine, model_width)
-        ready = following()
+        weights = front_w
+        gain_a, gain_m = gains_of(weights, layer)
+        attn_in, query, pair, _ = project(hidden, gain_a, weights, layer, cosine, sine, model_width)
         around = [pair]
         for shift in range(1, n_ctx):
             around.append(
                 lax.ppermute(pair, "ctx", [(i, (i + shift) % n_ctx) for i in range(n_ctx)])
             )
         pairs = jnp.concatenate(around, axis=1)
-        mixed, total = attend_call(query, pairs, after=ready)
-        ready = following()
-        first, last, mid, mlp_in = out_forward(mixed, weights, hidden, gain_m, model_width, after=ready)
-        ready = following()
-        result, gate, up = mlp_forward(mlp_in, mid, mlp_w[layer], after=ready)
-        following()
+        mixed, total, _ = attend_call(query, pairs)
+        first, last, mid, mlp_in, _ = out_forward(mixed, weights, layer, hidden, gain_m, model_width)
+        result, gate, up, _ = mlp_forward(mlp_in, mid, *mlp_w[layer], columns)
         kept.append(
             (hidden, weights, gain_a, gain_m, attn_in, query, pairs, mixed, total, first, last, mid, mlp_in, gate, up)
         )
@@ -881,39 +862,31 @@
 
     core = tp_rank % 2
     grad_run = mm(out_grad[0], spread)
+    grad_in = grad_run.astype(BF)
     blank = jnp.zeros_like(grad_run)
     mlp_done, attn_done = [None] * DECODER_LAYERS, [None] * DECODER_LAYERS
-    attn_sum = None
     for layer in reversed(range(DECODER_LAYERS)):
         (hidden, weights, gain_a, gain_m, attn_in, query, pairs, mixed, total, first, last, mid, mlp_in, gate, up) = kept[layer]
-        attn_step = attn_sum.advance if attn_sum is not None else tuple
-        grad_in = grad_run.astype(BF)
-        sources = (gate, up, mlp_w[layer])
-        mlp_step = tuple
-        if layer > 0:
-            back, parts = mlp_backward(jnp.arange(4, dtype=jnp.int32), grad_in, mlp_in, blank, *sources)
-            summed = lax.psum_scatter(
-                parts.reshape(4 * WIDE, -1), ("tp", "shard", "ctx"), scatter_dimension=0, tiled=True
-            )
-            mlp_done[layer] = summed
-            ready = ()
-        else:
-            pair_at = jnp.array([0, 2], jnp.int32)
-            ready = attn_step()
-            back, there = mlp_backward(pair_at + 1 - core, grad_in, mlp_in, blank, *sources)
-            ready = attn_step()
-            back, here = mlp_backward(pair_at + core, grad_in, mlp_in, back, *sources, after=ready[:0])
-            mlp_sum = Reduction(there, here, n_shard, n_ctx, rows)
-            mlp_step = mlp_sum.advance
-            mlp_step()
-            ready = ready + mlp_sum.values[1:]
-        mid_g, rounded, mixed_g, gain_m_grad = out_backward(
-            back, mid, grad_run, gain_m, weights, model_width, after=ready
-        )
-        ready = attn_step()
-        mlp_step()
-        query_g, pair_g = attend_back_call(query, pairs, mixed_g, mixed, total, cosine_t, sine_t, after=ready)
-        ready = attn_step() + (mlp_sum.values if layer == 0 else ())
+        sources = (gate, up, *mlp_w[layer])
+        final = layer == 0
+        ready = ()
+        if final:
+            ready = tips(attn_sum.advance()[:2])
+        order = jnp.arange(4, dtype=jnp.int32)
+        back, parts, token = mlp_backward(order, 1, grad_in, mlp_in, blank, *sources)
+        mlp_done[layer] = lax.psum_scatter(
+            parts.reshape(4 * WIDE, -1), ("tp", "shard", "ctx"), scatter_dimension=0, tiled=True
+        )
+        mid_g, rounded, mixed_g, gain_m_grad, _ = out_backward(
+            back, mid, grad_run, gain_m, weights, layer, model_width, after=ready
+        )
+        ready = ()
+        if final:
+            ready = tips(attn_sum.advance(token[0]))
+        query_g, pair_g, token = attend_back_call(query, pairs, mixed_g, mixed, total, cosine_t, sine_t)
+        if final:
+            attn_sum.advance(token[0])
+            ready = ready + tips(mlp_done[layer + 1 :])
         arrived = [
             lax.ppermute(
                 pair_g[:, shift * local_length : (shift + 1) * local_length].astype(BF),
@@ -922,29 +895,27 @@
             )
             for shift in range(1, n_ctx)
         ]
-        first_g, early = query_backward(query_g, attn_in, rounded, last, after=ready)
-        mlp_step()
-        if attn_sum is not None:
-            attn_done[layer + 1] = gather_core(gather_pair(attn_sum.values[0]), 1)
-        ready = mlp_sum.values if layer == 0 else ()
-        grad_run, late, gain_a_grad = key_backward(
+        back, early, mixed_w, token = query_backward(
+            query_g, attn_in, rounded, first, last, weights, layer, after=ready
+        )
+        grad_run, grad_in, late, gain_a_grad, token = key_backward(
             pair_g,
             arrived,
             query_g,
-            first_g,
-            first,
+            back,
+            mixed_w,
             attn_in,
-            rounded,
             weights,
+            layer,
             hidden,
             mid_g,
             gain_a,
             cosine,
             sine,
             model_width,
-            after=ready,
-        )
-        mlp_step()
+        )
+        if final:
+            attn_done[layer + 1] = attn_sum.advance(token[0])[0]
         lines = jnp.concatenate(
             [
                 jnp.pad(gain_a_grad.reshape(blocks, rows), ((0, 0), (0, 128 - rows))),
@@ -955,21 +926,28 @@
         at = lax.broadcasted_iota(jnp.int32, (1, rows, 1), 1)
         second_w = jnp.where(at == own_rows, lines[:, None, :], late[0].reshape(blocks, rows, 640))
         second_w = second_w.reshape(WIDE, 640)
-        there = jnp.stack([jnp.where(core == 0, second_w, early[0]), jnp.where(core == 0, early[1], late[1])])
-        here = jnp.stack([jnp.where(core == 0, early[0], second_w), jnp.where(core == 0, late[1], early[1])])
+        there, here = [], []
+        for part in (slice(0, WIDE // 2), slice(WIDE // 2, WIDE)):
+            parts = early[0, part], second_w[part], late[1, part], early[1, part]
+            there.append(
+                jnp.stack([jnp.where(core == 0, parts[1], parts[0]), jnp.where(core == 0, parts[3], parts[2])])
+            )
+            here.append(
+                jnp.stack([jnp.where(core == 0, parts[0], parts[1]), jnp.where(core == 0, parts[2], parts[3])])
+            )
         attn_sum = Reduction(there, here, n_shard, n_ctx, rows)
     for _ in range(4):
         attn_sum.advance()
-    attn_done[0] = gather_core(gather_pair(attn_sum.values[0]), 1)
-    mlp_done[0] = mlp_sum.values[0]
+    attn_done[0] = attn_sum.values[0]
+    attn_done = gather_core(gather_pair(jnp.stack(attn_done)), 1)
 
     grad_high = grad_run.astype(BF)
     grad_low = (grad_run - grad_high.astype(F32)).astype(BF)
     tokens_grad = (mm(grad_high, spread, NT) + mm(grad_low, spread, NT))[None]
 
     outs = [[] for _ in range(9)]
-    for mlp, attn in zip(mlp_done, attn_done):
-        attn = attn.reshape(4, rows, 640)
+    for layer, mlp in enumerate(mlp_done):
+        attn = attn_done[:, :, layer].reshape(4, rows, 640)
         line = attn[1, own_rows].astype(F32)
         attn = attn[:, :own_rows].transpose(1, 0, 2).reshape(own_rows, 2560).astype(F32)
         mlp = mlp[:own_rows].astype(F32)

time: 945 us -> 839 us (0.89)
  starting transfers between devices: 95.4 us -> 23.4 us
  other arithmetic: 66.8 us -> 35.7 us
  local copies, waits for them, and re-layouts: 68.3 us -> 47.8 us
  Pallas kernels: 344 us -> 362 us
  waiting for transfers between devices: 331 us -> 317 us
    ppermute x19 -> x8, waiting for transfers between devices: 196 us -> 29.3 us  [the longest x4 29.3 us: pair_reduce(): lax.ppermute(pick_sum(arrays, 1 - pair + start, axis), 'tp', PAIR_SWAP)]
    all_gather x2, waiting for transfers between devices: 0.01 us -> 153 us  [gather(): lax.all_gather(share, ('tp', 'shard', 'ctx'), axis=0, tiled=True)]
    ppermute x15 -> x10, waiting for transfers between devices: 75.4 us -> 37.4 us  [line_reduce(): lax.ppermute(sent, name, [(i, (i + shift) % count) for i in range(count)])]
    ppermute x2, starting transfers between devices: 37.1 us -> 1.92 us  [local(): lax.ppermute(pair_g[:, shift * local_length:(shift + 1) * local_length].a...]
    ppermute x2, waiting for transfers between devices: 13.4 us -> 36.7 us  [local(): lax.ppermute(pair_g[:, shift * local_length:(shift + 1) * local_length].a...]
    pallas_call x19 -> x18, Pallas kernels: 344 us -> 362 us  [call(): pl.pallas_call(body, grid_spec=pltpu.PrefetchScalarGridSpec(num_scalar_pr...]
    ppermute x19 -> x8, starting transfers between devices: 20.1 us -> 3.37 us  [the longest x4 2.24 us: pair_reduce(): lax.ppermute(pick_sum(arrays, 1 - pair + start, axis), 'tp', PAIR_SWAP)]
    ppermute x15 -> x10, starting transfers between devices: 22.1 us -> 13.5 us  [line_reduce(): lax.ppermute(sent, name, [(i, (i + shift) % count) for i in range(count)])]
  transfers between devices with their start and end apart: 51 -> 28, of which waited for: 26 -> 14; matrix products, arithmetic and copies ran while one was open for 12% -> 8% of each run, Pallas kernels for 21% -> 36%
where the time goes in v2:
time: 839 us; the launch traced here: 824 us
  Pallas kernels  362 us (43%)
  waiting for transfers between devices  317 us (38%)
  local copies, waits for them, and re-layouts  47.8 us (6%)
  other arithmetic  35.7 us (4%)
  starting transfers between devices  23.4 us (3%)
  matrix products  19.6 us (2%)
  between operations  19.4 us (2%)
    pallas_call x18, Pallas kernels, call(): pl.pallas_call(body, grid_spec=pltpu.PrefetchScalarGridSpec(num_scalar_pr...  362 us
    all_gather x2, waiting for transfers between devices, gather(): lax.all_gather(share, ('tp', 'shard', 'ctx'), axis=0, tiled=True)  153 us
    ppermute x2, waiting for transfers between devices, local(): lax.ppermute(pair, 'ctx', [(i, (i + shift) % n_ctx) for i in range(n_ctx)])  43.5 us
    ppermute x10, waiting for transfers between devices, line_reduce(): lax.ppermute(sent, name, [(i, (i + shift) % count) for i in range(count)])  37.4 us
    ppermute x2, waiting for transfers between devices, local(): lax.ppermute(pair_g[:, shift * local_length:(shift + 1) * local_length].a...  36.7 us
    ppermute x4, waiting for transfers between devices, pair_reduce(): lax.ppermute(pick_sum(arrays, 1 - pair + start, axis), 'tp', PAIR_SWAP)  29.3 us
    dot_general x5, matrix products, mm(): return lax.dot_general(left, right, dims, preferred_element_type=F32)  19.6 us
  transfers between devices with their start and end apart: 28, of which 14 were waited for; matrix products, arithmetic and copies ran while one was open for 8% of the time, Pallas kernels for 36%

profile of v2, /device:TPU:0, one launch (start us, length us, event | category | flops | bytes accessed | tf_op | source)
XLA Modules:
  0.0 824.3 jit_solution(8116219904275647230)
XLA Ops:
  26.1 5.0 fusion.10.refs_0_.refs_2_.refs_7_
  31.1 152.8 %all-gather.3.cloned.1.call-done = bf16[4096,3200]{1,0:T(8,128)(2,1)} async-done(((bf16[128,3200]{1,0:T(8,128)(2,1)}), bf16[4096,3200]{1,0:T(8,128)(2,1)}) %all-gather.3.cloned.1.call-update) | async-done | bytes 26214416 | tf_op jit(solution)/shard_map/all_gather | solution.py:816
  186.5 8.9 %shard_map.203 = (bf16[768,1024]{1,0:T(8,128)(2,1)}, bf16[15,768,128]{2,1,0:T(8,128)(2,1)}, bf16[5,768,128]{2,1,0:T(8,128)(2,1)}, s32[1]{0:T(128)}) custom-call(f32[768,1024]{1,0:T(8,128)} %fusion.10.refs_0_.refs_2_.refs_7_, f32[1,1024]{1,0:T(1,128)} %bitcast.341, bf16[4,1024,3200]{2,1,0:T(8,128)(2,1)} %bitcast.274, ...), custom_call_target="tpu_custom_call" | custom-call | flops 2516582400 | bytes 12713984 | tf_op jit(solution)/shard_map/pallas_call | solution.py:123
  198.6 25.5 %collective-permute-done = bf16[5,768,128]{2,1,0:T(8,128)(2,1)S(1)} collective-permute-done((bf16[5,768,128]{2,1,0:T(8,128)(2,1)}, bf16[5,768,128]{2,1,0:T(8,128)(2,1)S(1)}, u32[]{:S(2)}, u32[]{:S(2)}) %collective-permute-start) | collective-permute-done | bytes 983072 | tf_op jit(solution)/shard_map/ppermute | solution.py:851
  225.5 26.8 %shard_map.204 = (bf16[15,768,128]{2,1,0:T(8,128)(2,1)}, f32[5,2,1,1152]{3,2,1,0:T(1,128)}, s32[1]{0:T(128)}) custom-call(s32[4]{0:T(128)} %get-tuple-element.157.refs_0_, bf16[15,768,128]{2,1,0:T(8,128)(2,1)} %get-tuple-element.67.refs_1_, bf16[5,1536,128]{2,1,0:T(8,128)(2,1)} %copy-done.13), custom_call_target="tpu_custom_call" | custom-call | flops 18119393280 | bytes 11796480 | tf_op jit(solution)/shard_map/pallas_call | solution.py:123
  252.2 8.8 %shard_map.205 = (bf16[768,640]{1,0:T(8,128)(2,1)}, bf16[768,640]{1,0:T(8,128)(2,1)}, f32[768,1024]{1,0:T(8,128)}, bf16[768,1024]{1,0:T(8,128)(2,1)}, s32[1]{0:T(128)}) custom-call(bf16[15,768,128]{2,1,0:T(8,128)(2,1)} %get-tuple-element.69.refs_0_.refs_4_, bf16[4,1024,3200]{2,1,0:T(8,128)(2,1)} %bitcast.275, f32[768,1024]{1,0:T(8,128)} %fusion.10.refs_0_.refs_2_.refs_7_, ...), custom_call_target="tpu_custom_call" | custom-call | flops 2013265920 | bytes 15400960 | tf_op jit(solution)/shard_map/pallas_call | solution.py:123
  261.0 22.1 %shard_map.206 = (f32[768,1024]{1,0:T(8,128)}, f32[4,768,640]{2,1,0:T(8,128)}, f32[4,768,640]{2,1,0:T(8,128)}, s32[1]{0:T(128)}) custom-call(bf16[768,1024]{1,0:T(8,128)(2,1)} %get-tuple-element.70.refs_0_.refs_2_, f32[768,1024]{1,0:T(8,128)} %get-tuple-element.71.refs_1_, bf16[4,1024,3200]{2,1,0:T(8,128)(2,1)} %bitcast.276, ...), custom_call_target="tpu_custom_call" | custom-call | flops 12079595520 | bytes 39321600 | tf_op jit(solution)/shard_map/pallas_call | solution.py:123
  283.2 8.9 %shard_map.207 = (bf16[768,1024]{1,0:T(8,128)(2,1)}, bf16[15,768,128]{2,1,0:T(8,128)(2,1)}, bf16[5,768,128]{2,1,0:T(8,128)(2,1)}, s32[1]{0:T(128)}) custom-call(f32[768,1024]{1,0:T(8,128)} %get-tuple-element.72.refs_0_.refs_2_.refs_7_, f32[1,1024]{1,0:T(1,128)} %bitcast.343, bf16[4,1024,3200]{2,1,0:T(8,128)(2,1)} %bitcast.279, ...), custom_call_target="tpu_custom_call" | custom-call | flops 2516582400 | bytes 12713984 | tf_op jit(solution)/shard_map/pallas_call | solution.py:123
  297.8 18.1 %collective-permute-done.1 = bf16[5,768,128]{2,1,0:T(8,128)(2,1)S(1)} collective-permute-done((bf16[5,768,128]{2,1,0:T(8,128)(2,1)}, bf16[5,768,128]{2,1,0:T(8,128)(2,1)S(1)}, u32[]{:S(2)}, u32[]{:S(2)}) %collective-permute-start.1) | collective-permute-done | bytes 983072 | tf_op jit(solution)/shard_map/ppermute | solution.py:851
  317.2 26.5 %shard_map.208 = (bf16[15,768,128]{2,1,0:T(8,128)(2,1)}, f32[5,2,1,1152]{3,2,1,0:T(1,128)}, s32[1]{0:T(128)}) custom-call(s32[4]{0:T(128)} %get-tuple-element.157.refs_0_, bf16[15,768,128]{2,1,0:T(8,128)(2,1)} %get-tuple-element.73.refs_1_, bf16[5,1536,128]{2,1,0:T(8,128)(2,1)} %copy-done.14), custom_call_target="tpu_custom_call" | custom-call | flops 18119393280 | bytes 11796480 | tf_op jit(solution)/shard_map/pallas_call | solution.py:123
  343.7 8.8 %shard_map.209 = (bf16[768,640]{1,0:T(8,128)(2,1)}, bf16[768,640]{1,0:T(8,128)(2,1)}, f32[768,1024]{1,0:T(8,128)}, bf16[768,1024]{1,0:T(8,128)(2,1)}, s32[1]{0:T(128)}) custom-call(bf16[15,768,128]{2,1,0:T(8,128)(2,1)} %get-tuple-element.75.refs_0_.refs_4_, bf16[4,1024,3200]{2,1,0:T(8,128)(2,1)} %bitcast.280, ...), custom_call_target="tpu_custom_call" | custom-call | flops 2013265920 | bytes 15400960 | tf_op jit(solution)/shard_map/pallas_call | solution.py:123
  352.6 22.2 %shard_map.210 = (f32[768,1024]{1,0:T(8,128)}, f32[4,768,640]{2,1,0:T(8,128)}, f32[4,768,640]{2,1,0:T(8,128)}, s32[1]{0:T(128)}) custom-call(bf16[768,1024]{1,0:T(8,128)(2,1)} %get-tuple-element.76.refs_0_.refs_2_, f32[768,1024]{1,0:T(8,128)} %get-tuple-element.77.refs_1_, bf16[4,1024,1920]{2,1,0:T(8,128)(2,1)} %bitcast.290, ...), custom_call_target="tpu_custom_call" | custom-call | flops 12079595520 | bytes 39321600 | tf_op jit(solution)/shard_map/pallas_call | solution.py:123
  377.3 40.4 %shard_map.211 = (f32[768,1024]{1,0:T(8,128)}, bf16[4,1024,1920]{2,1,0:T(8,128)(2,1)}, s32[1]{0:T(128)}) custom-call(s32[4]{0:T(128)} %iota.47.refs_0_, bf16[768,1024]{1,0:T(8,128)(2,1)} %get-tuple-element.254.refs_1_, bf16[768,1024]{1,0:T(8,128)(2,1)} %get-tuple-element.76.refs_0_.refs_2_, f32[768,1024]{1,0:T(8,128)} %broadcast_in_dim.56.refs_3_, ...), custom_call_target="tpu_custom_call" | custom-call | flops 24159191040 | bytes 56623104 | tf_op jit(solution)/shard_map/pallas_call | solution.py:123
  419.9 10.5 %shard_map.212 = (f32[768,1024]{1,0:T(8,128)}, bf16[768,1024]{1,0:T(8,128)(2,1)}, bf16[15,768,128]{2,1,0:T(8,128)(2,1)}, f32[1,1024]{1,0:T(1,128)}, s32[1]{0:T(128)}) custom-call(f32[768,1024]{1,0:T(8,128)} %get-tuple-element.81.refs_0_, f32[768,1024]{1,0:T(8,128)} %get-tuple-element.77.refs_1_, f32[768,1024]{1,0:T(8,128)} %get-tuple-element.255.refs_2_, ...), custom_call_target="tpu_custom_call" | custom-call | flops 2013265920 | bytes 19726336 | tf_op jit(solution)/shard_map/pallas_call | solution.py:123
  430.4 37.5 %shard_map.213 = (bf16[15,768,128]{2,1,0:T(8,128)(2,1)}, f32[5,1536,128]{2,1,0:T(8,128)}, s32[1]{0:T(128)}) custom-call(s32[4]{0:T(128)} %get-tuple-element.157.refs_0_, bf16[15,768,128]{2,1,0:T(8,128)(2,1)} %get-tuple-element.73.refs_1_, bf16[5,1536,128]{2,1,0:T(8,128)(2,1)} %copy-done.14, bf16[15,768,128]{2,1,0:T(8,128)(2,1)} %get-tuple-element.82.refs_3_, ...), custom_call_target="tpu_custom_call" | custom-call | flops 45298483200 | bytes 23592960 | tf_op jit(solution)/shard_map/pallas_call | solution.py:123
  470.9 10.6 %shard_map.214 = (f32[768,1024]{1,0:T(8,128)}, bf16[2,1024,640]{2,1,0:T(8,128)(2,1)}, f32[1024,640]{1,0:T(8,128)}, s32[1]{0:T(128)}) custom-call(bf16[15,768,128]{2,1,0:T(8,128)(2,1)} %get-tuple-element.85.refs_0_.refs_2_, bf16[768,1024]{1,0:T(8,128)(2,1)} %get-tuple-element.86.refs_1_.refs_5_, bf16[768,1024]{1,0:T(8,128)(2,1)} %get-tuple-element.87.refs_2_, ...), custom_call_target="tpu_custom_call" | custom-call | flops 4026531840 | bytes 16777216 | tf_op jit(solution)/shard_map/pallas_call | solution.py:123
  481.5 24.6 %collective-permute-done.2.refs_1_ = bf16[5,768,128]{2,1,0:T(8,128)(2,1)S(1)} collective-permute-done((bf16[5,768,128]{2,1,0:T(8,128)(2,1)S(1)}, bf16[5,768,128]{2,1,0:T(8,128)(2,1)S(1)}, u32[]{:S(2)}, u32[]{:S(2)}) %collective-permute-start.2) | collective-permute-done | bytes 983072 | tf_op jit(solution)/shard_map/ppermute | solution.py:891
  507.0 14.9 %shard_map.215 = (f32[768,1024]{1,0:T(8,128)}, bf16[768,1024]{1,0:T(8,128)(2,1)}, bf16[2,1024,640]{2,1,0:T(8,128)(2,1)}, f32[1,1024]{1,0:T(1,128)}, s32[1]{0:T(128)}) custom-call(f32[5,1536,128]{2,1,0:T(8,128)} %get-tuple-element.84.refs_0_, bf16[5,768,128]{2,1,0:T(8,128)(2,1)} %copy-done.8, bf16[15,768,128]{2,1,0:T(8,128)(2,1)} %get-tuple-element.85.refs_0_.refs_2_, ...), custom_call_target="tpu_custom_call" | custom-call | flops 3523215360 | bytes 33423360 | tf_op jit(solution)/shard_map/pallas_call | solution.py:123
  522.4 41.4 %shard_map.216 = (f32[768,1024]{1,0:T(8,128)}, bf16[4,1024,1920]{2,1,0:T(8,128)(2,1)}, s32[1]{0:T(128)}) custom-call(s32[4]{0:T(128)} %iota.46.refs_0_, bf16[768,1024]{1,0:T(8,128)(2,1)} %get-tuple-element.93.refs_1_, bf16[768,1024]{1,0:T(8,128)(2,1)} %get-tuple-element.70.refs_0_.refs_2_, f32[768,1024]{1,0:T(8,128)} %broadcast_in_dim.56.refs_3_, ...), custom_call_target="tpu_custom_call" | custom-call | flops 24159191040 | bytes 56623104 | tf_op jit(solution)/shard_map/pallas_call | solution.py:123
  572.1 4.9 fusion.16
  588.5 10.3 %shard_map.217 = (f32[768,1024]{1,0:T(8,128)}, bf16[768,1024]{1,0:T(8,128)(2,1)}, bf16[15,768,128]{2,1,0:T(8,128)(2,1)}, f32[1,1024]{1,0:T(1,128)}, s32[1]{0:T(128)}) custom-call(f32[768,1024]{1,0:T(8,128)} %get-tuple-element.96.refs_0_, f32[768,1024]{1,0:T(8,128)} %get-tuple-element.71.refs_1_, f32[768,1024]{1,0:T(8,128)} %get-tuple-element.97.refs_2_, ...), custom_call_target="tpu_custom_call" | custom-call | flops 2013265920 | bytes 19726336 | tf_op jit(solution)/shard_map/pallas_call | solution.py:123
  598.8 37.7 %shard_map.218 = (bf16[15,768,128]{2,1,0:T(8,128)(2,1)}, f32[5,1536,128]{2,1,0:T(8,128)}, s32[1]{0:T(128)}) custom-call(s32[4]{0:T(128)} %get-tuple-element.157.refs_0_, bf16[15,768,128]{2,1,0:T(8,128)(2,1)} %get-tuple-element.67.refs_1_, bf16[5,1536,128]{2,1,0:T(8,128)(2,1)} %copy-done.13, bf16[15,768,128]{2,1,0:T(8,128)(2,1)} %get-tuple-element.102.refs_3_, ...), custom_call_target="tpu_custom_call" | custom-call | flops 45298483200 | bytes 23592960 | tf_op jit(solution)/shard_map/pallas_call | solution.py:123
  649.2 10.6 %shard_map.219 = (f32[768,1024]{1,0:T(8,128)}, bf16[2,1024,640]{2,1,0:T(8,128)(2,1)}, f32[1024,640]{1,0:T(8,128)}, s32[1]{0:T(128)}) custom-call(bf16[15,768,128]{2,1,0:T(8,128)(2,1)} %get-tuple-element.105.refs_0_.refs_2_, bf16[768,1024]{1,0:T(8,128)(2,1)} %get-tuple-element.106.refs_1_.refs_5_, bf16[768,1024]{1,0:T(8,128)(2,1)} %get-tuple-element.107.refs_2_, ...), custom_call_target="tpu_custom_call" | custom-call | flops 4026531840 | bytes 16777216 | tf_op jit(solution)/shard_map/pallas_call | solution.py:123
  659.8 12.2 %collective-permute-done.5.refs_1_ = bf16[5,768,128]{2,1,0:T(8,128)(2,1)} collective-permute-done((bf16[5,768,128]{2,1,0:T(8,128)(2,1)}, bf16[5,768,128]{2,1,0:T(8,128)(2,1)}, u32[]{:S(2)}, u32[]{:S(2)}) %collective-permute-start.5) | collective-permute-done | bytes 983072 | tf_op jit(solution)/shard_map/ppermute | solution.py:891
  672.0 14.6 %shard_map.220 = (f32[768,1024]{1,0:T(8,128)}, bf16[768,1024]{1,0:T(8,128)(2,1)}, bf16[2,1024,640]{2,1,0:T(8,128)(2,1)}, f32[1,1024]{1,0:T(1,128)}, s32[1]{0:T(128)}) custom-call(f32[5,1536,128]{2,1,0:T(8,128)} %get-tuple-element.104.refs_0_, bf16[5,768,128]{2,1,0:T(8,128)(2,1)} %collective-permute-done.5.refs_1_, ...), custom_call_target="tpu_custom_call" | custom-call | flops 3523215360 | bytes 33423360 | tf_op jit(solution)/shard_map/pallas_call | solution.py:123
  693.5 12.2 %collective-permute-done.18 = bf16[2,128,640]{2,1,0:T(8,128)(2,1)S(1)} collective-permute-done((bf16[2,128,640]{2,1,0:T(8,128)(2,1)S(1)}, bf16[2,128,640]{2,1,0:T(8,128)(2,1)S(1)}, u32[]{:S(2)}, u32[]{:S(2)}) %collective-permute-start.18) | collective-permute-done | bytes 327712 | tf_op jit(solution)/shard_map/ppermute | solution.py:68
  716.0 14.0 %collective-permute-done.9 = bf16[2,2,128,640]{3,2,0,1:T(8,128)(2,1)} collective-permute-done((bf16[2,2,128,640]{3,2,0,1:T(8,128)(2,1)}, bf16[2,2,128,640]{3,2,0,1:T(8,128)(2,1)}, u32[]{:S(2)}, u32[]{:S(2)}) %collective-permute-start.9) | collective-permute-done | bytes 655392 | tf_op jit(solution)/shard_map/ppermute | solution.py:68
  739.0 8.5 %collective-permute-done.10 = bf16[2,128,640]{2,1,0:T(8,128)(2,1)S(1)} collective-permute-done((bf16[2,128,640]{2,1,0:T(8,128)(2,1)S(1)}, bf16[2,128,640]{2,1,0:T(8,128)(2,1)S(1)}, u32[]{:S(2)}, u32[]{:S(2)}) %collective-permute-start.10) | collective-permute-done | bytes 327712 | tf_op jit(solution)/shard_map/ppermute | solution.py:60
  755.8 11.0 %collective-permute-done.20 = bf16[128,640]{1,0:T(8,128)(2,1)S(1)} collective-permute-done((bf16[128,640]{1,0:T(8,128)(2,1)S(1)}, bf16[128,640]{1,0:T(8,128)(2,1)S(1)}, u32[]{:S(2)}, u32[]{:S(2)}) %collective-permute-start.20) | collective-permute-done | bytes 163872 | tf_op jit(solution)/shard_map/ppermute | solution.py:60
  768.9 16.0 %collective-permute-done.15 = bf16[128,640]{1,0:T(8,128)(2,1)S(1)} collective-permute-done((bf16[128,640]{1,0:T(8,128)(2,1)S(1)}, bf16[128,640]{1,0:T(8,128)(2,1)S(1)}, u32[]{:S(2)}, u32[]{:S(2)}) %collective-permute-start.15) | collective-permute-done | bytes 163872 | tf_op jit(solution)/shard_map/ppermute | solution.py:60
  786.8 11.2 %collective-permute-done.22 = bf16[2,128,640]{2,1,0:T(8,128)(2,1)S(1)} collective-permute-done((bf16[2,128,640]{2,1,0:T(8,128)(2,1)S(1)}, bf16[2,128,640]{2,1,0:T(8,128)(2,1)S(1)}, u32[]{:S(2)}, u32[]{:S(2)}) %collective-permute-start.22) | collective-permute-done | bytes 327712 | tf_op jit(solution)/shard_map/ppermute | solution.py:104
  798.2 5.9 reduce-scatter.5.cloned.1.call-done
  (257 shorter events, 121.7 us)
Async XLA Ops:
  7.2 286.3 %copy-start = (bf16[1,768,960]{1,2,0:T(8,128)(2,1)S(1)}, bf16[1,768,960]{1,2,0:T(8,128)(2,1)}, u32[]{:S(2)}) copy-start(bf16[1,768,960]{1,2,0:T(8,128)(2,1)} %param.23) | copy-start | bytes 4423684
  7.2 176.7 %all-gather.3.cloned.1.call-start = ((), (), s32[]{:S(2)}) async-start(), calls=%async_computation.2 | async-start | bytes 27033600 | tf_op jit(solution)/shard_map/all_gather | solution.py:816
  21.4 331.1 %all-gather.5.cloned.1.call-start = ((), (), s32[]{:S(2)}) async-start(), calls=%async_computation.3 | async-start | bytes 16220160 | tf_op jit(solution)/shard_map/all_gather | solution.py:816
  22.6 625.4 %reduce-scatter.3.cloned.1.call-start = ((), (), s32[]{:S(2)}) async-start(), calls=%async_computation.4 | async-start | bytes 16220160 | tf_op jit(solution)/shard_map/reduce_scatter | solution.py:877
  23.5 269.9 %copy-start.26 = (s32[960]{0:T(1024)}, s32[960]{0:T(1024)S(1)}, u32[]{:S(2)}) copy-start(s32[960]{0:T(1024)S(1)} %fusion.108) | copy-start | bytes 11524
  195.4 28.7 %collective-permute-start = (bf16[5,768,128]{2,1,0:T(8,128)(2,1)}, bf16[5,768,128]{2,1,0:T(8,128)(2,1)S(1)}, u32[]{:S(2)}, u32[]{:S(2)}) collective-permute-start(bf16[5,768,128]{2,1,0:T(8,128)(2,1)} %get-tuple-element.68), channel_id=1, source_target_pairs={{0,4},{4,0},{1,5},{5,1},{2,6},{6,2},{3,7},{7,3},{8,12},{12,8},{9,1... | collective-permute-start | bytes 2949128 | tf_op jit(solution)/shard_map/ppermute | solution.py:851
  292.1 23.7 %collective-permute-start.1 = (bf16[5,768,128]{2,1,0:T(8,128)(2,1)}, bf16[5,768,128]{2,1,0:T(8,128)(2,1)S(1)}, u32[]{:S(2)}, u32[]{:S(2)}) collective-permute-start(bf16[5,768,128]{2,1,0:T(8,128)(2,1)} %get-tuple-element.74), channel_id=1, source_target_pairs={{0,4},{4,0},{1,5},{5,1},{2,6},{6,2},{3,7},{7,3},{8,12},{12,8},{9,1... | collective-permute-start | bytes 2949128 | tf_op jit(solution)/shard_map/ppermute | solution.py:851
  417.7 386.4 %reduce-scatter.5.cloned.1.call-start = ((), (), s32[]{:S(2)}) async-start(), calls=%async_computation.5 | async-start | bytes 16220160 | tf_op jit(solution)/shard_map/reduce_scatter | solution.py:877
  469.6 36.4 %collective-permute-start.2 = (bf16[5,768,128]{2,1,0:T(8,128)(2,1)S(1)}, bf16[5,768,128]{2,1,0:T(8,128)(2,1)S(1)}, u32[]{:S(2)}, u32[]{:S(2)}) collective-permute-start(bf16[5,768,128]{2,1,0:T(8,128)(2,1)S(1)} %slice.478), channel_id=1, source_target_pairs={{0,4},{4,0},{1,5},{5,1},{2,6},{6,2},{3,7},{7,3},{8,12},{12,8},{9,1... | collective-permute-start | bytes 2949128 | tf_op jit(solution)/shard_map/ppermute | solution.py:891
  570.4 7.7 collective-permute-start.3
  571.6 8.2 %collective-permute-start.4 = (bf16[2,512,640]{2,1,0:T(8,128)(2,1)}, bf16[2,512,640]{2,1,0:T(8,128)(2,1)}, u32[]{:S(2)}, u32[]{:S(2)}) collective-permute-start(bf16[2,512,640]{2,1,0:T(8,128)(2,1)} %pad_maximum_fusion.1), channel_id=1, source_target_pairs={{0,1},{1,0},{2,3},{3,2},{4,5},{5,4},{6,7},{7,6},{8,9},{9,8},{10,11... | collective-permute-start | bytes 3932168 | tf_op jit(solution)/shard_map/ppermute | solution.py:82
  583.0 58.3 %collective-permute-start.6 = (bf16[2,2,128,640]{3,2,1,0:T(8,128)(2,1)S(1)}, bf16[2,2,128,640]{3,2,1,0:T(8,128)(2,1)}, u32[]{:S(2)}, u32[]{:S(2)}) collective-permute-start(bf16[2,2,128,640]{3,2,1,0:T(8,128)(2,1)S(1)} %fusion.49), channel_id=1, source_target_pairs={{0,2},{2,0},{1,3},{3,1},{4,6},{6,4},{5,7},{7,5},{8,10},{10,8},{9,1... | collective-permute-start | bytes 1966088 | tf_op jit(solution)/shard_map/ppermute | solution.py:68
  587.1 56.5 %collective-permute-start.7 = (bf16[2,2,128,640]{3,2,1,0:T(8,128)(2,1)}, bf16[2,2,128,640]{3,2,1,0:T(8,128)(2,1)}, u32[]{:S(2)}, u32[]{:S(2)}) collective-permute-start(bf16[2,2,128,640]{3,2,1,0:T(8,128)(2,1)} %fusion.42), channel_id=1, source_target_pairs={{0,4},{4,0},{1,5},{5,1},{2,6},{6,2},{3,7},{7,3},{8,12},{12,8},{9,1... | collective-permute-start | bytes 1966088 | tf_op jit(solution)/shard_map/ppermute | solution.py:60
  640.6 31.4 %collective-permute-start.5 = (bf16[5,768,128]{2,1,0:T(8,128)(2,1)}, bf16[5,768,128]{2,1,0:T(8,128)(2,1)}, u32[]{:S(2)}, u32[]{:S(2)}) collective-permute-start(bf16[5,768,128]{2,1,0:T(8,128)(2,1)} %slice.477), channel_id=1, source_target_pairs={{0,4},{4,0},{1,5},{5,1},{2,6},{6,2},{3,7},{7,3},{8,12},{12,8},{9,1... | collective-permute-start | bytes 2949128 | tf_op jit(solution)/shard_map/ppermute | solution.py:891
  646.6 45.9 %collective-permute-start.17 = (bf16[2,128,640]{2,1,0:T(8,128)(2,1)}, bf16[2,128,640]{2,1,0:T(8,128)(2,1)}, u32[]{:S(2)}, u32[]{:S(2)}) collective-permute-start(bf16[2,128,640]{2,1,0:T(8,128)(2,1)} %dynamic-slice_bitcast_fusion.1), channel_id=1, source_target_pairs={{0,4},{4,0},{1,5},{5,1},{2,6},{6,2},{3,7},{7,3},{8,12},{12,8},{9,1... | collective-permute-start | bytes 983048 | tf_op jit(solution)/shard_map/ppermute | solution.py:60
  691.5 16.7 %collective-permute-start.8 = (bf16[2,512,640]{2,1,0:T(8,128)(2,1)S(1)}, bf16[2,512,640]{2,1,0:T(8,128)(2,1)S(1)}, u32[]{:S(2)}, u32[]{:S(2)}) collective-permute-start(bf16[2,512,640]{2,1,0:T(8,128)(2,1)S(1)} %pad_maximum_fusion.2), channel_id=1, source_target_pairs={{0,1},{1,0},{2,3},{3,2},{4,5},{5,4},{6,7},{7,6},{8,9},{9,8},{10,11... | collective-permute-start | bytes 3932168 | tf_op jit(solution)/shard_map/ppermute | solution.py:82
  691.6 14.0 %collective-permute-start.18 = (bf16[2,128,640]{2,1,0:T(8,128)(2,1)S(1)}, bf16[2,128,640]{2,1,0:T(8,128)(2,1)S(1)}, u32[]{:S(2)}, u32[]{:S(2)}) collective-permute-start(bf16[2,128,640]{2,1,0:T(8,128)(2,1)S(1)} %dynamic-slice_bitcast_fusion), channel_id=1, source_target_pairs={{0,2},{2,0},{1,3},{3,1},{4,6},{6,4},{5,7},{7,5},{8,10},{10,8},{9,1... | collective-permute-start | bytes 983048 | tf_op jit(solution)/shard_map/ppermute | solution.py:68
  691.9 17.4 %collective-permute-start.11 = (bf16[2,512,640]{2,1,0:T(8,128)(2,1)S(1)}, bf16[2,512,640]{2,1,0:T(8,128)(2,1)S(1)}, u32[]{:S(2)}, u32[]{:S(2)}) collective-permute-start(bf16[2,512,640]{2,1,0:T(8,128)(2,1)S(1)} %pad_maximum_fusion.3), channel_id=1, source_target_pairs={{0,1},{1,0},{2,3},{3,2},{4,5},{5,4},{6,7},{7,6},{8,9},{9,8},{10,11... | collective-permute-start | bytes 3932168 | tf_op jit(solution)/shard_map/ppermute | solution.py:82
  693.5 12.8 %copy-start.33 = (f32[768,1024]{1,0:T(8,128)S(1)}, f32[768,1024]{1,0:T(8,128)}, u32[]{:S(2)}) copy-start(f32[768,1024]{1,0:T(8,128)} %get-tuple-element.115) | copy-start | bytes 9437188
  709.3 20.7 %collective-permute-start.9 = (bf16[2,2,128,640]{3,2,0,1:T(8,128)(2,1)}, bf16[2,2,128,640]{3,2,0,1:T(8,128)(2,1)}, u32[]{:S(2)}, u32[]{:S(2)}) collective-permute-start(bf16[2,2,128,640]{3,2,0,1:T(8,128)(2,1)} %fusion.54), channel_id=1, source_target_pairs={{0,2},{2,0},{1,3},{3,1},{4,6},{6,4},{5,7},{7,5},{8,10},{10,8},{9,1... | collective-permute-start | bytes 1966088 | tf_op jit(solution)/shard_map/ppermute | solution.py:68
  710.4 22.0 %collective-permute-start.12 = (bf16[2,2,128,640]{3,2,1,0:T(8,128)(2,1)}, bf16[2,2,128,640]{3,2,1,0:T(8,128)(2,1)}, u32[]{:S(2)}, u32[]{:S(2)}) collective-permute-start(bf16[2,2,128,640]{3,2,1,0:T(8,128)(2,1)} %fusion.32), channel_id=1, source_target_pairs={{0,4},{4,0},{1,5},{5,1},{2,6},{6,2},{3,7},{7,3},{8,12},{12,8},{9,1... | collective-permute-start | bytes 1966088 | tf_op jit(solution)/shard_map/ppermute | solution.py:60
  731.3 16.2 %collective-permute-start.10 = (bf16[2,128,640]{2,1,0:T(8,128)(2,1)S(1)}, bf16[2,128,640]{2,1,0:T(8,128)(2,1)S(1)}, u32[]{:S(2)}, u32[]{:S(2)}) collective-permute-start(bf16[2,128,640]{2,1,0:T(8,128)(2,1)S(1)} %dynamic-slice_bitcast_fusion.3), channel_id=1, source_target_pairs={{0,4},{4,0},{1,5},{5,1},{2,6},{6,2},{3,7},{7,3},{8,12},{12,8},{9,1... | collective-permute-start | bytes 983048 | tf_op jit(solution)/shard_map/ppermute | solution.py:60
  733.9 16.9 %collective-permute-start.13 = (bf16[2,128,640]{2,1,0:T(8,128)(2,1)S(1)}, bf16[2,128,640]{2,1,0:T(8,128)(2,1)S(1)}, u32[]{:S(2)}, u32[]{:S(2)}) collective-permute-start(bf16[2,128,640]{2,1,0:T(8,128)(2,1)S(1)} %dynamic-slice_bitcast_fusion.2), channel_id=1, source_target_pairs={{0,2},{2,0},{1,3},{3,1},{4,6},{6,4},{5,7},{7,5},{8,10},{10,8},{9,1... | collective-permute-start | bytes 983048 | tf_op jit(solution)/shard_map/ppermute | solution.py:68
  734.3 20.1 %collective-permute-start.21 = (bf16[128,640]{1,0:T(8,128)(2,1)S(1)}, bf16[128,640]{1,0:T(8,128)(2,1)S(1)}, u32[]{:S(2)}, u32[]{:S(2)}) collective-permute-start(bf16[128,640]{1,0:T(8,128)(2,1)S(1)} %get-tuple-element.219), channel_id=1, source_target_pairs={{0,24},{8,0},{16,8},{24,16},{1,25},{9,1},{17,9},{25,17},{2,26},{10... | collective-permute-start | bytes 491528 | tf_op jit(solution)/shard_map/ppermute | solution.py:60
  737.6 29.3 %collective-permute-start.20 = (bf16[128,640]{1,0:T(8,128)(2,1)S(1)}, bf16[128,640]{1,0:T(8,128)(2,1)S(1)}, u32[]{:S(2)}, u32[]{:S(2)}) collective-permute-start(bf16[128,640]{1,0:T(8,128)(2,1)S(1)} %get-tuple-element.218), channel_id=1, source_target_pairs={{0,16},{8,24},{16,0},{24,8},{1,17},{9,25},{17,1},{25,9},{2,18},{10... | collective-permute-start | bytes 491528 | tf_op jit(solution)/shard_map/ppermute | solution.py:60
  737.6 29.3 %collective-permute-start.19 = (bf16[128,640]{1,0:T(8,128)(2,1)S(1)}, bf16[128,640]{1,0:T(8,128)(2,1)S(1)}, u32[]{:S(2)}, u32[]{:S(2)}) collective-permute-start(bf16[128,640]{1,0:T(8,128)(2,1)S(1)} %get-tuple-element.217), channel_id=1, source_target_pairs={{0,8},{8,16},{16,24},{24,0},{1,9},{9,17},{17,25},{25,1},{2,10},{10... | collective-permute-start | bytes 491528 | tf_op jit(solution)/shard_map/ppermute | solution.py:60
  751.0 17.9 %collective-permute-start.16 = (bf16[128,640]{1,0:T(8,128)(2,1)S(1)}, bf16[128,640]{1,0:T(8,128)(2,1)S(1)}, u32[]{:S(2)}, u32[]{:S(2)}) collective-permute-start(bf16[128,640]{1,0:T(8,128)(2,1)S(1)} %get-tuple-element.216), channel_id=1, source_target_pairs={{0,24},{8,0},{16,8},{24,16},{1,25},{9,1},{17,9},{25,17},{2,26},{10... | collective-permute-start | bytes 491528 | tf_op jit(solution)/shard_map/ppermute | solution.py:60
  754.4 30.5 %collective-permute-start.15 = (bf16[128,640]{1,0:T(8,128)(2,1)S(1)}, bf16[128,640]{1,0:T(8,128)(2,1)S(1)}, u32[]{:S(2)}, u32[]{:S(2)}) collective-permute-start(bf16[128,640]{1,0:T(8,128)(2,1)S(1)} %get-tuple-element.215), channel_id=1, source_target_pairs={{0,16},{8,24},{16,0},{24,8},{1,17},{9,25},{17,1},{25,9},{2,18},{10... | collective-permute-start | bytes 491528 | tf_op jit(solution)/shard_map/ppermute | solution.py:60
  754.4 32.3 %copy-start.16 = (bf16[128,1920]{1,0:T(8,128)(2,1)S(1)}, bf16[128,1920]{1,0:T(8,128)(2,1)}, u32[]{:S(2)}) copy-start(bf16[128,1920]{1,0:T(8,128)(2,1)} %reduce-scatter.3.cloned.1.call-done) | copy-start | bytes 1474564
  754.4 30.5 %collective-permute-start.14 = (bf16[128,640]{1,0:T(8,128)(2,1)S(1)}, bf16[128,640]{1,0:T(8,128)(2,1)S(1)}, u32[]{:S(2)}, u32[]{:S(2)}) collective-permute-start(bf16[128,640]{1,0:T(8,128)(2,1)S(1)} %get-tuple-element.214), channel_id=1, source_target_pairs={{0,8},{8,16},{16,24},{24,0},{1,9},{9,17},{17,25},{25,1},{2,10},{10... | collective-permute-start | bytes 491528 | tf_op jit(solution)/shard_map/ppermute | solution.py:60
  785.1 12.9 %collective-permute-start.22 = (bf16[2,128,640]{2,1,0:T(8,128)(2,1)S(1)}, bf16[2,128,640]{2,1,0:T(8,128)(2,1)S(1)}, u32[]{:S(2)}, u32[]{:S(2)}) collective-permute-start(bf16[2,128,640]{2,1,0:T(8,128)(2,1)S(1)} %pad_maximum_fusion.14), channel_id=1, source_target_pairs={{0,2},{2,0},{1,3},{3,1},{4,6},{6,4},{5,7},{7,5},{8,10},{10,8},{9,1... | collective-permute-start | bytes 983048 | tf_op jit(solution)/shard_map/ppermute | solution.py:104
  798.1 9.7 %collective-permute-start.23 = (bf16[2,2,128,640]{3,2,1,0:T(8,128)(2,1)S(1)}, bf16[2,2,128,640]{3,2,1,0:T(8,128)(2,1)S(1)}, u32[]{:S(2)}, u32[]{:S(2)}) collective-permute-start(bf16[2,2,128,640]{3,2,1,0:T(8,128)(2,1)S(1)} %pad_maximum_fusion.8), channel_id=1, source_target_pairs={{0,1},{1,0},{2,3},{3,2},{4,5},{5,4},{6,7},{7,6},{8,9},{9,8},{10,11... | collective-permute-start | bytes 1966088 | tf_op jit(solution)/shard_map/ppermute | solution.py:110
  (30 other events, 78.5 us)
Sparse Core Ops, SparseCore 0:
  21.5 162.3 all-gather.2
  187.5 113.1 all-gather.4
  417.8 177.5 reduce-scatter.2
  601.3 202.7 reduce-scatter.4
